TPU v7x, 256 devices: a whole 4x4x8 slice. The times are simulated.
256 devices in a mesh: lon: 16 (over x, y_lo, core), lat: 16 (over y_hi, z).
Axes of the slice: x: 4, y: 4 (y_hi: 2, y_lo: 2; y = y_hi * 2 + y_lo), z: 8, core: 2. Of those that a mesh axis runs over, the one named last changes fastest.
Arguments:
- thermal_state: float32 [8, 2048, 4096], P(None, 'lat', 'lon'), may hold values from -6 to 6
- zonal_boundary_speed: float32 [8, 2048, 4096], P(None, 'lat', 'lon'), may hold values from -6 to 6
- meridional_boundary_speed: float32 [8, 2048, 4096], P(None, 'lat', 'lon'), may hold values from -6 to 6
- sea_indicator_grid: int32 [8, 2048, 4096], P(None, 'lat', 'lon'), may hold values from 0 to 1, as said below
- bathymetry_depth_index: int32 [2048, 4096], P('lat', 'lon'), may hold values from 0 to 8, as said below
- revised_thermal_adjoint: float32 [8, 2048, 4096], P(None, 'lat', 'lon'), may hold values from -6 to 6
- input_stratum_matrix: float32 [128, 32], replicated, may hold values from -1 to 1
- input_stratum_offset: float32 [128], replicated, may hold values from -3 to 3
- hidden_stratum_matrix: float32 [128, 128], replicated, may hold values from -0.5 to 0.5
- hidden_stratum_offset: float32 [128], replicated, may hold values from -3 to 3
- output_stratum_matrix: float32 [8, 128], replicated, may hold values from -0.5 to 0.5
- output_stratum_offset: float32 [8], replicated, may hold values from -4 to 4
Outputs:
- revised_thermal_state: float32 [8, 2048, 4096], P(None, 'lat', 'lon')
- surface_height: float32 [2048, 4096], P('lat', 'lon')
- inner_weight_gradient: float32 [128, 32], replicated
- inner_bias_gradient: float32 [128], replicated
- hidden_weight_gradient: float32 [128, 128], replicated
- hidden_bias_gradient: float32 [128], replicated
- outer_weight_gradient: float32 [8, 128], replicated
- outer_bias_gradient: float32 [8], replicated
Inputs may be any that keep to these rules, and one draw needn't show every extreme that they name: sea_indicator_grid is 1 only at levels below the column's bathymetry_depth_index. `bathymetry_depth_index`: levels of each column; 0 is land.
All inputs are finite; a program needn't handle non-finite values.
Results may differ from a plain program's by a relative error of at most 0.0071.
The roundings to bfloat16 on the way count: a program that leaves them out, or rounds other values in their place, can miss the bound.
Values sent between devices are 32-bit elements; how exact they have to be, the bound alone decides.
No kernel may reach another device: no remote copies, remote signals or barrier semaphores. Data moves between devices by JAX's collectives and lax.ppermute only.
A program may use at most 128 MiB of HBM per device.

v0:
```python
import math

import jax
import jax.numpy as jnp
from jax import lax
from jax.sharding import PartitionSpec as P

DEPTH_STRATA = 8
ITERS = 3


SIGMA = 0.5
PRESSURE_STEP = 1.0
TRANSPORT_TICK = 0.2
KAPPA_FLOOR = 0.02
KAPPA_SPAN = 0.4
GRADIENT_GAIN = 16.0


def extended(block, sides, width):
    for axis, dim in sides:
        count = lax.axis_size(axis)
        forward = [(i, i + 1) for i in range(count - 1)]
        forward.append((count - 1, 0))
        backward = [(target, source) for source, target in forward]
        low = lax.ppermute(
            lax.slice_in_dim(block, block.shape[dim] - width, None, axis=dim), axis, forward
        )
        high = lax.ppermute(lax.slice_in_dim(block, 0, width, axis=dim), axis, backward)
        block = jnp.concatenate([low, block, high], axis=dim)
    return block


def poles(padded, width, lat_dim):
    position = lax.axis_index("lat")
    extent = padded.shape[lat_dim]
    meridian_strips = lax.broadcasted_iota(jnp.int32, padded.shape, lat_dim)
    outside = jnp.logical_or(
        jnp.logical_and(meridian_strips < width, position == 0),
        jnp.logical_and(meridian_strips >= extent - width, position == lax.axis_size("lat") - 1),
    )
    return jnp.where(outside, jnp.zeros_like(padded), padded)


def window(padded, width, row_start, row_count, col_start, col_count):
    return padded[
        ...,
        width + row_start : width + row_start + row_count,
        width + col_start : width + col_start + col_count,
    ]


def contract_columns(left, right):
    return lax.dot_general(
        left, right, (((1,), (1,)), ((), ())), preferred_element_type=jnp.float32
    )


def contract_rows(left, right):
    return lax.dot_general(
        left, right, (((0,), (0,)), ((), ())), preferred_element_type=jnp.float32
    )


def closure_block(features, pull, weights, biases):
    input_stratum_matrix, hidden_stratum_matrix, output_stratum_matrix = weights
    input_stratum_offset, hidden_stratum_offset, output_stratum_offset = biases
    first_value = jnp.tanh(
        jnp.dot(input_stratum_matrix, features, preferred_element_type=jnp.float32)
        + input_stratum_offset[:, None]
    )
    first_stored = first_value.astype(jnp.bfloat16)
    second_value = jnp.tanh(
        jnp.dot(hidden_stratum_matrix, first_stored, preferred_element_type=jnp.float32)
        + hidden_stratum_offset[:, None]
    )
    second_stored = second_value.astype(jnp.bfloat16)
    squash = jax.nn.sigmoid(
        jnp.dot(output_stratum_matrix, second_stored, preferred_element_type=jnp.float32)
        + output_stratum_offset[:, None]
    )
    kappa = KAPPA_FLOOR + KAPPA_SPAN * squash
    outer_term = pull * KAPPA_SPAN * squash * (1.0 - squash)
    outer_grad = outer_term.astype(jnp.bfloat16)
    hidden_term = contract_rows(output_stratum_matrix, outer_grad) * (
        1.0 - second_value * second_value
    )
    hidden_grad = hidden_term.astype(jnp.bfloat16)
    inner_term = contract_rows(hidden_stratum_matrix, hidden_grad) * (
        1.0 - first_value * first_value
    )
    inner_grad = inner_term.astype(jnp.bfloat16)
    sums = (
        contract_columns(inner_grad, features),
        jnp.sum(inner_term, axis=1),
        contract_columns(hidden_grad, first_stored),
        jnp.sum(hidden_term, axis=1),
        contract_columns(outer_grad, second_stored),
        jnp.sum(outer_term, axis=1),
    )
    return (kappa, sums)


def closure_field(features, pull, weights, biases, sum_shapes):
    feature_rows, meridian_strips, profile_points = features.shape
    populated_strata = pull.shape[0]
    strip_rows = 16

    def turn(index, carry):
        kappa, cumulative_sums_list = carry
        start = (index * strip_rows).astype(jnp.int32)
        block_features = lax.dynamic_slice_in_dim(features, start, strip_rows, 1).reshape(
            feature_rows, strip_rows * profile_points
        )
        block_pull = lax.dynamic_slice_in_dim(pull, start, strip_rows, 1).reshape(
            populated_strata, strip_rows * profile_points
        )
        block_kappa, block_sums = closure_block(block_features, block_pull, weights, biases)
        kappa = lax.dynamic_update_slice_in_dim(
            kappa, block_kappa.reshape(populated_strata, strip_rows, profile_points), start, 1
        )
        return (kappa, jax.tree.map(jnp.add, cumulative_sums_list, block_sums))

    initial = (
        jnp.zeros(pull.shape, jnp.float32),
        tuple((jnp.zeros(array_dimensions, jnp.float32) for array_dimensions in sum_shapes)),
    )
    return lax.fori_loop(0, meridian_strips // strip_rows, turn, initial)


def squares(values):
    return lax.psum(jnp.sum(values * values), ("lon", "lat"))


def local(
    thermal_state,
    zonal_boundary_speed,
    meridional_boundary_speed,
    sea_indicator_grid,
    bathymetry_depth_index,
    revised_thermal_adjoint,
    input_stratum_matrix,
    input_stratum_offset,
    hidden_stratum_matrix,
    hidden_stratum_offset,
    output_stratum_matrix,
    output_stratum_offset,
):
    populated_strata, meridian_strips, profile_points = thermal_state.shape
    sea_indicator = sea_indicator_grid.astype(jnp.float32)
    scalar_quantity = thermal_state * sea_indicator
    depth = bathymetry_depth_index.astype(jnp.float32)
    stacked = jnp.concatenate(
        [
            scalar_quantity,
            zonal_boundary_speed,
            meridional_boundary_speed,
            sea_indicator,
            depth[None],
        ],
        axis=0,
    )
    padded = poles(extended(stacked, (("lon", 2), ("lat", 1)), 2), 2, 1)
    tracer_pad = padded[:populated_strata]
    flow_pad = padded[populated_strata:]
    flow_width = 2
    zonal_pad = flow_pad[:populated_strata]
    meridional_pad = flow_pad[populated_strata : 2 * populated_strata]
    wet_pad = flow_pad[2 * populated_strata : 3 * populated_strata]
    depth_pad = flow_pad[3 * populated_strata]
    east_wet = window(wet_pad, flow_width, 0, meridian_strips, -1, profile_points + 1) * window(
        wet_pad, flow_width, 0, meridian_strips, 0, profile_points + 1
    )
    north_wet = window(wet_pad, flow_width, -1, meridian_strips + 1, 0, profile_points) * window(
        wet_pad, flow_width, 0, meridian_strips + 1, 0, profile_points
    )
    east_depth = jnp.minimum(
        window(depth_pad, flow_width, 0, meridian_strips, -1, profile_points + 1),
        window(depth_pad, flow_width, 0, meridian_strips, 0, profile_points + 1),
    )
    north_depth = jnp.minimum(
        window(depth_pad, flow_width, -1, meridian_strips + 1, 0, profile_points),
        window(depth_pad, flow_width, 0, meridian_strips + 1, 0, profile_points),
    )
    east_flow = window(zonal_pad, flow_width, 0, meridian_strips, -1, profile_points + 1)
    north_flow = window(meridional_pad, flow_width, -1, meridian_strips + 1, 0, profile_points)
    east_transport = jnp.sum(east_wet * east_flow, axis=0)
    north_transport = jnp.sum(north_wet * north_flow, axis=0)
    source = -(
        east_transport[:, 1:] - east_transport[:, :-1] + north_transport[1:] - north_transport[:-1]
    )
    sea_height_anomaly = jnp.zeros_like(source)
    residual = source
    direction = source
    norm_now = squares(residual)
    for step in range(ITERS):
        rim = poles(extended(direction, (("lon", 1), ("lat", 0)), 1), 1, 0)
        image = (
            SIGMA * direction
            + east_depth[:, 1:] * (direction - rim[1:-1, 2:])
            + east_depth[:, :-1] * (direction - rim[1:-1, :-2])
            + north_depth[1:] * (direction - rim[2:, 1:-1])
            + north_depth[:-1] * (direction - rim[:-2, 1:-1])
        )
        image, rim = (image, rim)
        alpha = norm_now / lax.psum(jnp.sum(direction * image), ("lon", "lat"))
        sea_height_anomaly = sea_height_anomaly + alpha * direction
        if step + 1 < ITERS:
            residual = residual - alpha * image
            norm_next = squares(residual)
            direction = residual + norm_next / norm_now * direction
            norm_now = norm_next
    height_rim = poles(extended(sea_height_anomaly, (("lon", 1), ("lat", 0)), 1), 1, 0)
    zonal_fixed = east_flow - PRESSURE_STEP * (height_rim[1:-1, 1:] - height_rim[1:-1, :-1])
    meridional_fixed = north_flow - PRESSURE_STEP * (height_rim[1:, 1:-1] - height_rim[:-1, 1:-1])

    def along_east(offset):
        return window(tracer_pad, 2, 0, meridian_strips, offset - 1, profile_points + 1)

    def along_north(offset):
        return window(tracer_pad, 2, offset - 1, meridian_strips + 1, 0, profile_points)

    east_face = (7.0 * (along_east(0) + along_east(1)) - (along_east(-1) + along_east(2))) / 12.0
    north_face = (
        7.0 * (along_north(0) + along_north(1)) - (along_north(-1) + along_north(2))
    ) / 12.0
    east_flux = east_wet * zonal_fixed * east_face
    north_flux = north_wet * meridional_fixed * north_face
    carry_scalar_downstream = -(
        east_flux[..., 1:] - east_flux[..., :-1] + north_flux[:, 1:] - north_flux[:, :-1]
    )
    zonal_slope = 0.5 * (
        window(tracer_pad, 2, 0, meridian_strips, 1, profile_points)
        - window(tracer_pad, 2, 0, meridian_strips, -1, profile_points)
    )
    meridional_slope = 0.5 * (
        window(tracer_pad, 2, 1, meridian_strips, 0, profile_points)
        - window(tracer_pad, 2, -1, meridian_strips, 0, profile_points)
    )
    levels = jnp.arange(populated_strata, dtype=jnp.float32)[:, None, None]
    clearance = sea_indicator * (depth[None] - levels) / DEPTH_STRATA
    features = jnp.concatenate(
        [scalar_quantity, zonal_slope, meridional_slope, clearance], axis=0
    ).astype(jnp.bfloat16)
    sea_indicator_couple = sea_indicator[:-1] * sea_indicator[1:]
    depth_stride_amount = scalar_quantity[1:] - scalar_quantity[:-1]
    zero_level = jnp.zeros_like(scalar_quantity[:1])
    neighbour_connection = (
        sea_indicator_couple
        * (revised_thermal_adjoint[:-1] - revised_thermal_adjoint[1:])
        * depth_stride_amount
    )
    pull = 0.5 * (
        jnp.concatenate([neighbour_connection, zero_level], axis=0)
        + jnp.concatenate([zero_level, neighbour_connection], axis=0)
    )
    weights = (
        input_stratum_matrix.astype(jnp.bfloat16),
        hidden_stratum_matrix.astype(jnp.bfloat16),
        output_stratum_matrix.astype(jnp.bfloat16),
    )
    biases = (input_stratum_offset, hidden_stratum_offset, output_stratum_offset)
    sum_shapes = (
        input_stratum_matrix.shape,
        input_stratum_offset.shape,
        hidden_stratum_matrix.shape,
        hidden_stratum_offset.shape,
        output_stratum_matrix.shape,
        output_stratum_offset.shape,
    )
    kappa, cumulative_sums_list = closure_field(features, pull, weights, biases, sum_shapes)
    down = 0.5 * (kappa[:-1] + kappa[1:]) * sea_indicator_couple * depth_stride_amount
    downward_mixing_operator = jnp.concatenate([down, zero_level], axis=0) - jnp.concatenate(
        [zero_level, down], axis=0
    )
    revised_thermal_state = sea_indicator * (
        scalar_quantity + TRANSPORT_TICK * carry_scalar_downstream + downward_mixing_operator
    )
    multiplier_amount = GRADIENT_GAIN / math.sqrt(
        meridian_strips * lax.axis_size("lat") * profile_points * lax.axis_size("lon")
    )
    summed = lax.psum(
        (
            cumulative_sums_list[0] * multiplier_amount,
            cumulative_sums_list[1] * multiplier_amount,
            cumulative_sums_list[2] * multiplier_amount,
            cumulative_sums_list[3] * multiplier_amount,
            cumulative_sums_list[4] * multiplier_amount,
            cumulative_sums_list[5] * multiplier_amount,
        ),
        ("lon", "lat"),
    )
    return (
        revised_thermal_state,
        sea_height_anomaly,
        summed[0],
        summed[1],
        summed[2],
        summed[3],
        summed[4],
        summed[5],
    )


def solution(mesh):
    placed = (
        P(None, "lat", "lon"),
        P(None, "lat", "lon"),
        P(None, "lat", "lon"),
        P(None, "lat", "lon"),
        P("lat", "lon"),
        P(None, "lat", "lon"),
        P(),
        P(),
        P(),
        P(),
        P(),
        P(),
    )
    return jax.shard_map(
        local,
        mesh=mesh,
        in_specs=placed,
        out_specs=(P(None, "lat", "lon"), P("lat", "lon"), P(), P(), P(), P(), P(), P()),
        check_vma=False,
    )
```

profile of v0, /device:TPU:1, one launch (start us, length us, event | category | flops | bytes accessed | tf_op | source)
XLA Modules:
  0.0 878.1 jit_solution(17308916902785576374)
XLA Ops:
  21.3 2.8 collective-permute-start
  24.8 3.2 fusion.73
  36.2 2.6 pad_maximum_fusion
  38.8 4.9 fusion.71
  43.6 3.7 copy.43
  48.4 3.7 copy.44
  52.1 6.9 collective-permute-start.3
  59.6 3.1 copy.45
  62.7 3.0 copy.46
  65.7 8.2 maximum_select_fusion
  83.7 5.1 collective-permute-start.7
  89.1 2.9 copy.50
  95.0 81.7 %all-reduce.5 = (f32[]{:T(128)}, f32[]{:T(128)}) all-reduce(f32[]{:T(128)} %get-tuple-element.396, f32[]{:T(128)} %get-tuple-element.395), channel_id=1, replica_groups=mesh['lon'=16,'lat'=16] {'lon','lat'}, use_global_device_ids=true, to_apply=%region_3.4 | all-reduce | flops 2 | bytes 16 | tf_op jit(solution)/shard_map/psum | solution.py:132
  179.6 72.8 %psum.86 = f32[]{:T(128)} all-reduce(f32[]{:T(128)} %get-tuple-element.441), channel_id=1, replica_groups=mesh['lon'=16,'lat'=16] {'lon','lat'}, use_global_device_ids=true, to_apply=%region_7.8 | all-reduce | flops 1 | bytes 8 | tf_op jit(solution)/shard_map/psum | solution.py:132
  256.2 101.1 %while.26 = (s32[]{:T(128)}, f32[8,128,256]{2,0,1:T(8,128)}, f32[128,32]{0,1:T(8,128)}, f32[128]{0:T(128)S(1)}, f32[128,128]{1,0:T(8,128)}, /*index=5*/f32[128]{...) while((s32[]{:T(128)}, f32[8,128,256]{2,0,1:T(8,128)}, ...), condition=%wide.region_18.19_spmd.clone, body=%wide.region_14.18_spmd.clone.sunk | while | flops 503752960 | bytes 42401896 | solution.py:128
  360.4 3.3 collective-permute-start.11
  369.1 80.5 %psum.87 = f32[]{:T(128)} all-reduce(f32[]{:T(128)} %get-tuple-element.439), channel_id=1, replica_groups=mesh['lon'=16,'lat'=16] {'lon','lat'}, use_global_device_ids=true, to_apply=%region_9.10 | all-reduce | flops 1 | bytes 8 | tf_op jit(solution)/shard_map/psum | solution.py:206
  451.6 72.4 %psum.88 = f32[]{:T(128)} all-reduce(f32[]{:T(128)} %multiply_reduce_fusion.2), channel_id=1, replica_groups=mesh['lon'=16,'lat'=16] {'lon','lat'}, use_global_device_ids=true, to_apply=%region_11.12 | all-reduce | flops 1 | bytes 8 | tf_op jit(solution)/shard_map/psum | solution.py:132
  532.0 3.6 collective-permute-start.15
  541.0 80.6 %all-reduce.4 = (f32[]{:T(128)}, f32[128,32]{0,1:T(8,128)}, f32[128]{0:T(128)}, f32[128]{0:T(128)}, f32[8,128]{1,0:T(8,128)}, /*index=5*/f32[8]{0:T(128)}) all-reduce(f32[]{:T(128)} %fusion.42, f32[128,32]{0,1:T(8,128)} %broadcast_multiply_fusion.1, f32[128]{0:T(128)} %get-tuple-element.481, ...), channel_id=1, replica_groups=mesh['lon'=16,'lat'=16] {'lon','lat'}, use_global_device_ids=true, to_apply=%region_13.14 | all-reduce | flops 5385 | bytes 43080 | tf_op jit(solution)/shard_map/psum | solution.py:206
  627.3 5.3 collective-permute-start.19
  635.3 7.7 fusion.25
  643.0 9.0 %fusion.21 = f32[8,129,256]{1,2,0:T(8,128)S(1)} fusion(f32[33,132,260]{1,2,0:T(8,128)} %copy-done.2, f32[129,256]{0,1:T(8,128)S(1)} %slice_subtract_fusion.5), kind=kLoop, calls=%fused_computation.40 | loop fusion | flops 2377728 | bytes 8586240 | tf_op jit(solution)/shard_map/mul | solution.py:228
  653.9 215.6 %all-reduce.8.cloned.1.call-done = f32[128,128]{1,0:T(8,128)} async-done(((f32[128,128]{1,0:T(8,128)}), f32[128,128]{1,0:T(8,128)}) %all-reduce.8.cloned.1.call-update) | async-done | bytes 65552 | tf_op jit(solution)/shard_map/psum | solution.py:282
  (480 shorter events, 172.7 us)
Async XLA Ops:
  7.2 862.3 %all-reduce.8.cloned.1.call-start = ((), (), s32[]{:S(2)}) async-start(), calls=%async_computation | async-start | bytes 131072 | tf_op jit(solution)/shard_map/psum | solution.py:282
  21.3 14.9 %collective-permute-start = (f32[33,128,2]{1,2,0:T(2,128)S(1)}, f32[33,128,2]{1,2,0:T(2,128)S(1)}, u32[]{:S(2)}, u32[]{:S(2)}) collective-permute-start(f32[33,128,2]{1,2,0:T(2,128)S(1)} %get-tuple-element.459), channel_id=1, source_target_pairs={{0,16},{16,32},{32,48},{48,64},{64,80},{80,96},{96,112},{112,128},... | collective-permute-start | bytes 101384 | tf_op jit(solution)/shard_map/ppermute | solution.py:26
  24.0 12.2 %collective-permute-start.1 = (f32[33,128,2]{1,2,0:T(2,128)S(1)}, f32[33,128,2]{1,2,0:T(2,128)S(1)}, u32[]{:S(2)}, u32[]{:S(2)}) collective-permute-start(f32[33,128,2]{1,2,0:T(2,128)S(1)} %get-tuple-element.460), channel_id=1, source_target_pairs={{16,0},{32,16},{48,32},{64,48},{80,64},{96,80},{112,96},{128,112},... | collective-permute-start | bytes 101384 | tf_op jit(solution)/shard_map/ppermute | solution.py:29
  47.4 12.3 %collective-permute-start.2 = (f32[33,2,260]{2,1,0:T(2,128)S(1)}, f32[33,2,260]{2,1,0:T(2,128)S(1)}, u32[]{:S(2)}, u32[]{:S(2)}) collective-permute-start(f32[33,2,260]{2,1,0:T(2,128)S(1)} %copy.43), channel_id=1, source_target_pairs={{0,1},{1,2},{2,3},{3,4},{4,5},{5,6},{6,7},{7,8},{8,9},{9,10},{10,1... | collective-permute-start | bytes 205928 | tf_op jit(solution)/shard_map/ppermute | solution.py:26
  52.1 10.5 %collective-permute-start.3 = (f32[33,2,260]{2,1,0:T(2,128)S(1)}, f32[33,2,260]{2,1,0:T(2,128)S(1)}, u32[]{:S(2)}, u32[]{:S(2)}) collective-permute-start(f32[33,2,260]{2,1,0:T(2,128)S(1)} %copy.44), channel_id=1, source_target_pairs={{1,0},{2,1},{3,2},{4,3},{5,4},{6,5},{7,6},{8,7},{9,8},{10,9},{11,1... | collective-permute-start | bytes 205928 | tf_op jit(solution)/shard_map/ppermute | solution.py:29
  78.5 3.9 collective-permute-start.4
  79.9 3.0 collective-permute-start.5
  83.7 8.3 collective-permute-start.6
  83.7 8.3 collective-permute-start.7
  254.5 102.8 %collective-permute-start.8 = (f32[128,1]{0,1:T(1,128)S(1)}, f32[128,1]{0,1:T(1,128)S(1)}, u32[]{:S(2)}, u32[]{:S(2)}) collective-permute-start(f32[128,1]{0,1:T(1,128)S(1)} %get-tuple-element.476), channel_id=1, source_target_pairs={{0,16},{16,32},{32,48},{48,64},{64,80},{80,96},{96,112},{112,128},... | collective-permute-start | bytes 1544 | tf_op jit(solution)/shard_map/ppermute | solution.py:26
  255.1 102.3 %collective-permute-start.9 = (f32[128,1]{0,1:T(1,128)S(1)}, f32[128,1]{0,1:T(1,128)S(1)}, u32[]{:S(2)}, u32[]{:S(2)}) collective-permute-start(f32[128,1]{0,1:T(1,128)S(1)} %get-tuple-element.477), channel_id=1, source_target_pairs={{16,0},{32,16},{48,32},{64,48},{80,64},{96,80},{112,96},{128,112},... | collective-permute-start | bytes 1544 | tf_op jit(solution)/shard_map/ppermute | solution.py:29
  357.3 168.0 %copy-start.11 = (f32[128,256]{0,1:T(8,128)S(1)}, f32[128,256]{0,1:T(8,128)}, u32[]{:S(2)}) copy-start(f32[128,256]{0,1:T(8,128)} %copy-done.10) | copy-start | bytes 393220
  357.3 169.1 %copy-start.29 = (f32[128]{0:T(128)S(1)}, f32[128]{0:T(128)}, u32[]{:S(2)}) copy-start(f32[128]{0:T(128)} %get-tuple-element.277) | copy-start | bytes 1540
  358.4 177.2 %copy-start.35 = (f32[8]{0:T(128)S(1)}, f32[8]{0:T(128)}, u32[]{:S(2)}) copy-start(f32[8]{0:T(128)} %get-tuple-element.279) | copy-start | bytes 100
  358.5 7.6 collective-permute-start.10
  360.4 5.7 collective-permute-start.11
  525.4 1.8 collective-permute-start.12
  526.5 3.0 collective-permute-start.13
  530.2 7.8 collective-permute-start.14
  532.0 6.0 collective-permute-start.15
  624.0 2.5 collective-permute-start.16
  624.1 3.0 collective-permute-start.17
  627.2 7.6 collective-permute-start.18
  627.3 7.6 collective-permute-start.19
  (125 other events, 790.3 us)
Sparse Core Ops, SparseCore 0:
  634.2 235.2 all-reduce.7
where the time goes:
time: 887 us; the launch traced here: 878 us
  blocking collectives  388 us (44%)
  waiting for transfers between devices  221 us (25%)
  local copies, waits for them, and re-layouts  72.9 us (8%)
  matrix products  68.2 us (8%)
  other arithmetic  66.4 us (7%)
  starting transfers between devices  38.8 us (4%)
  between operations  21.7 us (2%)
    psum x3, blocking collectives, squares(): return lax.psum(jnp.sum(values * values), ('lon', 'lat'))  227 us
    psum x1, waiting for transfers between devices, local(): lax.psum((cumulative_sums_list[0] * multiplier_amount, cumulative_sums_li...  216 us
    psum x2, blocking collectives, local(): alpha = norm_now / lax.psum(jnp.sum(direction * image), ('lon', 'lat'))  161 us
    dot_general x24, matrix products, contract_columns(): lax.dot_general(left, right, (((1,), (1,)), ((), ())), preferred_element_...  33.2 us
    ppermute x10, starting transfers between devices, extended(): lax.ppermute(lax.slice_in_dim(block, 0, width, axis=dim), axis, backward)  28.1 us
    unnamed x80, local copies, waits for them, and re-layouts  23.1 us
  transfers between devices with their start and end apart: 21, of which 8 were waited for; matrix products, arithmetic and copies ran while one was open for 16% of the time, Pallas kernels for 0%

commit v1 on v0

v1 whole, which is shorter than its diff:
```python
import functools
import math

import jax
import jax.numpy as jnp
from jax import lax
from jax.experimental import pallas as pl
from jax.experimental.pallas import tpu as pltpu
from jax.sharding import PartitionSpec as P

LEVELS = 8
HID = 128
FIN = 32
ROWS = 128
COLS = 256
EXT_ROWS = ROWS + 16
EXT_COLS = COLS + 128
BLOCKS = ROWS // 8

SIGMA = 0.5
TRANSPORT_TICK = 0.2
KAPPA_FLOOR = 0.02
KAPPA_SPAN = 0.4
GRADIENT_GAIN = 16.0

CENTRE = 32.5
HALF_WIDTH = 32.0

TRACER_LANE, TRACER_WIDE = 0, 2
ZONAL_LANE, MERIDIAN_LANE, WET_LANE, DEPTH_LANE, WIDE = 16, 48, 80, 112, 4

ROW_INNER = 128
ROW_OUTER = 160
ROW_OUTER_BIAS = 168
ROW_BIAS = 176
ROW_GRAM = 184
SUM_ROWS = 256

F32 = jnp.float32
BF16 = jnp.bfloat16
VMEM_LIMIT = 48 * 1024 * 1024


def iota(shape, axis):
    return lax.broadcasted_iota(jnp.int32, shape, axis)


def turn(value, shift, axis):
    shift %= value.shape[axis]
    return pltpu.roll(value, shift, axis) if shift else value


def east(value):
    return turn(value, -1, value.ndim - 1)


def west(value):
    return turn(value, 1, value.ndim - 1)


def north(value):
    return turn(value, -1, value.ndim - 2)


def south(value):
    return turn(value, 1, value.ndim - 2)


def dot(left, right):
    return lax.dot_general(left, right, (((1,), (0,)), ((), ())), preferred_element_type=F32)


def dot_nt(left, right):
    return lax.dot_general(left, right, (((1,), (1,)), ((), ())), preferred_element_type=F32)


def pack_kernel(thermal, zonal, meridian, sea, depth, to_east, to_west, to_north, to_south):
    lane = iota((ROWS, 128), 1)
    low = iota((8, COLS), 0) < 4
    high_edge = jnp.zeros((ROWS, 128), F32)
    low_edge = jnp.zeros((ROWS, 128), F32)

    def place(edges, field, lane_start, wide):
        high, low_ = edges
        mask = jnp.logical_and(lane >= lane_start, lane < lane_start + wide)
        high = jnp.where(mask, turn(field[:, 128:], lane_start + wide, 1), high)
        low_ = jnp.where(mask, turn(field[:, :128], lane_start, 1), low_)
        return high, low_

    edges = (high_edge, low_edge)
    for k in range(LEVELS):
        wet = sea[k].astype(F32)
        tracer = thermal[k] * wet
        u = zonal[k]
        v = meridian[k]
        edges = place(edges, tracer, TRACER_LANE + TRACER_WIDE * k, TRACER_WIDE)
        edges = place(edges, u, ZONAL_LANE + WIDE * k, WIDE)
        edges = place(edges, v, MERIDIAN_LANE + WIDE * k, WIDE)
        edges = place(edges, wet, WET_LANE + WIDE * k, WIDE)
        to_north[k] = jnp.where(low, turn(v[ROWS - 8 :], 4, 0), tracer[ROWS - 8 :])
        to_north[LEVELS + k] = jnp.where(low, turn(wet[ROWS - 8 :], 4, 0), u[ROWS - 8 :])
        to_south[k] = jnp.where(low, tracer[:8], turn(v[:8], 4, 0))
        to_south[LEVELS + k] = jnp.where(low, u[:8], turn(wet[:8], 4, 0))
    floor = depth[...].astype(F32)
    edges = place(edges, floor, DEPTH_LANE, WIDE)
    to_north[2 * LEVELS] = floor[ROWS - 8 :]
    to_south[2 * LEVELS] = floor[:8]
    to_east[...] = edges[0]
    to_west[...] = edges[1]


def rows_extended(inside, south_tile, north_tile, second):
    if second:
        south_tile = turn(south_tile, 4, 0)
        north_tile = turn(north_tile, 4, 0)
    return jnp.concatenate([south_tile, inside, north_tile], axis=0)


def edge_columns(west_tile, east_tile, lane_start, wide):
    ahead = turn(east_tile, -lane_start, 1)
    behind = turn(west_tile, -wide - lane_start, 1)
    return jnp.where(iota(ahead.shape, 1) < 64, ahead, behind)


def closure_kernel(
    thermal, sea, depth, adjoint, south_edge, north_edge, west_edge, east_edge,
    w1, b1, w2, b2, w3, b3,
    base, sums,
    tracer_ext, tracer_cols, w1_big, w2_t, w3_big, w3_t, b1_wide, b2_wide,
    first, left, right, second, outer, slope1, slope2, grad, grad_outer, bias1, bias2, bias3,
):
    for k in range(LEVELS):
        tracer_ext[k, 0:8] = south_edge[k]
        tracer_ext[k, 8 : ROWS + 8] = thermal[k] * sea[k].astype(F32)
        tracer_ext[k, ROWS + 8 :] = north_edge[k]
        tracer_cols[k] = edge_columns(
            west_edge[...], east_edge[...], TRACER_LANE + TRACER_WIDE * k, TRACER_WIDE
        )
    inner_weight = w1[...].astype(BF16)
    hidden_weight = w2[...].astype(BF16)
    outer_weight = w3[...].astype(BF16)
    spread = (iota((FIN, 8 * FIN), 1) // 8 == iota((FIN, 8 * FIN), 0)).astype(BF16)
    inner_wide = dot(inner_weight, spread)
    inner_lane = iota((HID + FIN, 8 * FIN), 1)
    inner_row = iota((HID + FIN, 8 * FIN), 0) - HID
    stacked = jnp.concatenate([inner_wide, (inner_lane[HID:] // 8 == inner_row[HID:]).astype(F32)], 0)
    spread3 = (iota((LEVELS, 64), 1) // 8 == iota((LEVELS, 64), 0)).astype(BF16)
    outer_tall = lax.dot_general(
        spread3, outer_weight, (((0,), (0,)), ((), ())), preferred_element_type=F32
    )
    outer_wide = lax.dot_general(
        outer_weight, spread3, (((0,), (0,)), ((), ())), preferred_element_type=F32
    )
    pick_lane = iota((16, 64), 1)
    pick = (pick_lane // 8 == iota((16, 64), 0)).astype(F32)
    stacked3 = jnp.concatenate([outer_wide, pick], 0)
    lane3 = iota((HID + 16, 64), 1)
    row3 = iota((64, HID), 0)
    for r in range(8):
        w1_big[r] = jnp.where(inner_lane % 8 == r, stacked, 0.0).astype(BF16)
        w3_t[r] = jnp.where(lane3 % 8 == r, stacked3, 0.0).astype(BF16)
        w3_big[:, r * HID : (r + 1) * HID] = jnp.where(row3 % 8 == r, outer_tall, 0.0).astype(BF16)
    w2_t[...] = w2[...].T.astype(BF16)
    b1_wide[...] = jnp.broadcast_to(b1[...], (HID, COLS))
    b2_wide[...] = jnp.broadcast_to(b2[...], (HID, COLS))
    grad[...] = jnp.zeros_like(grad)
    grad_outer[...] = jnp.zeros_like(grad_outer)
    bias1[...] = jnp.zeros_like(bias1)
    bias2[...] = jnp.zeros_like(bias2)
    bias3[...] = jnp.zeros_like(bias3)
    level = iota((LEVELS, 8, COLS), 0).astype(F32)
    b3_cube = b3[...]

    def step(j, carry):
        start = pl.multiple_of(j * 8, 8)
        tall = tracer_ext[:, pl.ds(start, 24), :]
        tracer = tall[:, 8:16]
        wet = sea[:, pl.ds(start, 8), :].astype(F32)
        floor = depth[pl.ds(start, 8), :].astype(F32)
        wide = jnp.concatenate([tracer, tracer_cols[:, pl.ds(start, 8), :]], axis=2)
        zonal_slope = 0.5 * (east(wide)[:, :, :COLS] - west(wide)[:, :, :COLS])
        meridian_slope = 0.5 * (north(tall)[:, 8:16] - south(tall)[:, 8:16])
        clearance = wet * (floor[None] - level) * (1.0 / LEVELS)
        features = (
            jnp.concatenate([tracer, zonal_slope, meridian_slope, clearance], axis=0)
            .reshape(8 * FIN, COLS)
            .astype(BF16)
        )
        for r in range(8):
            z = dot(w1_big[r], features)
            value = jnp.tanh(z[:HID] + b1_wide[...])
            right[r, HID:] = value.astype(BF16)
            slope1[r] = 1.0 - value * value
            left[r, HID:] = z[HID:].astype(BF16)
        for r in range(8):
            value = jnp.tanh(dot(hidden_weight, right[r, HID:]) + b2_wide[...])
            second[r] = value.astype(BF16)
            slope2[r] = 1.0 - value * value
        squash = jax.nn.sigmoid(
            dot(w3_big[...], second[...].reshape(8 * HID, COLS)).reshape(LEVELS, 8, COLS) + b3_cube
        )
        kappa = KAPPA_FLOOR + KAPPA_SPAN * squash
        jump = tracer[1:] - tracer[:-1]
        pair_jump = wet[:-1] * wet[1:] * jump
        adj = adjoint[:, pl.ds(start, 8), :]
        bond = pair_jump * (adj[:-1] - adj[1:])
        none = jnp.zeros((1, 8, COLS), F32)
        pull = 0.5 * (jnp.concatenate([bond, none], 0) + jnp.concatenate([none, bond], 0))
        down = 0.5 * (kappa[:-1] + kappa[1:]) * pair_jump
        mixing = jnp.concatenate([down, none], 0) - jnp.concatenate([none, down], 0)
        base[:, pl.ds(start, 8), :] = wet * (tracer + mixing)
        outer_term = pull * KAPPA_SPAN * squash * (1.0 - squash)
        bias3[...] += outer_term
        outer_grad = outer_term.reshape(64, COLS).astype(BF16)
        total = grad[...]
        total_outer = grad_outer[...]
        total1 = bias1[...]
        total2 = bias2[...]
        for r in range(8):
            back = dot(w3_t[r], outer_grad)
            hidden_term = back[:HID] * slope2[r]
            total2 = total2 + hidden_term
            hidden_grad = hidden_term.astype(BF16)
            left[r, :HID] = hidden_grad
            outer[r] = back[HID:].astype(BF16)
            inner_term = dot(w2_t[...], hidden_grad) * slope1[r]
            total1 = total1 + inner_term
            right[r, :HID] = inner_term.astype(BF16)
            total = total + dot_nt(left[r], right[r])
            total_outer = total_outer + dot_nt(outer[r], second[r])
        grad[...] = total
        grad_outer[...] = total_outer
        bias1[...] = total1
        bias2[...] = total2
        return carry

    lax.fori_loop(0, BLOCKS, step, 0)
    sums[0:HID] = grad[0:HID, HID:]
    sums[ROW_INNER : ROW_INNER + FIN] = grad[HID:, :HID]
    sums[ROW_OUTER : ROW_OUTER + LEVELS] = grad_outer[0:LEVELS]
    outer_bias = jnp.sum(bias3[...], axis=1)
    sums[ROW_OUTER_BIAS : ROW_OUTER_BIAS + LEVELS] = outer_bias[:, :128] + outer_bias[:, 128:]
    inner_row_sum = jnp.sum((bias1[:, :128] + bias1[:, 128:]).T, axis=0, keepdims=True)
    hidden_row_sum = jnp.sum((bias2[:, :128] + bias2[:, 128:]).T, axis=0, keepdims=True)
    sums[ROW_BIAS : ROW_BIAS + 8] = jnp.concatenate(
        [inner_row_sum, hidden_row_sum, jnp.zeros((6, 128), F32)], 0
    )


def field_extended(inside, south_tile, north_tile, second, west_tile, east_tile, lane_start, wide):
    tall = rows_extended(inside, south_tile, north_tile, second)
    return jnp.concatenate([tall, edge_columns(west_tile, east_tile, lane_start, wide)], axis=1)


def gram_kernel(
    zonal, meridian, sea, depth, south_edge, north_edge, west_edge, east_edge,
    south_corner, north_corner, sums,
    basis, summed,
):
    west_tile = jnp.concatenate([south_corner[:, :128], west_edge[...], north_corner[:, :128]], 0)
    east_tile = jnp.concatenate([south_corner[:, 128:], east_edge[...], north_corner[:, 128:]], 0)

    def extended(inside, index, second, lane_start):
        return field_extended(
            inside, south_edge[index], north_edge[index], second, west_tile, east_tile, lane_start, WIDE
        )

    east_transport = jnp.zeros((EXT_ROWS, EXT_COLS), F32)
    north_transport = jnp.zeros((EXT_ROWS, EXT_COLS), F32)
    for k in range(LEVELS):
        wet = extended(sea[k].astype(F32), LEVELS + k, True, WET_LANE + WIDE * k)
        east_transport = east_transport + wet * east(wet) * extended(
            zonal[k], LEVELS + k, False, ZONAL_LANE + WIDE * k
        )
        north_transport = north_transport + wet * north(wet) * extended(
            meridian[k], k, True, MERIDIAN_LANE + WIDE * k
        )
    source = -(
        (east_transport - west(east_transport)) + (north_transport - south(north_transport))
    )
    floor = extended(depth[...].astype(F32), 2 * LEVELS, False, DEPTH_LANE)
    east_depth = jnp.minimum(floor, east(floor))
    north_depth = jnp.minimum(floor, north(floor))
    west_depth = west(east_depth)
    south_depth = south(north_depth)

    def operate(field):
        return (
            SIGMA * field
            + east_depth * (field - east(field))
            + west_depth * (field - west(field))
            + north_depth * (field - north(field))
            + south_depth * (field - south(field))
        )

    image0 = operate(source)
    first = (image0 - CENTRE * source) * (1.0 / HALF_WIDTH)
    image1 = operate(first)
    second = (image1 - CENTRE * first) * (2.0 / HALF_WIDTH) - source
    image2 = operate(second)
    basis[0] = source
    basis[1] = first
    basis[2] = second

    def product(a, b):
        inside = jnp.sum(a[8 : ROWS + 8, :COLS] * b[8 : ROWS + 8, :COLS], axis=0, keepdims=True)
        return inside[:, :128] + inside[:, 128:]

    rows = [
        product(source, image0),
        product(first, image0),
        product(second, image0),
        product(first, image1),
        product(second, image1),
        product(second, image2),
        product(source, source),
        product(first, source),
        product(second, source),
    ]
    summed[0:ROW_GRAM] = sums[0:ROW_GRAM]
    summed[ROW_GRAM : ROW_GRAM + 16] = jnp.concatenate(rows + [jnp.zeros((7, 128), F32)], 0)
    summed[ROW_GRAM + 16 :] = jnp.zeros((SUM_ROWS - ROW_GRAM - 16, 128), F32)


def galerkin(h00, h01, h02, h11, h12, h22, g0, g1, g2):
    tiny = 1e-6

    def pivot(value, scale):
        good = value > tiny * scale
        return jnp.where(good, 1.0 / jnp.where(good, value, 1.0), 0.0)

    p0 = pivot(h00, 0.0)
    l10 = h01 * p0
    l20 = h02 * p0
    d1 = h11 - l10 * h01
    p1 = pivot(d1, h11)
    s21 = h12 - l20 * h01
    l21 = s21 * p1
    d2 = h22 - l20 * h02 - l21 * s21
    p2 = pivot(d2, h22)
    z0 = g0
    z1 = g1 - l10 * z0
    z2 = g2 - l20 * z0 - l21 * z1
    y2 = z2 * p2
    y1 = z1 * p1 - l21 * y2
    y0 = z0 * p0 - l10 * y1 - l20 * y2
    return y0, y1, y2


def final_kernel(
    scale, thermal, zonal, meridian, sea, base, south_edge, north_edge, west_edge, east_edge, basis, totals,
    revised, height_out, grad1, bias1, grad2, bias2, grad3, bias3,
):
    gram = jnp.sum(totals[ROW_GRAM : ROW_GRAM + 16], axis=1, keepdims=True)
    y0, y1, y2 = galerkin(*[gram[i : i + 1] for i in range(9)])
    height = y0 * basis[0] + y1 * basis[1] + y2 * basis[2]
    height_out[...] = height[8 : ROWS + 8, :COLS]
    east_fall = east(height) - height
    north_fall = north(height) - height
    blank = jnp.zeros((8, 128), F32)
    west_tile = jnp.concatenate([blank, west_edge[...], blank], 0)
    east_tile = jnp.concatenate([blank, east_edge[...], blank], 0)
    for k in range(LEVELS):
        inside_wet = sea[k].astype(F32)
        wet = field_extended(
            inside_wet, south_edge[LEVELS + k], north_edge[LEVELS + k], True,
            west_tile, east_tile, WET_LANE + WIDE * k, WIDE,
        )
        tracer = field_extended(
            thermal[k] * inside_wet, south_edge[k], north_edge[k], False,
            west_tile, east_tile, TRACER_LANE + TRACER_WIDE * k, TRACER_WIDE,
        )
        u = jnp.concatenate(
            [zonal[k], edge_columns(west_edge[...], east_edge[...], ZONAL_LANE + WIDE * k, WIDE)], 1
        )
        v = rows_extended(meridian[k], south_edge[k], north_edge[k], True)
        mid_wet = wet[8 : ROWS + 8]
        mid = tracer[8 : ROWS + 8]
        pair = mid + east(mid)
        face = (8.0 * pair - (west(pair) + east(pair))) * (1.0 / 12.0)
        flux = mid_wet * east(mid_wet) * (u - east_fall[8 : ROWS + 8]) * face
        spread = (flux - west(flux))[:, :COLS]
        mid_wet = wet[:, :COLS]
        mid = tracer[:, :COLS]
        pair = mid + north(mid)
        face = (8.0 * pair - (south(pair) + north(pair))) * (1.0 / 12.0)
        flux = mid_wet * north(mid_wet) * (v - north_fall[:, :COLS]) * face
        spread = spread + (flux - south(flux))[8 : ROWS + 8]
        revised[k] = base[k] - TRANSPORT_TICK * (inside_wet * spread)
    grad2[...] = totals[0:HID] * scale
    grad1[...] = (totals[ROW_INNER : ROW_INNER + FIN] * scale).T
    grad3[...] = totals[ROW_OUTER : ROW_OUTER + LEVELS] * scale
    bias1[...] = totals[ROW_BIAS : ROW_BIAS + 1] * scale
    bias2[...] = totals[ROW_BIAS + 1 : ROW_BIAS + 2] * scale
    bias3[...] = jnp.sum(totals[ROW_OUTER_BIAS : ROW_OUTER_BIAS + LEVELS], axis=1, keepdims=True) * scale


def struct(*shape, dtype=F32):
    return jax.ShapeDtypeStruct(shape, dtype)


def call(kernel, out_shape, scratch=(), flops=0, transcendentals=0, nbytes=0):
    return pl.pallas_call(
        kernel,
        out_shape=out_shape,
        scratch_shapes=list(scratch),
        compiler_params=pltpu.CompilerParams(vmem_limit_bytes=VMEM_LIMIT),
        cost_estimate=pl.CostEstimate(
            flops=flops, transcendentals=transcendentals, bytes_accessed=nbytes
        ),
    )


def share(value, axis):
    count = lax.axis_size(axis)
    copies = jnp.broadcast_to(value[None], (count,) + value.shape)
    return jnp.sum(lax.all_to_all(copies, axis, 0, 0), axis=0)


def total_over_devices(value):
    count = lax.axis_size("lon")
    parts = value.reshape(count, value.shape[0] // count, value.shape[1])
    part = jnp.sum(lax.all_to_all(parts, "lon", 0, 0), axis=0)
    part = share(part, "lat")
    copies = jnp.broadcast_to(part[None], (count,) + part.shape)
    return lax.all_to_all(copies, "lon", 0, 0).reshape(value.shape)


def local(thermal, zonal, meridian, sea, depth, adjoint, w1, b1, w2, b2, w3, b3):
    lons, lats = lax.axis_size("lon"), lax.axis_size("lat")
    ring = [(i, (i + 1) % lons) for i in range(lons)]
    line = [(i, i + 1) for i in range(lats - 1)]

    def back(pairs):
        return [(target, source) for source, target in pairs]

    to_east, to_west, to_north, to_south = call(
        pack_kernel,
        (struct(ROWS, 128), struct(ROWS, 128), struct(17, 8, COLS), struct(17, 8, COLS)),
        flops=4_000_000,
        nbytes=5_000_000,
    )(thermal, zonal, meridian, sea, depth)
    west_edge = lax.ppermute(to_east, "lon", ring)
    east_edge = lax.ppermute(to_west, "lon", back(ring))
    south_edge = lax.ppermute(to_north, "lat", line)
    north_edge = lax.ppermute(to_south, "lat", back(line))
    edges = jnp.concatenate([west_edge, east_edge], axis=1)
    south_corner = lax.ppermute(edges[ROWS - 8 :], "lat", line)
    north_corner = lax.ppermute(edges[:8], "lat", back(line))

    base, sums = call(
        closure_kernel,
        (struct(LEVELS, ROWS, COLS), struct(ROW_GRAM, 128)),
        scratch=[
            pltpu.VMEM((LEVELS, EXT_ROWS, COLS), F32),
            pltpu.VMEM((LEVELS, ROWS, 128), F32),
            pltpu.VMEM((8, HID + FIN, 8 * FIN), BF16),
            pltpu.VMEM((HID, HID), BF16),
            pltpu.VMEM((64, 8 * HID), BF16),
            pltpu.VMEM((8, HID + 16, 64), BF16),
            pltpu.VMEM((HID, COLS), F32),
            pltpu.VMEM((HID, COLS), F32),
            pltpu.VMEM((8, HID, COLS), BF16),
            pltpu.VMEM((8, HID + FIN, COLS), BF16),
            pltpu.VMEM((8, 2 * HID, COLS), BF16),
            pltpu.VMEM((8, HID, COLS), BF16),
            pltpu.VMEM((8, 16, COLS), BF16),
            pltpu.VMEM((8, HID, COLS), F32),
            pltpu.VMEM((8, HID, COLS), F32),
            pltpu.VMEM((HID + FIN, COLS), F32),
            pltpu.VMEM((16, HID), F32),
            pltpu.VMEM((HID, COLS), F32),
            pltpu.VMEM((HID, COLS), F32),
            pltpu.VMEM((LEVELS, 8, COLS), F32),
        ],
        flops=8_000_000_000,
        transcendentals=9_000_000,
        nbytes=5_000_000,
    )(
        thermal, sea, depth, adjoint, south_edge, north_edge, west_edge, east_edge,
        w1, b1[:, None], w2, b2[:, None], w3, jnp.broadcast_to(b3[:, None, None], (LEVELS, 8, COLS)),
    )
    basis, summed = call(
        gram_kernel,
        (struct(3, EXT_ROWS, EXT_COLS), struct(SUM_ROWS, 128)),
        flops=20_000_000,
        nbytes=5_000_000,
    )(
        zonal, meridian, sea, depth, south_edge, north_edge, west_edge, east_edge,
        south_corner, north_corner, sums,
    )
    totals = total_over_devices(summed)
    scale = GRADIENT_GAIN / math.sqrt(ROWS * lats * COLS * lons)
    out = call(
        functools.partial(final_kernel, scale),
        (
            struct(LEVELS, ROWS, COLS),
            struct(ROWS, COLS),
            struct(HID, FIN),
            struct(1, HID),
            struct(HID, HID),
            struct(1, HID),
            struct(LEVELS, HID),
            struct(LEVELS, 1),
        ),
        flops=20_000_000,
        nbytes=8_000_000,
    )(
        thermal, zonal, meridian, sea, base, south_edge, north_edge, west_edge, east_edge, basis, totals
    )
    revised, height, grad1, bias1, grad2, bias2, grad3, bias3 = out
    return (
        revised,
        height,
        grad1,
        bias1.reshape(HID),
        grad2,
        bias2.reshape(HID),
        grad3,
        bias3.reshape(LEVELS),
    )


def solution(mesh):
    cube, plane, whole = P(None, "lat", "lon"), P("lat", "lon"), P()
    return jax.shard_map(
        local,
        mesh=mesh,
        in_specs=(cube, cube, cube, cube, plane, cube) + (whole,) * 6,
        out_specs=(cube, plane) + (whole,) * 6,
        check_vma=False,
    )
```

time: 887 us -> 136 us (0.15)
  blocking collectives: 388 us -> 44.4 us
  waiting for transfers between devices: 221 us -> 0.02 us
  matrix products: 68.2 us -> 0 us
  other arithmetic: 66.4 us -> 3.67 us
  local copies, waits for them, and re-layouts: 72.9 us -> 20 us
  Pallas kernels: 0 us -> 52.6 us
  starting transfers between devices: 38.8 us -> 13.8 us
  between operations: 21.7 us -> 0.92 us
    psum x5 -> x0, blocking collectives: 388 us -> none  [the longest x3 227 us: squares(): return lax.psum(jnp.sum(values * values), ('lon', 'lat'))]
    psum x1 -> x0, waiting for transfers between devices: 216 us -> none  [local(): lax.psum((cumulative_sums_list[0] * multiplier_amount, cumulative_sums_li...]
    dot_general x64 -> x0, matrix products: 68.2 us -> none  [the longest x24 33.2 us: contract_columns(): lax.dot_general(left, right, (((1,), (1,)), ((), ())), preferred_element_...]
    pallas_call x0 -> x4, Pallas kernels: none -> 52.6 us  [the longest x1 42.6 us: local(): call(closure_kernel, (struct(LEVELS, ROWS, COLS), struct(ROW_GRAM, 128)),...]
    all_to_all x0 -> x3, blocking collectives: none -> 44.4 us  [the longest x1 21.1 us: share(): return jnp.sum(lax.all_to_all(copies, axis, 0, 0), axis=0)]
    mul x19 -> x0, other arithmetic: 32.3 us -> none  [the longest x1 9.02 us: local(): north_flux = north_wet * meridional_fixed * north_face]
    ppermute x20 -> x6, starting transfers between devices: 38.7 us -> 13.8 us  [the longest x1 4.79 us: local(): south_corner = lax.ppermute(edges[ROWS - 8:], 'lat', line)]
    slice x13 -> x1, local copies, waits for them, and re-layouts: 18.2 us -> 0.01 us  [local(): north_corner = lax.ppermute(edges[:8], 'lat', back(line))]
  transfers between devices with their start and end apart: 21 -> 6, of which waited for: 8 -> 0; matrix products, arithmetic and copies ran while one was open for 16% -> 2% of each run, Pallas kernels for 0% -> 31%
where the time goes in v1:
time: 136 us; the launch traced here: 135 us
  Pallas kernels  52.6 us (39%)
  blocking collectives  44.4 us (33%)
  local copies, waits for them, and re-layouts  20 us (15%)
  starting transfers between devices  13.8 us (10%)
  other arithmetic  3.67 us (3%)
    pallas_call x1, Pallas kernels, local(): call(closure_kernel, (struct(LEVELS, ROWS, COLS), struct(ROW_GRAM, 128)),...  42.6 us
    all_to_all x1, blocking collectives, share(): return jnp.sum(lax.all_to_all(copies, axis, 0, 0), axis=0)  21.1 us
    unnamed x57, local copies, waits for them, and re-layouts  17.1 us
    all_to_all x1, blocking collectives, total_over_devices(): part = jnp.sum(lax.all_to_all(parts, 'lon', 0, 0), axis=0)  12.6 us
    all_to_all x1, blocking collectives, total_over_devices(): return lax.all_to_all(copies, 'lon', 0, 0).reshape(value.shape)  10.7 us
    pallas_call x1, Pallas kernels, local(): call(functools.partial(final_kernel, scale), (struct(LEVELS, ROWS, COLS),...  6.06 us
    ppermute x1, starting transfers between devices, local(): south_corner = lax.ppermute(edges[ROWS - 8:], 'lat', line)  4.79 us
    ppermute x1, starting transfers between devices, local(): south_edge = lax.ppermute(to_north, 'lat', line)  2.9 us
  transfers between devices with their start and end apart: 6, of which 0 were waited for; matrix products, arithmetic and copies ran while one was open for 2% of the time, Pallas kernels for 31%

profile of v1, /device:TPU:1, one launch (start us, length us, event | category | flops | bytes accessed | tf_op | source)
XLA Modules:
  0.0 135.4 jit_solution(15452663180975546924)
XLA Ops:
  0.6 1.2 copy-done
  1.9 1.2 copy-done.2
  3.1 1.2 copy-done.4
  4.3 1.2 copy-done.6
  5.5 0.9 copy-done.12
  6.4 1.2 shard_map.179
  7.7 2.8 %collective-permute-start.2 = (f32[128,128]{1,0:T(8,128)S(1)}, f32[128,128]{1,0:T(8,128)S(1)}, u32[]{:S(2)}, u32[]{:S(2)}) collective-permute-start(f32[128,128]{1,0:T(8,128)S(1)} %get-tuple-element.26), channel_id=1, source_target_pairs={{0,16},{16,32},{32,48},{48,64},{64,80},{80,96},{96,112},{112,128},... | collective-permute-start | bytes 196616 | tf_op jit(solution)/shard_map/ppermute | solution.py:443
  11.1 2.9 %collective-permute-start = (f32[17,8,256]{2,1,0:T(8,128)S(1)}, f32[17,8,256]{2,1,0:T(8,128)S(1)}, u32[]{:S(2)}, u32[]{:S(2)}) collective-permute-start(f32[17,8,256]{2,1,0:T(8,128)S(1)} %get-tuple-element.24), channel_id=1, source_target_pairs={{0,1},{1,2},{2,3},{3,4},{4,5},{5,6},{6,7},{7,8},{8,9},{9,10},{10,1... | collective-permute-start | bytes 417800 | tf_op jit(solution)/shard_map/ppermute | solution.py:445
  14.0 1.3 collective-permute-start.1
  18.9 1.4 %collective-permute-start.5 = (f32[8,256]{1,0:T(8,128)S(1)}, f32[8,256]{1,0:T(8,128)S(1)}, u32[]{:S(2)}, u32[]{:S(2)}) collective-permute-start(f32[8,256]{1,0:T(8,128)S(1)} %get-tuple-element.64), channel_id=1, source_target_pairs={{1,0},{2,1},{3,2},{4,3},{5,4},{6,5},{7,6},{8,7},{9,8},{10,9},{11,1... | collective-permute-start | bytes 24584 | tf_op jit(solution)/shard_map/ppermute | solution.py:449
  20.4 4.8 %collective-permute-start.4 = (f32[8,256]{1,0:T(8,128)S(1)}, f32[8,256]{1,0:T(8,128)S(1)}, u32[]{:S(2)}, u32[]{:S(2)}) collective-permute-start(f32[8,256]{1,0:T(8,128)S(1)} %get-tuple-element.65), channel_id=1, source_target_pairs={{0,1},{1,2},{2,3},{3,4},{4,5},{5,6},{6,7},{7,8},{8,9},{9,10},{10,1... | collective-permute-start | bytes 24584 | tf_op jit(solution)/shard_map/ppermute | solution.py:448
  25.3 1.2 copy-done.7
  26.5 1.2 copy-done.20
  28.6 42.6 %shard_map.180 = (f32[8,128,256]{2,1,0:T(8,128)S(1)}, f32[184,128]{1,0:T(8,128)S(1)}) custom-call(f32[8,128,256]{2,1,0:T(8,128)S(1)} %copy-done.7, s32[8,128,256]{2,1,0:T(8,128)S(1)} %copy-done.5, s32[128,256]{1,0:T(8,128)S(1)} %copy-done.13, f32[8,128,256]{2,1,0:T(8,128)S(1)} %copy-done.20, f32[17,8,256]{2,1,0:T(8,128)S(1)} %collective-permute-done.south_edge, ...), custom_call_target="tpu_custom_call" | custom-call | flops 8000000000 | bytes 5000000 | tf_op jit(solution)/shard_map/pallas_call | solution.py:451
  71.3 2.7 %shard_map.181 = (f32[3,144,384]{2,1,0:T(8,128)S(1)}, f32[256,128]{1,0:T(8,128)S(1)}) custom-call(f32[8,128,256]{2,1,0:T(8,128)S(1)} %copy-done.1, f32[8,128,256]{2,1,0:T(8,128)S(1)} %copy-done.3, s32[8,128,256]{2,1,0:T(8,128)S(1)} %copy-done.5, s32[128,256]{1,0:T(8,128)S(1)} %copy-done.13, f32[17,8,256]{2,1,0:T(8,128)S(1)} %collective-permute-done.south_edge, ...), custom_call_target="tpu_custom_call" | custom-call | flops 20000000 | bytes 5000000 | tf_op jit(solution)/shard_map/pallas_call | solution.py:483
  74.9 12.6 %all_to_all.15 = f32[16,16,128]{2,1,0:T(8,128)} all-to-all(f32[16,16,128]{2,1,0:T(8,128)S(1)} %bitcast.7), channel_id=1, replica_groups=mesh['lon'=16,'lat'=16] {'lon'}, dimensions={0} | all-to-all | bytes 262144 | tf_op jit(solution)/shard_map/all_to_all | solution.py:423
  87.5 1.5 %reduce_sum.18 = f32[16,128]{1,0:T(8,128)} reduce(f32[16,16,128]{2,1,0:T(8,128)} %all_to_all.15, f32[]{:T(128)} %constant.0.clone.1), dimensions={0}, to_apply=%region_0.0 | reduce | flops 30720 | bytes 139268 | tf_op jit(solution)/shard_map/reduce_sum | solution.py:423
  89.7 21.1 %all_to_all.16 = f32[16,16,128]{2,1,0:T(8,128)} all-to-all(f32[16,16,128]{2,1,0:T(8,128)S(1)} %broadcast_in_dim.13), channel_id=1, replica_groups=mesh['lon'=16,'lat'=16] {'lat'}, dimensions={0} | all-to-all | bytes 262144 | tf_op jit(solution)/shard_map/all_to_all | solution.py:417
  110.8 1.5 %reduce_sum.19 = f32[16,128]{1,0:T(8,128)} reduce(f32[16,16,128]{2,1,0:T(8,128)} %all_to_all.16, f32[]{:T(128)} %constant.0.clone.1), dimensions={0}, to_apply=%region_1.0 | reduce | flops 30720 | bytes 139268 | tf_op jit(solution)/shard_map/reduce_sum | solution.py:417
  113.0 10.7 %all_to_all.17 = f32[16,16,128]{2,1,0:T(8,128)S(1)} all-to-all(f32[16,16,128]{2,1,0:T(8,128)S(1)} %broadcast_in_dim.28), channel_id=1, replica_groups=mesh['lon'=16,'lat'=16] {'lon'}, dimensions={0} | all-to-all | bytes 262144 | tf_op jit(solution)/shard_map/all_to_all | solution.py:426
  123.7 1.2 copy-done.8
  124.9 1.1 copy-done.11
  126.0 6.1 %shard_map.182 = (f32[8,128,256]{2,1,0:T(8,128)}, f32[128,256]{1,0:T(8,128)}, f32[128,32]{1,0:T(8,128)S(1)}, f32[1,128]{1,0:T(1,128)}, f32[128,128]{1,0:T(8,128)...) custom-call(f32[8,128,256]{2,1,0:T(8,128)S(1)} %copy-done.8, f32[8,128,256]{2,1,0:T(8,128)S(1)} %copy-done.1, ...), custom_call_target="tpu_custom_call" | custom-call | flops 20000000 | bytes 8000000 | tf_op jit(solution)/shard_map/pallas_call | solution.py:494
  133.3 1.5 %copy.31 = f32[128,32]{0,1:T(8,128)} copy(f32[128,32]{1,0:T(8,128)} %copy-done.15) | data formatting | bytes 32768
  (62 shorter events, 9.3 us)
Async XLA Ops:
  0.6 1.2 copy-start
  1.9 1.2 copy-start.2
  3.1 1.2 copy-start.4
  6.4 8.8 %copy-start.23 = (f32[128,32]{0,1:T(8,128)S(1)}, f32[128,32]{0,1:T(8,128)}, u32[]{:S(2)}) copy-start(f32[128,32]{0,1:T(8,128)} %param.18) | copy-start | bytes 49156
  6.4 18.8 %copy-start.5 = (s32[8,128,256]{2,1,0:T(8,128)S(1)}, s32[8,128,256]{2,1,0:T(8,128)}, u32[]{:S(2)}) copy-start(s32[8,128,256]{2,1,0:T(8,128)} %sea.7) | copy-start | bytes 3145732
  7.7 11.1 %collective-permute-start.2 = (f32[128,128]{1,0:T(8,128)S(1)}, f32[128,128]{1,0:T(8,128)S(1)}, u32[]{:S(2)}, u32[]{:S(2)}) collective-permute-start(f32[128,128]{1,0:T(8,128)S(1)} %get-tuple-element.26), channel_id=1, source_target_pairs={{0,16},{16,32},{32,48},{48,64},{64,80},{80,96},{96,112},{112,128},... | collective-permute-start | bytes 196616 | tf_op jit(solution)/shard_map/ppermute | solution.py:443
  10.4 8.4 %collective-permute-start.3 = (f32[128,128]{1,0:T(8,128)S(1)}, f32[128,128]{1,0:T(8,128)S(1)}, u32[]{:S(2)}, u32[]{:S(2)}) collective-permute-start(f32[128,128]{1,0:T(8,128)S(1)} %get-tuple-element.27), channel_id=1, source_target_pairs={{16,0},{32,16},{48,32},{64,48},{80,64},{96,80},{112,96},{128,112},... | collective-permute-start | bytes 196616 | tf_op jit(solution)/shard_map/ppermute | solution.py:444
  11.1 14.1 %collective-permute-start = (f32[17,8,256]{2,1,0:T(8,128)S(1)}, f32[17,8,256]{2,1,0:T(8,128)S(1)}, u32[]{:S(2)}, u32[]{:S(2)}) collective-permute-start(f32[17,8,256]{2,1,0:T(8,128)S(1)} %get-tuple-element.24), channel_id=1, source_target_pairs={{0,1},{1,2},{2,3},{3,4},{4,5},{5,6},{6,7},{7,8},{8,9},{9,10},{10,1... | collective-permute-start | bytes 417800 | tf_op jit(solution)/shard_map/ppermute | solution.py:445
  14.0 11.2 %collective-permute-start.1 = (f32[17,8,256]{2,1,0:T(8,128)S(1)}, f32[17,8,256]{2,1,0:T(8,128)S(1)}, u32[]{:S(2)}, u32[]{:S(2)}) collective-permute-start(f32[17,8,256]{2,1,0:T(8,128)S(1)} %get-tuple-element.25), channel_id=1, source_target_pairs={{1,0},{2,1},{3,2},{4,3},{5,4},{6,5},{7,6},{8,7},{9,8},{10,9},{11,1... | collective-permute-start | bytes 417800 | tf_op jit(solution)/shard_map/ppermute | solution.py:446
  18.8 6.4 %copy-start.16 = (f32[128,1]{1,0:T(8,128)S(1)}, f32[128,1]{1,0:T(8,128)}, u32[]{:S(2)}) copy-start(f32[128,1]{1,0:T(8,128)} %copy.29.b1) | copy-start | bytes 1540
  18.8 6.4 %copy-start.17 = (f32[128,1]{1,0:T(8,128)S(1)}, f32[128,1]{1,0:T(8,128)}, u32[]{:S(2)}) copy-start(f32[128,1]{1,0:T(8,128)} %copy.30.b2) | copy-start | bytes 1540
  18.8 6.4 %copy-start.13 = (s32[128,256]{1,0:T(8,128)S(1)}, s32[128,256]{1,0:T(8,128)}, u32[]{:S(2)}) copy-start(s32[128,256]{1,0:T(8,128)} %depth.5) | copy-start | bytes 393220
  18.9 6.3 %copy-start.26 = (f32[8]{0:T(128)S(1)}, f32[8]{0:T(128)}, u32[]{:S(2)}) copy-start(f32[8]{0:T(128)} %param.23) | copy-start | bytes 100
  18.9 6.4 %copy-start.14 = (f32[128,32]{1,0:T(8,128)S(1)}, f32[128,32]{1,0:T(8,128)}, u32[]{:S(2)}) copy-start(f32[128,32]{1,0:T(8,128)} %copy.28.w1) | copy-start | bytes 49156
  18.9 52.3 %collective-permute-start.5 = (f32[8,256]{1,0:T(8,128)S(1)}, f32[8,256]{1,0:T(8,128)S(1)}, u32[]{:S(2)}, u32[]{:S(2)}) collective-permute-start(f32[8,256]{1,0:T(8,128)S(1)} %get-tuple-element.64), channel_id=1, source_target_pairs={{1,0},{2,1},{3,2},{4,3},{5,4},{6,5},{7,6},{8,7},{9,8},{10,9},{11,1... | collective-permute-start | bytes 24584 | tf_op jit(solution)/shard_map/ppermute | solution.py:449
  20.3 5.0 %copy-start.22 = (f32[8,128]{1,0:T(8,128)S(1)}, f32[8,128]{1,0:T(8,128)}, u32[]{:S(2)}) copy-start(f32[8,128]{1,0:T(8,128)} %w3.1) | copy-start | bytes 12292
  20.4 50.9 %collective-permute-start.4 = (f32[8,256]{1,0:T(8,128)S(1)}, f32[8,256]{1,0:T(8,128)S(1)}, u32[]{:S(2)}, u32[]{:S(2)}) collective-permute-start(f32[8,256]{1,0:T(8,128)S(1)} %get-tuple-element.65), channel_id=1, source_target_pairs={{0,1},{1,2},{2,3},{3,4},{4,5},{5,6},{6,7},{7,8},{8,9},{9,10},{10,1... | collective-permute-start | bytes 24584 | tf_op jit(solution)/shard_map/ppermute | solution.py:448
  25.3 1.2 copy-start.7
  26.5 1.2 copy-start.20
  28.6 42.7 %copy-start.1 = (f32[8,128,256]{2,1,0:T(8,128)S(1)}, f32[8,128,256]{2,1,0:T(8,128)}, u32[]{:S(2)}) copy-start(f32[8,128,256]{2,1,0:T(8,128)} %zonal.5) | copy-start | bytes 3145732
  28.6 42.7 %copy-start.3 = (f32[8,128,256]{2,1,0:T(8,128)S(1)}, f32[8,128,256]{2,1,0:T(8,128)}, u32[]{:S(2)}) copy-start(f32[8,128,256]{2,1,0:T(8,128)} %meridian.5) | copy-start | bytes 3145732
  71.2 2.8 %copy-start.9 = (f32[8,128,256]{2,1,0:T(8,128)}, f32[8,128,256]{2,1,0:T(8,128)S(1)}, u32[]{:S(2)}) copy-start(f32[8,128,256]{2,1,0:T(8,128)S(1)} %get-tuple-element.28.base) | copy-start | bytes 3145732
  123.7 1.2 copy-start.8
  133.3 1.5 %copy-start.19 = (f32[8,1]{1,0:T(8,128)S(1)}, f32[8,1]{1,0:T(8,128)}, u32[]{:S(2)}) copy-start(f32[8,1]{1,0:T(8,128)} %copy-done.18) | copy-start | bytes 100
  (9 other events, 7.4 us)

commit v2 on v1

--- a/solution.py
+++ b/solution.py
@@ -38,7 +38,6 @@
 
 F32 = jnp.float32
 BF16 = jnp.bfloat16
-VMEM_LIMIT = 48 * 1024 * 1024
 
 
 def iota(shape, axis):
@@ -46,8 +45,10 @@
 
 
 def turn(value, shift, axis):
-    shift %= value.shape[axis]
-    return pltpu.roll(value, shift, axis) if shift else value
+    if isinstance(shift, int):
+        shift %= value.shape[axis]
+        return pltpu.roll(value, shift, axis) if shift else value
+    return pltpu.roll(value, lax.rem(shift + value.shape[axis], value.shape[axis]), axis)
 
 
 def east(value):
@@ -74,7 +75,24 @@
     return lax.dot_general(left, right, (((1,), (1,)), ((), ())), preferred_element_type=F32)
 
 
-def pack_kernel(thermal, zonal, meridian, sea, depth, to_east, to_west, to_north, to_south):
+def pack_kernel(
+    thermal_far, zonal_far, meridian_far, sea_far, depth_far,
+    to_east, to_west, to_north, to_south,
+    thermal, zonal, meridian, sea, depth, arrived,
+):
+    fields = ((thermal_far, thermal), (zonal_far, zonal), (meridian_far, meridian), (sea_far, sea))
+    depth_copy = pltpu.make_async_copy(depth_far, depth, arrived.at[4 * LEVELS])
+    copies = []
+    for k in range(LEVELS):
+        copies.append(
+            [
+                pltpu.make_async_copy(far.at[k], near.at[k], arrived.at[4 * k + i])
+                for i, (far, near) in enumerate(fields)
+            ]
+        )
+        for copy in copies[k]:
+            copy.start()
+    depth_copy.start()
     lane = iota((ROWS, 128), 1)
     low = iota((8, COLS), 0) < 4
     high_edge = jnp.zeros((ROWS, 128), F32)
@@ -89,6 +107,8 @@
 
     edges = (high_edge, low_edge)
     for k in range(LEVELS):
+        for copy in copies[k]:
+            copy.wait()
         wet = sea[k].astype(F32)
         tracer = thermal[k] * wet
         u = zonal[k]
@@ -101,6 +121,7 @@
         to_north[LEVELS + k] = jnp.where(low, turn(wet[ROWS - 8 :], 4, 0), u[ROWS - 8 :])
         to_south[k] = jnp.where(low, tracer[:8], turn(v[:8], 4, 0))
         to_south[LEVELS + k] = jnp.where(low, u[:8], turn(wet[:8], 4, 0))
+    depth_copy.wait()
     floor = depth[...].astype(F32)
     edges = place(edges, floor, DEPTH_LANE, WIDE)
     to_north[2 * LEVELS] = floor[ROWS - 8 :]
@@ -118,7 +139,7 @@
 
 def edge_columns(west_tile, east_tile, lane_start, wide):
     ahead = turn(east_tile, -lane_start, 1)
-    behind = turn(west_tile, -wide - lane_start, 1)
+    behind = turn(west_tile, 128 - wide - lane_start, 1)
     return jnp.where(iota(ahead.shape, 1) < 64, ahead, behind)
 
 
@@ -126,8 +147,10 @@
     thermal, sea, depth, adjoint, south_edge, north_edge, west_edge, east_edge,
     w1, b1, w2, b2, w3, b3,
     base, sums,
-    tracer_ext, tracer_cols, w1_big, w2_t, w3_big, w3_t, b1_wide, b2_wide,
-    first, left, right, second, outer, slope1, slope2, grad, grad_outer, bias1, bias2, bias3,
+    tracer_ext, tracer_cols, w1_big, w2_pair, w2_pair_t, w3_big, w3_t, b1_wide, b2_wide,
+    first0, left0, second0, slope10, slope20, outer0,
+    first1, left1, second1, slope11, slope21, outer1,
+    grad, grad_outer, bias1, bias2, bias3,
 ):
     for k in range(LEVELS):
         tracer_ext[k, 0:8] = south_edge[k]
@@ -136,14 +159,14 @@
         tracer_cols[k] = edge_columns(
             west_edge[...], east_edge[...], TRACER_LANE + TRACER_WIDE * k, TRACER_WIDE
         )
-    inner_weight = w1[...].astype(BF16)
     hidden_weight = w2[...].astype(BF16)
     outer_weight = w3[...].astype(BF16)
     spread = (iota((FIN, 8 * FIN), 1) // 8 == iota((FIN, 8 * FIN), 0)).astype(BF16)
-    inner_wide = dot(inner_weight, spread)
-    inner_lane = iota((HID + FIN, 8 * FIN), 1)
-    inner_row = iota((HID + FIN, 8 * FIN), 0) - HID
-    stacked = jnp.concatenate([inner_wide, (inner_lane[HID:] // 8 == inner_row[HID:]).astype(F32)], 0)
+    inner_wide = lax.dot_general(
+        w1[...].astype(BF16), spread, (((0,), (0,)), ((), ())), preferred_element_type=F32
+    )
+    lane1 = iota((HID, 8 * FIN), 1)
+    feature_lane = iota((FIN, 8 * FIN), 1) - 8 * iota((FIN, 8 * FIN), 0)
     spread3 = (iota((LEVELS, 64), 1) // 8 == iota((LEVELS, 64), 0)).astype(BF16)
     outer_tall = lax.dot_general(
         spread3, outer_weight, (((0,), (0,)), ((), ())), preferred_element_type=F32
@@ -151,27 +174,35 @@
     outer_wide = lax.dot_general(
         outer_weight, spread3, (((0,), (0,)), ((), ())), preferred_element_type=F32
     )
-    pick_lane = iota((16, 64), 1)
-    pick = (pick_lane // 8 == iota((16, 64), 0)).astype(F32)
-    stacked3 = jnp.concatenate([outer_wide, pick], 0)
-    lane3 = iota((HID + 16, 64), 1)
+    lane3 = iota((HID, 64), 1)
     row3 = iota((64, HID), 0)
     for r in range(8):
-        w1_big[r] = jnp.where(inner_lane % 8 == r, stacked, 0.0).astype(BF16)
-        w3_t[r] = jnp.where(lane3 % 8 == r, stacked3, 0.0).astype(BF16)
+        w1_big[r * (HID + FIN) : r * (HID + FIN) + HID] = jnp.where(
+            lane1 % 8 == r, inner_wide, 0.0
+        ).astype(BF16)
+        w1_big[r * (HID + FIN) + HID : (r + 1) * (HID + FIN)] = (feature_lane == r).astype(BF16)
+        w3_t[r * HID : (r + 1) * HID] = jnp.where(lane3 % 8 == r, outer_wide, 0.0).astype(BF16)
         w3_big[:, r * HID : (r + 1) * HID] = jnp.where(row3 % 8 == r, outer_tall, 0.0).astype(BF16)
-    w2_t[...] = w2[...].T.astype(BF16)
-    b1_wide[...] = jnp.broadcast_to(b1[...], (HID, COLS))
-    b2_wide[...] = jnp.broadcast_to(b2[...], (HID, COLS))
+    blank = jnp.zeros((HID, HID), BF16)
+    flipped = w2[...].T.astype(BF16)
+    w2_pair[...] = jnp.concatenate(
+        [jnp.concatenate([hidden_weight, blank], 1), jnp.concatenate([blank, hidden_weight], 1)], 0
+    )
+    w2_pair_t[...] = jnp.concatenate(
+        [jnp.concatenate([flipped, blank], 1), jnp.concatenate([blank, flipped], 1)], 0
+    )
+    for bias, wide_bias in ((b1, b1_wide), (b2, b2_wide)):
+        tall_bias = jnp.broadcast_to(bias[...], (HID, HID)).T
+        wide_bias[...] = jnp.concatenate([tall_bias, tall_bias], 1)
     grad[...] = jnp.zeros_like(grad)
     grad_outer[...] = jnp.zeros_like(grad_outer)
     bias1[...] = jnp.zeros_like(bias1)
     bias2[...] = jnp.zeros_like(bias2)
     bias3[...] = jnp.zeros_like(bias3)
     level = iota((LEVELS, 8, COLS), 0).astype(F32)
-    b3_cube = b3[...]
-
-    def step(j, carry):
+    b3_cube = jnp.concatenate([jnp.full((1, 8, COLS), b3[k], F32) for k in range(LEVELS)], 0)
+
+    def forward(j, first, left, second, slope1, slope2, outer):
         start = pl.multiple_of(j * 8, 8)
         tall = tracer_ext[:, pl.ds(start, 24), :]
         tracer = tall[:, 8:16]
@@ -186,18 +217,27 @@
             .reshape(8 * FIN, COLS)
             .astype(BF16)
         )
-        for r in range(8):
-            z = dot(w1_big[r], features)
-            value = jnp.tanh(z[:HID] + b1_wide[...])
-            right[r, HID:] = value.astype(BF16)
-            slope1[r] = 1.0 - value * value
-            left[r, HID:] = z[HID:].astype(BF16)
-        for r in range(8):
-            value = jnp.tanh(dot(hidden_weight, right[r, HID:]) + b2_wide[...])
-            second[r] = value.astype(BF16)
-            slope2[r] = 1.0 - value * value
+        yield
+        for p in range(4):
+            z = dot(w1_big[p * 2 * (HID + FIN) : (p + 1) * 2 * (HID + FIN)], features)
+            for q in range(2):
+                r = 2 * p + q
+                z0 = q * (HID + FIN)
+                value = jnp.tanh(z[z0 : z0 + HID] + b1_wide[...])
+                first[r * HID : (r + 1) * HID] = value.astype(BF16)
+                slope1[r] = 1.0 - value * value
+                left[r, HID:] = z[z0 + HID : z0 + HID + FIN].astype(BF16)
+            yield
+        for p in range(4):
+            z = dot(w2_pair[...], first[p * 2 * HID : (p + 1) * 2 * HID])
+            for q in range(2):
+                r = 2 * p + q
+                value = jnp.tanh(z[q * HID : (q + 1) * HID] + b2_wide[...])
+                second[r * HID : (r + 1) * HID] = value.astype(BF16)
+                slope2[r] = 1.0 - value * value
+            yield
         squash = jax.nn.sigmoid(
-            dot(w3_big[...], second[...].reshape(8 * HID, COLS)).reshape(LEVELS, 8, COLS) + b3_cube
+            dot(w3_big[...], second[...]).reshape(LEVELS, 8, COLS) + b3_cube
         )
         kappa = KAPPA_FLOOR + KAPPA_SPAN * squash
         jump = tracer[1:] - tracer[:-1]
@@ -209,35 +249,66 @@
         down = 0.5 * (kappa[:-1] + kappa[1:]) * pair_jump
         mixing = jnp.concatenate([down, none], 0) - jnp.concatenate([none, down], 0)
         base[:, pl.ds(start, 8), :] = wet * (tracer + mixing)
-        outer_term = pull * KAPPA_SPAN * squash * (1.0 - squash)
+        outer[...] = pull * KAPPA_SPAN * squash * (1.0 - squash)
+
+    def backward(first, left, second, slope1, slope2, outer):
+        outer_term = outer[...]
         bias3[...] += outer_term
         outer_grad = outer_term.reshape(64, COLS).astype(BF16)
-        total = grad[...]
-        total_outer = grad_outer[...]
         total1 = bias1[...]
         total2 = bias2[...]
-        for r in range(8):
-            back = dot(w3_t[r], outer_grad)
-            hidden_term = back[:HID] * slope2[r]
-            total2 = total2 + hidden_term
-            hidden_grad = hidden_term.astype(BF16)
-            left[r, :HID] = hidden_grad
-            outer[r] = back[HID:].astype(BF16)
-            inner_term = dot(w2_t[...], hidden_grad) * slope1[r]
-            total1 = total1 + inner_term
-            right[r, :HID] = inner_term.astype(BF16)
-            total = total + dot_nt(left[r], right[r])
-            total_outer = total_outer + dot_nt(outer[r], second[r])
+        terms = []
+        for p in range(4):
+            back = dot(w3_t[p * 2 * HID : (p + 1) * 2 * HID], outer_grad)
+            for q in range(2):
+                r = 2 * p + q
+                hidden_term = back[q * HID : (q + 1) * HID] * slope2[r]
+                total2 = total2 + hidden_term
+                left[r, :HID] = hidden_term.astype(BF16)
+            yield
+        bias2[...] = total2
+        total = grad[...]
+        for p in range(4):
+            z = dot(w2_pair_t[...], jnp.concatenate([left[2 * p, :HID], left[2 * p + 1, :HID]], 0))
+            for q in range(2):
+                r = 2 * p + q
+                inner_term = z[q * HID : (q + 1) * HID] * slope1[r]
+                total1 = total1 + inner_term
+                right = jnp.concatenate(
+                    [inner_term.astype(BF16), first[r * HID : (r + 1) * HID]], 0
+                )
+                total = total + dot_nt(left[r], right)
+            yield
+        bias1[...] = total1
         grad[...] = total
-        grad_outer[...] = total_outer
-        bias1[...] = total1
-        bias2[...] = total2
+        grad_outer[...] += dot_nt(outer_grad, second[...])
+
+    def together(*parts):
+        parts = list(parts)
+        while parts:
+            for part in list(parts):
+                if next(part, parts) is parts:
+                    parts.remove(part)
+
+    even = (first0, left0, second0, slope10, slope20, outer0)
+    odd = (first1, left1, second1, slope11, slope21, outer1)
+    together(forward(0, *even))
+
+    def step(i, carry):
+        together(forward(2 * i + 1, *odd), backward(*even))
+        together(forward(jnp.minimum(2 * i + 2, BLOCKS - 1), *even), backward(*odd))
         return carry
 
-    lax.fori_loop(0, BLOCKS, step, 0)
+    lax.fori_loop(0, BLOCKS // 2, step, 0)
     sums[0:HID] = grad[0:HID, HID:]
     sums[ROW_INNER : ROW_INNER + FIN] = grad[HID:, :HID]
-    sums[ROW_OUTER : ROW_OUTER + LEVELS] = grad_outer[0:LEVELS]
+    row_outer = iota((64, HID), 0)
+    outer_sum = jnp.zeros((64, HID), F32)
+    for r in range(8):
+        outer_sum = outer_sum + jnp.where(
+            row_outer % 8 == r, grad_outer[:, r * HID : (r + 1) * HID], 0.0
+        )
+    sums[ROW_OUTER : ROW_OUTER + LEVELS] = jnp.sum(outer_sum.reshape(LEVELS, 8, HID), axis=1)
     outer_bias = jnp.sum(bias3[...], axis=1)
     sums[ROW_OUTER_BIAS : ROW_OUTER_BIAS + LEVELS] = outer_bias[:, :128] + outer_bias[:, 128:]
     inner_row_sum = jnp.sum((bias1[:, :128] + bias1[:, 128:]).T, axis=0, keepdims=True)
@@ -256,6 +327,7 @@
     zonal, meridian, sea, depth, south_edge, north_edge, west_edge, east_edge,
     south_corner, north_corner, sums,
     basis, summed,
+    east_transport, north_transport,
 ):
     west_tile = jnp.concatenate([south_corner[:, :128], west_edge[...], north_corner[:, :128]], 0)
     east_tile = jnp.concatenate([south_corner[:, 128:], east_edge[...], north_corner[:, 128:]], 0)
@@ -265,18 +337,24 @@
             inside, south_edge[index], north_edge[index], second, west_tile, east_tile, lane_start, WIDE
         )
 
-    east_transport = jnp.zeros((EXT_ROWS, EXT_COLS), F32)
-    north_transport = jnp.zeros((EXT_ROWS, EXT_COLS), F32)
-    for k in range(LEVELS):
+    def gather(k, carry):
         wet = extended(sea[k].astype(F32), LEVELS + k, True, WET_LANE + WIDE * k)
-        east_transport = east_transport + wet * east(wet) * extended(
+        east_part = wet * east(wet) * extended(
             zonal[k], LEVELS + k, False, ZONAL_LANE + WIDE * k
         )
-        north_transport = north_transport + wet * north(wet) * extended(
+        north_part = wet * north(wet) * extended(
             meridian[k], k, True, MERIDIAN_LANE + WIDE * k
         )
+        east_transport[...] += east_part
+        north_transport[...] += north_part
+        return carry
+
+    east_transport[...] = jnp.zeros_like(east_transport)
+    north_transport[...] = jnp.zeros_like(north_transport)
+    lax.fori_loop(0, LEVELS, gather, 0)
     source = -(
-        (east_transport - west(east_transport)) + (north_transport - south(north_transport))
+        (east_transport[...] - west(east_transport[...]))
+        + (north_transport[...] - south(north_transport[...]))
     )
     floor = extended(depth[...].astype(F32), 2 * LEVELS, False, DEPTH_LANE)
     east_depth = jnp.minimum(floor, east(floor))
@@ -350,17 +428,18 @@
 def final_kernel(
     scale, thermal, zonal, meridian, sea, base, south_edge, north_edge, west_edge, east_edge, basis, totals,
     revised, height_out, grad1, bias1, grad2, bias2, grad3, bias3,
+    falls,
 ):
     gram = jnp.sum(totals[ROW_GRAM : ROW_GRAM + 16], axis=1, keepdims=True)
     y0, y1, y2 = galerkin(*[gram[i : i + 1] for i in range(9)])
     height = y0 * basis[0] + y1 * basis[1] + y2 * basis[2]
     height_out[...] = height[8 : ROWS + 8, :COLS]
-    east_fall = east(height) - height
-    north_fall = north(height) - height
     blank = jnp.zeros((8, 128), F32)
     west_tile = jnp.concatenate([blank, west_edge[...], blank], 0)
     east_tile = jnp.concatenate([blank, east_edge[...], blank], 0)
-    for k in range(LEVELS):
+    falls[0] = east(height) - height
+    falls[1] = north(height) - height
+    def advect(k, carry):
         inside_wet = sea[k].astype(F32)
         wet = field_extended(
             inside_wet, south_edge[LEVELS + k], north_edge[LEVELS + k], True,
@@ -378,52 +457,73 @@
         mid = tracer[8 : ROWS + 8]
         pair = mid + east(mid)
         face = (8.0 * pair - (west(pair) + east(pair))) * (1.0 / 12.0)
-        flux = mid_wet * east(mid_wet) * (u - east_fall[8 : ROWS + 8]) * face
+        flux = mid_wet * east(mid_wet) * (u - falls[0, 8 : ROWS + 8]) * face
         spread = (flux - west(flux))[:, :COLS]
         mid_wet = wet[:, :COLS]
         mid = tracer[:, :COLS]
         pair = mid + north(mid)
         face = (8.0 * pair - (south(pair) + north(pair))) * (1.0 / 12.0)
-        flux = mid_wet * north(mid_wet) * (v - north_fall[:, :COLS]) * face
+        flux = mid_wet * north(mid_wet) * (v - falls[1, :, :COLS]) * face
         spread = spread + (flux - south(flux))[8 : ROWS + 8]
         revised[k] = base[k] - TRANSPORT_TICK * (inside_wet * spread)
+        return carry
+
+    lax.fori_loop(0, LEVELS, advect, 0)
     grad2[...] = totals[0:HID] * scale
-    grad1[...] = (totals[ROW_INNER : ROW_INNER + FIN] * scale).T
+    grad1[...] = totals[ROW_INNER : ROW_INNER + FIN] * scale
     grad3[...] = totals[ROW_OUTER : ROW_OUTER + LEVELS] * scale
     bias1[...] = totals[ROW_BIAS : ROW_BIAS + 1] * scale
     bias2[...] = totals[ROW_BIAS + 1 : ROW_BIAS + 2] * scale
-    bias3[...] = jnp.sum(totals[ROW_OUTER_BIAS : ROW_OUTER_BIAS + LEVELS], axis=1, keepdims=True) * scale
+    outer_bias = jnp.sum(totals[ROW_OUTER_BIAS : ROW_OUTER_BIAS + LEVELS], axis=1, keepdims=True)
+    diagonal = iota((LEVELS, LEVELS), 0) == iota((LEVELS, LEVELS), 1)
+    bias3[...] = jnp.sum(jnp.where(diagonal, outer_bias * scale, 0.0), axis=0, keepdims=True)
 
 
 def struct(*shape, dtype=F32):
     return jax.ShapeDtypeStruct(shape, dtype)
 
 
-def call(kernel, out_shape, scratch=(), flops=0, transcendentals=0, nbytes=0):
+def call(kernel, out_shape, scratch=(), in_specs=None, mib=16, flops=0, transcendentals=0, nbytes=0):
+    specs = {} if in_specs is None else {"in_specs": in_specs}
     return pl.pallas_call(
         kernel,
         out_shape=out_shape,
         scratch_shapes=list(scratch),
-        compiler_params=pltpu.CompilerParams(vmem_limit_bytes=VMEM_LIMIT),
+        compiler_params=pltpu.CompilerParams(vmem_limit_bytes=mib * 1024 * 1024),
         cost_estimate=pl.CostEstimate(
             flops=flops, transcendentals=transcendentals, bytes_accessed=nbytes
         ),
-    )
-
-
-def share(value, axis):
-    count = lax.axis_size(axis)
-    copies = jnp.broadcast_to(value[None], (count,) + value.shape)
-    return jnp.sum(lax.all_to_all(copies, axis, 0, 0), axis=0)
+        **specs,
+    )
+
+
+def near(count):
+    return [pl.BlockSpec(memory_space=pltpu.VMEM)] * count
+
+
+def far(count):
+    return [pl.BlockSpec(memory_space=pltpu.HBM)] * count
+
+
+def sum_kernel(parts, copies):
+    total = parts[0]
+    for i in range(1, parts.shape[0]):
+        total = total + parts[i]
+    for i in range(copies.shape[0]):
+        copies[i] = total
+
+
+def summed_copies(parts, count):
+    return call(sum_kernel, struct(count, *parts.shape[1:]), mib=4, nbytes=300_000)(parts)
 
 
 def total_over_devices(value):
-    count = lax.axis_size("lon")
-    parts = value.reshape(count, value.shape[0] // count, value.shape[1])
-    part = jnp.sum(lax.all_to_all(parts, "lon", 0, 0), axis=0)
-    part = share(part, "lat")
-    copies = jnp.broadcast_to(part[None], (count,) + part.shape)
-    return lax.all_to_all(copies, "lon", 0, 0).reshape(value.shape)
+    lons, lats = lax.axis_size("lon"), lax.axis_size("lat")
+    parts = value.reshape(lons, value.shape[0] // lons, value.shape[1])
+    parts = lax.all_to_all(parts, "lon", 0, 0)
+    parts = lax.all_to_all(summed_copies(parts, lats), "lat", 0, 0)
+    parts = lax.all_to_all(summed_copies(parts, lons), "lon", 0, 0)
+    return parts.reshape(value.shape)
 
 
 def local(thermal, zonal, meridian, sea, depth, adjoint, w1, b1, w2, b2, w3, b3):
@@ -437,6 +537,16 @@
     to_east, to_west, to_north, to_south = call(
         pack_kernel,
         (struct(ROWS, 128), struct(ROWS, 128), struct(17, 8, COLS), struct(17, 8, COLS)),
+        scratch=[
+            pltpu.VMEM((LEVELS, ROWS, COLS), F32),
+            pltpu.VMEM((LEVELS, ROWS, COLS), F32),
+            pltpu.VMEM((LEVELS, ROWS, COLS), F32),
+            pltpu.VMEM((LEVELS, ROWS, COLS), jnp.int32),
+            pltpu.VMEM((ROWS, COLS), jnp.int32),
+            pltpu.SemaphoreType.DMA((4 * LEVELS + 1,)),
+        ],
+        in_specs=far(5),
+        mib=58,
         flops=4_000_000,
         nbytes=5_000_000,
     )(thermal, zonal, meridian, sea, depth)
@@ -454,35 +564,43 @@
         scratch=[
             pltpu.VMEM((LEVELS, EXT_ROWS, COLS), F32),
             pltpu.VMEM((LEVELS, ROWS, 128), F32),
-            pltpu.VMEM((8, HID + FIN, 8 * FIN), BF16),
-            pltpu.VMEM((HID, HID), BF16),
+            pltpu.VMEM((8 * (HID + FIN), 8 * FIN), BF16),
+            pltpu.VMEM((2 * HID, 2 * HID), BF16),
+            pltpu.VMEM((2 * HID, 2 * HID), BF16),
             pltpu.VMEM((64, 8 * HID), BF16),
-            pltpu.VMEM((8, HID + 16, 64), BF16),
+            pltpu.VMEM((8 * HID, 64), BF16),
             pltpu.VMEM((HID, COLS), F32),
             pltpu.VMEM((HID, COLS), F32),
-            pltpu.VMEM((8, HID, COLS), BF16),
+        ]
+        + 2
+        * [
+            pltpu.VMEM((8 * HID, COLS), BF16),
             pltpu.VMEM((8, HID + FIN, COLS), BF16),
-            pltpu.VMEM((8, 2 * HID, COLS), BF16),
-            pltpu.VMEM((8, HID, COLS), BF16),
-            pltpu.VMEM((8, 16, COLS), BF16),
+            pltpu.VMEM((8 * HID, COLS), BF16),
             pltpu.VMEM((8, HID, COLS), F32),
             pltpu.VMEM((8, HID, COLS), F32),
+            pltpu.VMEM((LEVELS, 8, COLS), F32),
+        ]
+        + [
             pltpu.VMEM((HID + FIN, COLS), F32),
-            pltpu.VMEM((16, HID), F32),
+            pltpu.VMEM((64, 8 * HID), F32),
             pltpu.VMEM((HID, COLS), F32),
             pltpu.VMEM((HID, COLS), F32),
             pltpu.VMEM((LEVELS, 8, COLS), F32),
         ],
+        in_specs=near(13) + [pl.BlockSpec(memory_space=pltpu.SMEM)],
+        mib=24,
         flops=8_000_000_000,
         transcendentals=9_000_000,
         nbytes=5_000_000,
     )(
         thermal, sea, depth, adjoint, south_edge, north_edge, west_edge, east_edge,
-        w1, b1[:, None], w2, b2[:, None], w3, jnp.broadcast_to(b3[:, None, None], (LEVELS, 8, COLS)),
+        w1.T, b1[None], w2, b2[None], w3, b3,
     )
     basis, summed = call(
         gram_kernel,
         (struct(3, EXT_ROWS, EXT_COLS), struct(SUM_ROWS, 128)),
+        scratch=[pltpu.VMEM((EXT_ROWS, EXT_COLS), F32)] * 2,
         flops=20_000_000,
         nbytes=5_000_000,
     )(
@@ -496,13 +614,14 @@
         (
             struct(LEVELS, ROWS, COLS),
             struct(ROWS, COLS),
-            struct(HID, FIN),
+            struct(FIN, HID),
             struct(1, HID),
             struct(HID, HID),
             struct(1, HID),
             struct(LEVELS, HID),
-            struct(LEVELS, 1),
+            struct(1, LEVELS),
         ),
+        scratch=[pltpu.VMEM((2, EXT_ROWS, EXT_COLS), F32)],
         flops=20_000_000,
         nbytes=8_000_000,
     )(
@@ -512,7 +631,7 @@
     return (
         revised,
         height,
-        grad1,
+        grad1.T,
         bias1.reshape(HID),
         grad2,
         bias2.reshape(HID),

time: 136 us -> 95.7 us (0.70)
  local copies, waits for them, and re-layouts: 20 us -> 0.66 us
  Pallas kernels: 52.6 us -> 36 us
  other arithmetic: 3.67 us -> 0 us
    pallas_call x1, Pallas kernels: 42.6 us -> 23.1 us  [local(): call(closure_kernel, (struct(LEVELS, ROWS, COLS), struct(ROW_GRAM, 128)),...]
    unnamed x57 -> x25, local copies, waits for them, and re-layouts: 17.1 us -> 0.65 us
    reduce_sum x2 -> x0, other arithmetic: 3.04 us -> none  [the longest x1 1.52 us: total_over_devices(): part = jnp.sum(lax.all_to_all(parts, 'lon', 0, 0), axis=0)]
    broadcast_in_dim x5 -> x0, local copies, waits for them, and re-layouts: 2.96 us -> none  [the longest x1 0.74 us: local(): b1[:, None]]
    pallas_call x1, Pallas kernels: 1.22 us -> 3.98 us  [local(): call(pack_kernel, (struct(ROWS, 128), struct(ROWS, 128), struct(17, 8, CO...]
  transfers between devices with their start and end apart: 6 -> 6, of which waited for: 0 -> 0; matrix products, arithmetic and copies ran while one was open for 2% -> 0% of each run, Pallas kernels for 31% -> 24%
where the time goes in v2:
time: 95.7 us; the launch traced here: 95.4 us
  blocking collectives  44 us (46%)
  Pallas kernels  36 us (38%)
  starting transfers between devices  13.8 us (14%)
    pallas_call x1, Pallas kernels, local(): call(closure_kernel, (struct(LEVELS, ROWS, COLS), struct(ROW_GRAM, 128)),...  23.1 us
    all_to_all x1, blocking collectives, total_over_devices(): parts = lax.all_to_all(summed_copies(parts, lats), 'lat', 0, 0)  20.8 us
    all_to_all x1, blocking collectives, total_over_devices(): parts = lax.all_to_all(parts, 'lon', 0, 0)  12.5 us
    all_to_all x1, blocking collectives, total_over_devices(): parts = lax.all_to_all(summed_copies(parts, lons), 'lon', 0, 0)  10.6 us
    pallas_call x1, Pallas kernels, local(): call(functools.partial(final_kernel, scale), (struct(LEVELS, ROWS, COLS),...  5.81 us
    ppermute x1, starting transfers between devices, local(): south_corner = lax.ppermute(edges[ROWS - 8:], 'lat', line)  4.79 us
    pallas_call x1, Pallas kernels, local(): call(pack_kernel, (struct(ROWS, 128), struct(ROWS, 128), struct(17, 8, CO...  3.98 us
    pallas_call x1, Pallas kernels, local(): call(gram_kernel, (struct(3, EXT_ROWS, EXT_COLS), struct(SUM_ROWS, 128)),...  3.1 us
  transfers between devices with their start and end apart: 6, of which 0 were waited for; matrix products, arithmetic and copies ran while one was open for 0% of the time, Pallas kernels for 24%

profile of v2, /device:TPU:1, one launch (start us, length us, event | category | flops | bytes accessed | tf_op | source)
XLA Modules:
  0.0 95.4 jit_solution(3105393676581820349)
XLA Ops:
  0.7 4.0 %shard_map.179 = (f32[128,128]{1,0:T(8,128)}, f32[128,128]{1,0:T(8,128)}, f32[17,8,256]{2,1,0:T(8,128)}, f32[17,8,256]{2,1,0:T(8,128)}) custom-call(f32[8,128,256]{2,1,0:T(8,128)} %thermal.3, f32[8,128,256]{2,1,0:T(8,128)} %zonal.3, f32[8,128,256]{2,1,0:T(8,128)} %meridian.3, s32[8,128,256]{2,1,0:T(8,128)} %sea.5, s32[128,256]{1,0:T(8,128)} %depth.3), custom_call_target="tpu_custom_call" | custom-call | flops 4000000 | bytes 5000000 | tf_op jit(solution)/shard_map/pallas_call | solution.py:537
  4.6 2.8 %collective-permute-start.2 = (f32[128,128]{1,0:T(8,128)}, f32[128,128]{1,0:T(8,128)S(1)}, u32[]{:S(2)}, u32[]{:S(2)}) collective-permute-start(f32[128,128]{1,0:T(8,128)} %get-tuple-element.26), channel_id=1, source_target_pairs={{0,16},{16,32},{32,48},{48,64},{64,80},{80,96},{96,112},{112,128},... | collective-permute-start | bytes 196616 | tf_op jit(solution)/shard_map/ppermute | solution.py:553
  7.4 0.6 collective-permute-start.3
  8.1 2.9 %collective-permute-start = (f32[17,8,256]{2,1,0:T(8,128)}, f32[17,8,256]{2,1,0:T(8,128)S(1)}, u32[]{:S(2)}, u32[]{:S(2)}) collective-permute-start(f32[17,8,256]{2,1,0:T(8,128)} %get-tuple-element.24), channel_id=1, source_target_pairs={{0,1},{1,2},{2,3},{3,4},{4,5},{5,6},{6,7},{7,8},{8,9},{9,10},{10,1... | collective-permute-start | bytes 417800 | tf_op jit(solution)/shard_map/ppermute | solution.py:555
  11.0 0.0 copy-start.4
  11.0 1.4 %collective-permute-start.1 = (f32[17,8,256]{2,1,0:T(8,128)}, f32[17,8,256]{2,1,0:T(8,128)S(1)}, u32[]{:S(2)}, u32[]{:S(2)}) collective-permute-start(f32[17,8,256]{2,1,0:T(8,128)} %get-tuple-element.25), channel_id=1, source_target_pairs={{1,0},{2,1},{3,2},{4,3},{5,4},{6,5},{7,6},{8,7},{9,8},{10,9},{11,1... | collective-permute-start | bytes 417800 | tf_op jit(solution)/shard_map/ppermute | solution.py:556
  12.4 0.0 copy-start.6
  12.5 0.0 copy-start.7
  12.5 0.0 copy-start.8
  12.5 1.3 %collective-permute-start.5 = (f32[8,256]{1,0:T(8,128)S(1)}, f32[8,256]{1,0:T(8,128)S(1)}, u32[]{:S(2)}, u32[]{:S(2)}) collective-permute-start(f32[8,256]{1,0:T(8,128)S(1)} %get-tuple-element.40), channel_id=1, source_target_pairs={{1,0},{2,1},{3,2},{4,3},{5,4},{6,5},{7,6},{8,7},{9,8},{10,9},{11,1... | collective-permute-start | bytes 24584 | tf_op jit(solution)/shard_map/ppermute | solution.py:559
  13.8 4.8 %collective-permute-start.4 = (f32[8,256]{1,0:T(8,128)S(1)}, f32[8,256]{1,0:T(8,128)S(1)}, u32[]{:S(2)}, u32[]{:S(2)}) collective-permute-start(f32[8,256]{1,0:T(8,128)S(1)} %get-tuple-element.41), channel_id=1, source_target_pairs={{0,1},{1,2},{2,3},{3,4},{4,5},{5,6},{6,7},{7,8},{8,9},{9,10},{10,1... | collective-permute-start | bytes 24584 | tf_op jit(solution)/shard_map/ppermute | solution.py:558
  18.6 0.0 collective-permute-done.south_edge
  18.6 0.0 copy-start.9
  18.6 0.0 copy-start.10
  18.7 0.0 copy-start.11
  18.7 0.6 copy-done.9
  19.3 0.0 copy-done.10
  19.3 0.0 copy-done.11
  19.3 23.1 %shard_map.180 = (f32[8,128,256]{2,1,0:T(8,128)S(1)}, f32[184,128]{1,0:T(8,128)S(1)}) custom-call(f32[8,128,256]{2,1,0:T(8,128)S(1)} %copy-done.3, s32[8,128,256]{2,1,0:T(8,128)S(1)} %copy-done.2, s32[128,256]{1,0:T(8,128)S(1)} %copy-done.4, f32[8,128,256]{2,1,0:T(8,128)S(1)} %copy-done.5, f32[17,8,256]{2,1,0:T(8,128)S(1)} %collective-permute-done.south_edge, ...), custom_call_target="tpu_custom_call" | custom-call | flops 8000000000 | bytes 5000000 | tf_op jit(solution)/shard_map/pallas_call | solution.py:561
  42.4 3.1 %shard_map.181 = (f32[3,144,384]{2,1,0:T(8,128)S(1)}, f32[256,128]{1,0:T(8,128)S(1)}) custom-call(f32[8,128,256]{2,1,0:T(8,128)S(1)} %copy-done, f32[8,128,256]{2,1,0:T(8,128)S(1)} %copy-done.1, s32[8,128,256]{2,1,0:T(8,128)S(1)} %copy-done.2, s32[128,256]{1,0:T(8,128)S(1)} %copy-done.4, f32[17,8,256]{2,1,0:T(8,128)S(1)} %collective-permute-done.south_edge, ...), custom_call_target="tpu_custom_call" | custom-call | flops 20000000 | bytes 5000000 | tf_op jit(solution)/shard_map/pallas_call | solution.py:600
  45.5 12.5 %all_to_all.15.parts = f32[16,16,128]{2,1,0:T(8,128)S(1)} all-to-all(f32[16,16,128]{2,1,0:T(8,128)S(1)} %bitcast.10), channel_id=1, replica_groups=mesh['lon'=16,'lat'=16] {'lon'}, dimensions={0} | all-to-all | bytes 262144 | tf_op jit(solution)/shard_map/all_to_all | solution.py:523
  58.1 20.8 %all_to_all.16.parts = f32[16,16,128]{2,1,0:T(8,128)S(1)} all-to-all(f32[16,16,128]{2,1,0:T(8,128)S(1)} %shard_map.182), channel_id=1, replica_groups=mesh['lon'=16,'lat'=16] {'lat'}, dimensions={0} | all-to-all | bytes 262144 | tf_op jit(solution)/shard_map/all_to_all | solution.py:524
  78.9 10.6 %all_to_all.17 = f32[16,16,128]{2,1,0:T(8,128)S(1)} all-to-all(f32[16,16,128]{2,1,0:T(8,128)S(1)} %shard_map.183), channel_id=1, replica_groups=mesh['lon'=16,'lat'=16] {'lon'}, dimensions={0} | all-to-all | bytes 262144 | tf_op jit(solution)/shard_map/all_to_all | solution.py:525
  89.6 5.8 %shard_map.184 = (f32[8,128,256]{2,1,0:T(8,128)}, f32[128,256]{1,0:T(8,128)}, f32[32,128]{1,0:T(8,128)}, f32[1,128]{1,0:T(1,128)}, f32[128,128]{1,0:T(8,128)}, /...) custom-call(f32[8,128,256]{2,1,0:T(8,128)S(1)} %copy-done.3, f32[8,128,256]{2,1,0:T(8,128)S(1)} %copy-done, ...), custom_call_target="tpu_custom_call" | custom-call | flops 20000000 | bytes 8000000 | tf_op jit(solution)/shard_map/pallas_call | solution.py:612
  (24 shorter events, 0.1 us)
Async XLA Ops:
  0.6 18.0 %copy-start.2 = (s32[8,128,256]{2,1,0:T(8,128)S(1)}, s32[8,128,256]{2,1,0:T(8,128)}, u32[]{:S(2)}) copy-start(s32[8,128,256]{2,1,0:T(8,128)} %sea.5) | copy-start | bytes 3145732
  0.6 18.0 %copy-start.3 = (f32[8,128,256]{2,1,0:T(8,128)S(1)}, f32[8,128,256]{2,1,0:T(8,128)}, u32[]{:S(2)}) copy-start(f32[8,128,256]{2,1,0:T(8,128)} %thermal.3) | copy-start | bytes 3145732
  0.7 18.0 %copy-start.5 = (f32[8,128,256]{2,1,0:T(8,128)S(1)}, f32[8,128,256]{2,1,0:T(8,128)}, u32[]{:S(2)}) copy-start(f32[8,128,256]{2,1,0:T(8,128)} %adjoint.1) | copy-start | bytes 3145732
  4.6 7.8 %collective-permute-start.2 = (f32[128,128]{1,0:T(8,128)}, f32[128,128]{1,0:T(8,128)S(1)}, u32[]{:S(2)}, u32[]{:S(2)}) collective-permute-start(f32[128,128]{1,0:T(8,128)} %get-tuple-element.26), channel_id=1, source_target_pairs={{0,16},{16,32},{32,48},{48,64},{64,80},{80,96},{96,112},{112,128},... | collective-permute-start | bytes 196616 | tf_op jit(solution)/shard_map/ppermute | solution.py:553
  7.4 5.0 %collective-permute-start.3 = (f32[128,128]{1,0:T(8,128)}, f32[128,128]{1,0:T(8,128)S(1)}, u32[]{:S(2)}, u32[]{:S(2)}) collective-permute-start(f32[128,128]{1,0:T(8,128)} %get-tuple-element.27), channel_id=1, source_target_pairs={{16,0},{32,16},{48,32},{64,48},{80,64},{96,80},{112,96},{128,112},... | collective-permute-start | bytes 196616 | tf_op jit(solution)/shard_map/ppermute | solution.py:554
  8.1 10.6 %collective-permute-start = (f32[17,8,256]{2,1,0:T(8,128)}, f32[17,8,256]{2,1,0:T(8,128)S(1)}, u32[]{:S(2)}, u32[]{:S(2)}) collective-permute-start(f32[17,8,256]{2,1,0:T(8,128)} %get-tuple-element.24), channel_id=1, source_target_pairs={{0,1},{1,2},{2,3},{3,4},{4,5},{5,6},{6,7},{7,8},{8,9},{9,10},{10,1... | collective-permute-start | bytes 417800 | tf_op jit(solution)/shard_map/ppermute | solution.py:555
  11.0 7.7 %copy-start.4 = (s32[128,256]{1,0:T(8,128)S(1)}, s32[128,256]{1,0:T(8,128)}, u32[]{:S(2)}) copy-start(s32[128,256]{1,0:T(8,128)} %depth.3) | copy-start | bytes 393220
  11.0 7.6 %collective-permute-start.1 = (f32[17,8,256]{2,1,0:T(8,128)}, f32[17,8,256]{2,1,0:T(8,128)S(1)}, u32[]{:S(2)}, u32[]{:S(2)}) collective-permute-start(f32[17,8,256]{2,1,0:T(8,128)} %get-tuple-element.25), channel_id=1, source_target_pairs={{1,0},{2,1},{3,2},{4,3},{5,4},{6,5},{7,6},{8,7},{9,8},{10,9},{11,1... | collective-permute-start | bytes 417800 | tf_op jit(solution)/shard_map/ppermute | solution.py:556
  12.4 6.3 %copy-start.6 = (f32[128,128]{1,0:T(8,128)S(1)}, f32[128,128]{1,0:T(8,128)}, u32[]{:S(2)}) copy-start(f32[128,128]{1,0:T(8,128)} %w2.1) | copy-start | bytes 196612
  12.5 6.2 %copy-start.7 = (f32[128,32]{0,1:T(8,128)S(1)}, f32[128,32]{0,1:T(8,128)}, u32[]{:S(2)}) copy-start(f32[128,32]{0,1:T(8,128)} %param.18) | copy-start | bytes 49156
  12.5 6.2 %copy-start.8 = (f32[8,128]{1,0:T(8,128)S(1)}, f32[8,128]{1,0:T(8,128)}, u32[]{:S(2)}) copy-start(f32[8,128]{1,0:T(8,128)} %w3.1) | copy-start | bytes 12292
  12.5 29.9 %collective-permute-start.5 = (f32[8,256]{1,0:T(8,128)S(1)}, f32[8,256]{1,0:T(8,128)S(1)}, u32[]{:S(2)}, u32[]{:S(2)}) collective-permute-start(f32[8,256]{1,0:T(8,128)S(1)} %get-tuple-element.40), channel_id=1, source_target_pairs={{1,0},{2,1},{3,2},{4,3},{5,4},{6,5},{7,6},{8,7},{9,8},{10,9},{11,1... | collective-permute-start | bytes 24584 | tf_op jit(solution)/shard_map/ppermute | solution.py:559
  13.8 28.6 %collective-permute-start.4 = (f32[8,256]{1,0:T(8,128)S(1)}, f32[8,256]{1,0:T(8,128)S(1)}, u32[]{:S(2)}, u32[]{:S(2)}) collective-permute-start(f32[8,256]{1,0:T(8,128)S(1)} %get-tuple-element.41), channel_id=1, source_target_pairs={{0,1},{1,2},{2,3},{3,4},{4,5},{5,6},{6,7},{7,8},{8,9},{9,10},{10,1... | collective-permute-start | bytes 24584 | tf_op jit(solution)/shard_map/ppermute | solution.py:558
  18.6 0.7 copy-start.9
  18.6 0.7 copy-start.10
  18.7 0.7 copy-start.11
  19.3 23.1 %copy-start = (f32[8,128,256]{2,1,0:T(8,128)S(1)}, f32[8,128,256]{2,1,0:T(8,128)}, u32[]{:S(2)}) copy-start(f32[8,128,256]{2,1,0:T(8,128)} %zonal.3) | copy-start | bytes 3145732
  19.3 23.1 %copy-start.1 = (f32[8,128,256]{2,1,0:T(8,128)S(1)}, f32[8,128,256]{2,1,0:T(8,128)}, u32[]{:S(2)}) copy-start(f32[8,128,256]{2,1,0:T(8,128)} %meridian.3) | copy-start | bytes 3145732

commit v3 on v2

--- a/solution.py
+++ b/solution.py
@@ -33,8 +33,7 @@
 ROW_OUTER = 160
 ROW_OUTER_BIAS = 168
 ROW_BIAS = 176
-ROW_GRAM = 184
-SUM_ROWS = 256
+SUM_ROWS = 192
 
 F32 = jnp.float32
 BF16 = jnp.bfloat16
@@ -75,59 +74,78 @@
     return lax.dot_general(left, right, (((1,), (1,)), ((), ())), preferred_element_type=F32)
 
 
-def pack_kernel(
+def pack_rows_kernel(
     thermal_far, zonal_far, meridian_far, sea_far, depth_far,
-    to_east, to_west, to_north, to_south,
-    thermal, zonal, meridian, sea, depth, arrived,
+    to_north, to_south,
+    floats, seas, floors, arrived,
 ):
-    fields = ((thermal_far, thermal), (zonal_far, zonal), (meridian_far, meridian), (sea_far, sea))
-    depth_copy = pltpu.make_async_copy(depth_far, depth, arrived.at[4 * LEVELS])
     copies = []
+    for side, start in enumerate((ROWS - 8, 0)):
+        rows = pl.ds(start, 8)
+        pairs = [
+            (thermal_far.at[:, rows], floats.at[3 * side]),
+            (zonal_far.at[:, rows], floats.at[3 * side + 1]),
+            (meridian_far.at[:, rows], floats.at[3 * side + 2]),
+            (sea_far.at[:, rows], seas.at[side]),
+            (depth_far.at[rows], floors.at[side]),
+        ]
+        copies += [
+            pltpu.make_async_copy(source, target, arrived.at[5 * side + i])
+            for i, (source, target) in enumerate(pairs)
+        ]
+    for copy in copies:
+        copy.start()
+    for copy in copies:
+        copy.wait()
+    low = iota((8, COLS), 0) < 4
     for k in range(LEVELS):
-        copies.append(
-            [
-                pltpu.make_async_copy(far.at[k], near.at[k], arrived.at[4 * k + i])
-                for i, (far, near) in enumerate(fields)
-            ]
-        )
-        for copy in copies[k]:
-            copy.start()
-    depth_copy.start()
-    lane = iota((ROWS, 128), 1)
-    low = iota((8, COLS), 0) < 4
-    high_edge = jnp.zeros((ROWS, 128), F32)
-    low_edge = jnp.zeros((ROWS, 128), F32)
-
-    def place(edges, field, lane_start, wide):
-        high, low_ = edges
-        mask = jnp.logical_and(lane >= lane_start, lane < lane_start + wide)
-        high = jnp.where(mask, turn(field[:, 128:], lane_start + wide, 1), high)
-        low_ = jnp.where(mask, turn(field[:, :128], lane_start, 1), low_)
-        return high, low_
-
-    edges = (high_edge, low_edge)
+        wet = seas[0, k].astype(F32)
+        to_north[k] = jnp.where(low, turn(floats[2, k], 4, 0), floats[0, k] * wet)
+        to_north[LEVELS + k] = jnp.where(low, turn(wet, 4, 0), floats[1, k])
+        wet = seas[1, k].astype(F32)
+        to_south[k] = jnp.where(low, floats[3, k] * wet, turn(floats[5, k], 4, 0))
+        to_south[LEVELS + k] = jnp.where(low, floats[4, k], turn(wet, 4, 0))
+    to_north[2 * LEVELS] = floors[0].astype(F32)
+    to_south[2 * LEVELS] = floors[1].astype(F32)
+
+
+def place(edges, field, lane_start, wide):
+    lane = iota((field.shape[0], 128), 1)
+    mask = jnp.logical_and(lane >= lane_start, lane < lane_start + wide)
+    high = jnp.where(mask, turn(field[:, 128:], lane_start + wide, 1), edges[0])
+    low = jnp.where(mask, turn(field[:, :128], lane_start, 1), edges[1])
+    return high, low
+
+
+def place_level(edges, k, tracer, u, v, wet):
+    edges = place(edges, tracer, TRACER_LANE + TRACER_WIDE * k, TRACER_WIDE)
+    edges = place(edges, u, ZONAL_LANE + WIDE * k, WIDE)
+    edges = place(edges, v, MERIDIAN_LANE + WIDE * k, WIDE)
+    return place(edges, wet, WET_LANE + WIDE * k, WIDE)
+
+
+def pack_columns_kernel(thermal, zonal, meridian, sea, depth, high, low):
+    edges = (jnp.zeros((ROWS, 128), F32), jnp.zeros((ROWS, 128), F32))
     for k in range(LEVELS):
-        for copy in copies[k]:
-            copy.wait()
         wet = sea[k].astype(F32)
-        tracer = thermal[k] * wet
-        u = zonal[k]
-        v = meridian[k]
-        edges = place(edges, tracer, TRACER_LANE + TRACER_WIDE * k, TRACER_WIDE)
-        edges = place(edges, u, ZONAL_LANE + WIDE * k, WIDE)
-        edges = place(edges, v, MERIDIAN_LANE + WIDE * k, WIDE)
-        edges = place(edges, wet, WET_LANE + WIDE * k, WIDE)
-        to_north[k] = jnp.where(low, turn(v[ROWS - 8 :], 4, 0), tracer[ROWS - 8 :])
-        to_north[LEVELS + k] = jnp.where(low, turn(wet[ROWS - 8 :], 4, 0), u[ROWS - 8 :])
-        to_south[k] = jnp.where(low, tracer[:8], turn(v[:8], 4, 0))
-        to_south[LEVELS + k] = jnp.where(low, u[:8], turn(wet[:8], 4, 0))
-    depth_copy.wait()
-    floor = depth[...].astype(F32)
-    edges = place(edges, floor, DEPTH_LANE, WIDE)
-    to_north[2 * LEVELS] = floor[ROWS - 8 :]
-    to_south[2 * LEVELS] = floor[:8]
-    to_east[...] = edges[0]
-    to_west[...] = edges[1]
+        edges = place_level(edges, k, thermal[k] * wet, zonal[k], meridian[k], wet)
+    edges = place(edges, depth[...].astype(F32), DEPTH_LANE, WIDE)
+    high[...], low[...] = edges
+
+
+def pack_corners_kernel(south_edge, north_edge, to_east, to_west):
+    for edge, start in ((south_edge, 0), (north_edge, 8)):
+        edges = (jnp.zeros((8, 128), F32), jnp.zeros((8, 128), F32))
+        for k in range(LEVELS):
+            edges = place_level(
+                edges, k, edge[k], edge[LEVELS + k], turn(edge[k], 4, 0), turn(edge[LEVELS + k], 4, 0)
+            )
+        edges = place(edges, edge[2 * LEVELS], DEPTH_LANE, WIDE)
+        to_east[start : start + 8], to_west[start : start + 8] = edges
+
+
+def with_corners(edge, corner):
+    return jnp.concatenate([corner[:8], edge[...], corner[8:]], axis=0)
 
 
 def rows_extended(inside, south_tile, north_tile, second):
@@ -248,7 +266,7 @@
         pull = 0.5 * (jnp.concatenate([bond, none], 0) + jnp.concatenate([none, bond], 0))
         down = 0.5 * (kappa[:-1] + kappa[1:]) * pair_jump
         mixing = jnp.concatenate([down, none], 0) - jnp.concatenate([none, down], 0)
-        base[:, pl.ds(start, 8), :] = wet * (tracer + mixing)
+        base[:, pl.ds(start, 8), :] = tracer + mixing
         outer[...] = pull * KAPPA_SPAN * squash * (1.0 - squash)
 
     def backward(first, left, second, slope1, slope2, outer):
@@ -265,23 +283,30 @@
                 hidden_term = back[q * HID : (q + 1) * HID] * slope2[r]
                 total2 = total2 + hidden_term
                 left[r, :HID] = hidden_term.astype(BF16)
+            cols = slice(p * 2 * HID, (p + 1) * 2 * HID)
+            grad_outer[:, cols] += dot_nt(outer_grad, second[cols])
             yield
         bias2[...] = total2
         total = grad[...]
+        rights = []
         for p in range(4):
             z = dot(w2_pair_t[...], jnp.concatenate([left[2 * p, :HID], left[2 * p + 1, :HID]], 0))
             for q in range(2):
                 r = 2 * p + q
                 inner_term = z[q * HID : (q + 1) * HID] * slope1[r]
                 total1 = total1 + inner_term
-                right = jnp.concatenate(
+                rights.append(jnp.concatenate(
                     [inner_term.astype(BF16), first[r * HID : (r + 1) * HID]], 0
-                )
-                total = total + dot_nt(left[r], right)
+                ))
+            if p:
+                for r in (2 * p - 2, 2 * p - 1):
+                    total = total + dot_nt(left[r], rights[r])
             yield
+        yield
+        for r in (6, 7):
+            total = total + dot_nt(left[r], rights[r])
         bias1[...] = total1
         grad[...] = total
-        grad_outer[...] += dot_nt(outer_grad, second[...])
 
     def together(*parts):
         parts = list(parts)
@@ -299,7 +324,9 @@
         together(forward(jnp.minimum(2 * i + 2, BLOCKS - 1), *even), backward(*odd))
         return carry
 
-    lax.fori_loop(0, BLOCKS // 2, step, 0)
+    lax.fori_loop(0, BLOCKS // 2 - 1, step, 0)
+    together(forward(BLOCKS - 1, *odd), backward(*even))
+    together(backward(*odd))
     sums[0:HID] = grad[0:HID, HID:]
     sums[ROW_INNER : ROW_INNER + FIN] = grad[HID:, :HID]
     row_outer = iota((64, HID), 0)
@@ -313,8 +340,8 @@
     sums[ROW_OUTER_BIAS : ROW_OUTER_BIAS + LEVELS] = outer_bias[:, :128] + outer_bias[:, 128:]
     inner_row_sum = jnp.sum((bias1[:, :128] + bias1[:, 128:]).T, axis=0, keepdims=True)
     hidden_row_sum = jnp.sum((bias2[:, :128] + bias2[:, 128:]).T, axis=0, keepdims=True)
-    sums[ROW_BIAS : ROW_BIAS + 8] = jnp.concatenate(
-        [inner_row_sum, hidden_row_sum, jnp.zeros((6, 128), F32)], 0
+    sums[ROW_BIAS:] = jnp.concatenate(
+        [inner_row_sum, hidden_row_sum, jnp.zeros((SUM_ROWS - ROW_BIAS - 2, 128), F32)], 0
     )
 
 
@@ -324,34 +351,40 @@
 
 
 def gram_kernel(
-    zonal, meridian, sea, depth, south_edge, north_edge, west_edge, east_edge,
-    south_corner, north_corner, sums,
-    basis, summed,
-    east_transport, north_transport,
+    zonal, meridian, sea, depth, south_edge, north_edge, west_edge, east_edge, west_corner, east_corner,
+    sums,
+    basis, parts, east_open, north_open,
+    east_transport, north_transport, east_bits, north_bits,
 ):
-    west_tile = jnp.concatenate([south_corner[:, :128], west_edge[...], north_corner[:, :128]], 0)
-    east_tile = jnp.concatenate([south_corner[:, 128:], east_edge[...], north_corner[:, 128:]], 0)
+    west_tile = with_corners(west_edge, west_corner)
+    east_tile = with_corners(east_edge, east_corner)
 
     def extended(inside, index, second, lane_start):
         return field_extended(
-            inside, south_edge[index], north_edge[index], second, west_tile, east_tile, lane_start, WIDE
+            inside, south_edge[index], north_edge[index], second,
+            west_tile, east_tile, lane_start, WIDE,
         )
 
     def gather(k, carry):
         wet = extended(sea[k].astype(F32), LEVELS + k, True, WET_LANE + WIDE * k)
-        east_part = wet * east(wet) * extended(
+        east_pair = wet * east(wet)
+        north_pair = wet * north(wet)
+        east_transport[...] += east_pair * extended(
             zonal[k], LEVELS + k, False, ZONAL_LANE + WIDE * k
         )
-        north_part = wet * north(wet) * extended(
+        north_transport[...] += north_pair * extended(
             meridian[k], k, True, MERIDIAN_LANE + WIDE * k
         )
-        east_transport[...] += east_part
-        north_transport[...] += north_part
+        place_value = lax.shift_left(jnp.int32(1), k).astype(F32)
+        east_bits[...] += east_pair[8 : ROWS + 8] * place_value
+        north_bits[...] += north_pair[:, :COLS] * place_value
         return carry
 
-    east_transport[...] = jnp.zeros_like(east_transport)
-    north_transport[...] = jnp.zeros_like(north_transport)
+    for total in (east_transport, north_transport, east_bits, north_bits):
+        total[...] = jnp.zeros_like(total)
     lax.fori_loop(0, LEVELS, gather, 0)
+    east_open[...] = east_bits[...].astype(jnp.int32)
+    north_open[...] = north_bits[...].astype(jnp.int32)
     source = -(
         (east_transport[...] - west(east_transport[...]))
         + (north_transport[...] - south(north_transport[...]))
@@ -380,24 +413,22 @@
     basis[1] = first
     basis[2] = second
 
-    def product(a, b):
-        inside = jnp.sum(a[8 : ROWS + 8, :COLS] * b[8 : ROWS + 8, :COLS], axis=0, keepdims=True)
-        return inside[:, :128] + inside[:, 128:]
-
-    rows = [
-        product(source, image0),
-        product(first, image0),
-        product(second, image0),
-        product(first, image1),
-        product(second, image1),
-        product(second, image2),
-        product(source, source),
-        product(first, source),
-        product(second, source),
-    ]
-    summed[0:ROW_GRAM] = sums[0:ROW_GRAM]
-    summed[ROW_GRAM : ROW_GRAM + 16] = jnp.concatenate(rows + [jnp.zeros((7, 128), F32)], 0)
-    summed[ROW_GRAM + 16 :] = jnp.zeros((SUM_ROWS - ROW_GRAM - 16, 128), F32)
+    lane = iota((1, 128), 1)
+    gram = jnp.zeros((1, 128), F32)
+    pairs = (
+        (source, image0), (first, image0), (second, image0),
+        (first, image1), (second, image1), (second, image2),
+        (source, source), (first, source), (second, source),
+    )
+    for i, (a, b) in enumerate(pairs):
+        total = jnp.sum(a[8 : ROWS + 8, :COLS] * b[8 : ROWS + 8, :COLS], axis=0, keepdims=True)
+        gram = jnp.where(lane == i, jnp.sum(total, axis=1, keepdims=True), gram)
+    count, tall, _ = parts.shape
+    own = SUM_ROWS // count
+    tail = jnp.broadcast_to(gram, (tall - own, 128))
+    for i in range(count):
+        parts[i, :own] = sums[i * own : (i + 1) * own]
+        parts[i, own:] = tail
 
 
 def galerkin(h00, h01, h02, h11, h12, h22, g0, g1, g2):
@@ -426,65 +457,67 @@
 
 
 def final_kernel(
-    scale, thermal, zonal, meridian, sea, base, south_edge, north_edge, west_edge, east_edge, basis, totals,
-    revised, height_out, grad1, bias1, grad2, bias2, grad3, bias3,
-    falls,
+    scale, thermal, zonal, meridian, sea, base, south_edge, north_edge, west_edge, east_edge,
+    west_corner, east_corner, basis, east_open, north_open, parts,
+    revised_far, height_out, grad1, bias1, grad2, bias2, grad3, bias3,
+    revised, falls, west_tile, east_tile, totals, sent,
 ):
-    gram = jnp.sum(totals[ROW_GRAM : ROW_GRAM + 16], axis=1, keepdims=True)
-    y0, y1, y2 = galerkin(*[gram[i : i + 1] for i in range(9)])
+    def store(k):
+        return pltpu.make_async_copy(revised.at[k], revised_far.at[k], sent.at[k])
+
+    count = parts.shape[0]
+    own = SUM_ROWS // count
+    gram = parts[0, own : own + 1]
+    y0, y1, y2 = galerkin(*[gram[:, i : i + 1] for i in range(9)])
     height = y0 * basis[0] + y1 * basis[1] + y2 * basis[2]
     height_out[...] = height[8 : ROWS + 8, :COLS]
-    blank = jnp.zeros((8, 128), F32)
-    west_tile = jnp.concatenate([blank, west_edge[...], blank], 0)
-    east_tile = jnp.concatenate([blank, east_edge[...], blank], 0)
     falls[0] = east(height) - height
     falls[1] = north(height) - height
-    def advect(k, carry):
-        inside_wet = sea[k].astype(F32)
-        wet = field_extended(
-            inside_wet, south_edge[LEVELS + k], north_edge[LEVELS + k], True,
-            west_tile, east_tile, WET_LANE + WIDE * k, WIDE,
-        )
+    west_tile[...] = with_corners(west_edge, west_corner)
+    east_tile[...] = with_corners(east_edge, east_corner)
+
+    def level(k, carry):
+        bit = lax.shift_left(jnp.int32(1), k)
         tracer = field_extended(
-            thermal[k] * inside_wet, south_edge[k], north_edge[k], False,
-            west_tile, east_tile, TRACER_LANE + TRACER_WIDE * k, TRACER_WIDE,
-        )
-        u = jnp.concatenate(
-            [zonal[k], edge_columns(west_edge[...], east_edge[...], ZONAL_LANE + WIDE * k, WIDE)], 1
-        )
+            thermal[k] * sea[k].astype(F32), south_edge[k], north_edge[k], False,
+            west_tile[...], east_tile[...], TRACER_LANE + TRACER_WIDE * k, TRACER_WIDE,
+        )
+        u = jnp.concatenate([zonal[k], turn(west_edge[...], 128 - WIDE - ZONAL_LANE - WIDE * k, 1)], 1)
         v = rows_extended(meridian[k], south_edge[k], north_edge[k], True)
-        mid_wet = wet[8 : ROWS + 8]
         mid = tracer[8 : ROWS + 8]
         pair = mid + east(mid)
-        face = (8.0 * pair - (west(pair) + east(pair))) * (1.0 / 12.0)
-        flux = mid_wet * east(mid_wet) * (u - falls[0, 8 : ROWS + 8]) * face
+        face = 8.0 * pair - (west(pair) + east(pair))
+        flux = jnp.where((east_open[...] & bit) != 0, (u - falls[0, 8 : ROWS + 8]) * face, 0.0)
         spread = (flux - west(flux))[:, :COLS]
-        mid_wet = wet[:, :COLS]
         mid = tracer[:, :COLS]
         pair = mid + north(mid)
-        face = (8.0 * pair - (south(pair) + north(pair))) * (1.0 / 12.0)
-        flux = mid_wet * north(mid_wet) * (v - falls[1, :, :COLS]) * face
+        face = 8.0 * pair - (south(pair) + north(pair))
+        flux = jnp.where((north_open[...] & bit) != 0, (v - falls[1, :, :COLS]) * face, 0.0)
         spread = spread + (flux - south(flux))[8 : ROWS + 8]
-        revised[k] = base[k] - TRANSPORT_TICK * (inside_wet * spread)
+        revised[k] = base[k] - (TRANSPORT_TICK / 12.0) * spread
+        store(k).start()
         return carry
 
-    lax.fori_loop(0, LEVELS, advect, 0)
-    grad2[...] = totals[0:HID] * scale
-    grad1[...] = totals[ROW_INNER : ROW_INNER + FIN] * scale
-    grad3[...] = totals[ROW_OUTER : ROW_OUTER + LEVELS] * scale
-    bias1[...] = totals[ROW_BIAS : ROW_BIAS + 1] * scale
-    bias2[...] = totals[ROW_BIAS + 1 : ROW_BIAS + 2] * scale
+    lax.fori_loop(0, LEVELS, level, 0)
+    for i in range(count):
+        totals[i * own : (i + 1) * own] = parts[i, :own] * scale
+    grad2[...] = totals[0:HID]
+    grad1[...] = totals[ROW_INNER : ROW_INNER + FIN]
+    grad3[...] = totals[ROW_OUTER : ROW_OUTER + LEVELS]
+    bias1[...] = totals[ROW_BIAS : ROW_BIAS + 1]
+    bias2[...] = totals[ROW_BIAS + 1 : ROW_BIAS + 2]
     outer_bias = jnp.sum(totals[ROW_OUTER_BIAS : ROW_OUTER_BIAS + LEVELS], axis=1, keepdims=True)
     diagonal = iota((LEVELS, LEVELS), 0) == iota((LEVELS, LEVELS), 1)
-    bias3[...] = jnp.sum(jnp.where(diagonal, outer_bias * scale, 0.0), axis=0, keepdims=True)
+    bias3[...] = jnp.sum(jnp.where(diagonal, outer_bias, 0.0), axis=0, keepdims=True)
+    for k in range(LEVELS):
+        store(k).wait()
 
 
 def struct(*shape, dtype=F32):
     return jax.ShapeDtypeStruct(shape, dtype)
 
 
-def call(kernel, out_shape, scratch=(), in_specs=None, mib=16, flops=0, transcendentals=0, nbytes=0):
-    specs = {} if in_specs is None else {"in_specs": in_specs}
+def call(kernel, out_shape, scratch=(), mib=16, flops=0, transcendentals=0, nbytes=0, **specs):
     return pl.pallas_call(
         kernel,
         out_shape=out_shape,
@@ -517,15 +550,6 @@
     return call(sum_kernel, struct(count, *parts.shape[1:]), mib=4, nbytes=300_000)(parts)
 
 
-def total_over_devices(value):
-    lons, lats = lax.axis_size("lon"), lax.axis_size("lat")
-    parts = value.reshape(lons, value.shape[0] // lons, value.shape[1])
-    parts = lax.all_to_all(parts, "lon", 0, 0)
-    parts = lax.all_to_all(summed_copies(parts, lats), "lat", 0, 0)
-    parts = lax.all_to_all(summed_copies(parts, lons), "lon", 0, 0)
-    return parts.reshape(value.shape)
-
-
 def local(thermal, zonal, meridian, sea, depth, adjoint, w1, b1, w2, b2, w3, b3):
     lons, lats = lax.axis_size("lon"), lax.axis_size("lat")
     ring = [(i, (i + 1) % lons) for i in range(lons)]
@@ -534,33 +558,42 @@
     def back(pairs):
         return [(target, source) for source, target in pairs]
 
-    to_east, to_west, to_north, to_south = call(
-        pack_kernel,
-        (struct(ROWS, 128), struct(ROWS, 128), struct(17, 8, COLS), struct(17, 8, COLS)),
+    to_north, to_south = call(
+        pack_rows_kernel,
+        (struct(17, 8, COLS), struct(17, 8, COLS)),
         scratch=[
-            pltpu.VMEM((LEVELS, ROWS, COLS), F32),
-            pltpu.VMEM((LEVELS, ROWS, COLS), F32),
-            pltpu.VMEM((LEVELS, ROWS, COLS), F32),
-            pltpu.VMEM((LEVELS, ROWS, COLS), jnp.int32),
-            pltpu.VMEM((ROWS, COLS), jnp.int32),
-            pltpu.SemaphoreType.DMA((4 * LEVELS + 1,)),
+            pltpu.VMEM((6, LEVELS, 8, COLS), F32),
+            pltpu.VMEM((2, LEVELS, 8, COLS), jnp.int32),
+            pltpu.VMEM((2, 8, COLS), jnp.int32),
+            pltpu.SemaphoreType.DMA((10,)),
         ],
         in_specs=far(5),
         mib=58,
+        nbytes=1_000_000,
+    )(thermal, zonal, meridian, sea, depth)
+    south_edge = lax.ppermute(to_north, "lat", line)
+    north_edge = lax.ppermute(to_south, "lat", back(line))
+    high, low = call(
+        pack_columns_kernel,
+        (struct(ROWS, 128), struct(ROWS, 128)),
+        mib=8,
         flops=4_000_000,
         nbytes=5_000_000,
     )(thermal, zonal, meridian, sea, depth)
-    west_edge = lax.ppermute(to_east, "lon", ring)
-    east_edge = lax.ppermute(to_west, "lon", back(ring))
-    south_edge = lax.ppermute(to_north, "lat", line)
-    north_edge = lax.ppermute(to_south, "lat", back(line))
-    edges = jnp.concatenate([west_edge, east_edge], axis=1)
-    south_corner = lax.ppermute(edges[ROWS - 8 :], "lat", line)
-    north_corner = lax.ppermute(edges[:8], "lat", back(line))
+    west_edge = lax.ppermute(high, "lon", ring)
+    east_edge = lax.ppermute(low, "lon", back(ring))
+    to_east, to_west = call(
+        pack_corners_kernel,
+        (struct(16, 128), struct(16, 128)),
+        mib=4,
+        nbytes=400_000,
+    )(south_edge, north_edge)
+    west_corner = lax.ppermute(to_east, "lon", ring)
+    east_corner = lax.ppermute(to_west, "lon", back(ring))
 
     base, sums = call(
         closure_kernel,
-        (struct(LEVELS, ROWS, COLS), struct(ROW_GRAM, 128)),
+        (struct(LEVELS, ROWS, COLS), struct(SUM_ROWS, 128)),
         scratch=[
             pltpu.VMEM((LEVELS, EXT_ROWS, COLS), F32),
             pltpu.VMEM((LEVELS, ROWS, 128), F32),
@@ -597,19 +630,27 @@
         thermal, sea, depth, adjoint, south_edge, north_edge, west_edge, east_edge,
         w1.T, b1[None], w2, b2[None], w3, b3,
     )
-    basis, summed = call(
+    basis, parts, east_open, north_open = call(
         gram_kernel,
-        (struct(3, EXT_ROWS, EXT_COLS), struct(SUM_ROWS, 128)),
-        scratch=[pltpu.VMEM((EXT_ROWS, EXT_COLS), F32)] * 2,
+        (
+            struct(3, EXT_ROWS, EXT_COLS),
+            struct(lons, (SUM_ROWS // lons // 8 + 1) * 8, 128),
+            struct(ROWS, EXT_COLS, dtype=jnp.int32),
+            struct(EXT_ROWS, COLS, dtype=jnp.int32),
+        ),
+        scratch=[pltpu.VMEM((EXT_ROWS, EXT_COLS), F32)] * 2
+        + [pltpu.VMEM((ROWS, EXT_COLS), F32), pltpu.VMEM((EXT_ROWS, COLS), F32)],
         flops=20_000_000,
         nbytes=5_000_000,
     )(
-        zonal, meridian, sea, depth, south_edge, north_edge, west_edge, east_edge,
-        south_corner, north_corner, sums,
-    )
-    totals = total_over_devices(summed)
+        zonal, meridian, sea, depth, south_edge, north_edge, west_edge, east_edge, west_corner, east_corner,
+        sums,
+    )
+    parts = lax.all_to_all(parts, "lon", 0, 0)
+    parts = lax.all_to_all(summed_copies(parts, lats), "lat", 0, 0)
+    parts = lax.all_to_all(summed_copies(parts, lons), "lon", 0, 0)
     scale = GRADIENT_GAIN / math.sqrt(ROWS * lats * COLS * lons)
-    out = call(
+    revised, height, grad1, bias1, grad2, bias2, grad3, bias3 = call(
         functools.partial(final_kernel, scale),
         (
             struct(LEVELS, ROWS, COLS),
@@ -621,13 +662,21 @@
             struct(LEVELS, HID),
             struct(1, LEVELS),
         ),
-        scratch=[pltpu.VMEM((2, EXT_ROWS, EXT_COLS), F32)],
+        scratch=[
+            pltpu.VMEM((LEVELS, ROWS, COLS), F32),
+            pltpu.VMEM((2, EXT_ROWS, EXT_COLS), F32),
+            pltpu.VMEM((EXT_ROWS, 128), F32),
+            pltpu.VMEM((EXT_ROWS, 128), F32),
+            pltpu.VMEM((SUM_ROWS, 128), F32),
+            pltpu.SemaphoreType.DMA((LEVELS,)),
+        ],
+        out_specs=tuple(far(1) + near(7)),
         flops=20_000_000,
         nbytes=8_000_000,
     )(
-        thermal, zonal, meridian, sea, base, south_edge, north_edge, west_edge, east_edge, basis, totals
-    )
-    revised, height, grad1, bias1, grad2, bias2, grad3, bias3 = out
+        thermal, zonal, meridian, sea, base, south_edge, north_edge, west_edge, east_edge,
+        west_corner, east_corner, basis, east_open, north_open, parts,
+    )
     return (
         revised,
         height,

time: 95.7 us -> 91.3 us (0.954)
  starting transfers between devices: 13.8 us -> 10.9 us
  waiting for transfers between devices: 0.02 us -> 2.41 us
  Pallas kernels: 36 us -> 33.8 us
  blocking collectives: 44 us -> 42.4 us
    ppermute x4, starting transfers between devices: 9.49 us -> 5.15 us  [the longest x1 2.93 us: local(): west_corner = lax.ppermute(to_east, 'lon', ring)]
    pallas_call x3 -> x5, Pallas kernels: 30.1 us -> 27.7 us  [the longest x1 21.2 us: local(): call(closure_kernel, (struct(LEVELS, ROWS, COLS), struct(SUM_ROWS, 128)),...]
    ppermute x1, waiting for transfers between devices: 0.01 us -> 1.91 us  [local(): north_edge = lax.ppermute(to_south, 'lat', back(line))]
    all_to_all x3, blocking collectives: 44 us -> 42.4 us  [the longest x1 20.4 us: local(): parts = lax.all_to_all(summed_copies(parts, lats), 'lat', 0, 0)]
    ppermute x1, starting transfers between devices: 2.9 us -> 4.38 us  [local(): south_edge = lax.ppermute(to_north, 'lat', line)]
  transfers between devices with their start and end apart: 6 -> 6, of which waited for: 0 -> 2; matrix products, arithmetic and copies ran while one was open for 0% -> 0% of each run, Pallas kernels for 24% -> 25%
where the time goes in v3:
time: 91.3 us; the launch traced here: 91 us
  blocking collectives  42.4 us (46%)
  Pallas kernels  33.8 us (37%)
  starting transfers between devices  10.9 us (12%)
  waiting for transfers between devices  2.41 us (3%)
    pallas_call x1, Pallas kernels, local(): call(closure_kernel, (struct(LEVELS, ROWS, COLS), struct(SUM_ROWS, 128)),...  21.2 us
    all_to_all x1, blocking collectives, local(): parts = lax.all_to_all(summed_copies(parts, lats), 'lat', 0, 0)  20.4 us
    all_to_all x1, blocking collectives, local(): parts = lax.all_to_all(parts, 'lon', 0, 0)  11.4 us
    all_to_all x1, blocking collectives, local(): parts = lax.all_to_all(summed_copies(parts, lons), 'lon', 0, 0)  10.6 us
    pallas_call x1, Pallas kernels, local(): call(functools.partial(final_kernel, scale), (struct(LEVELS, ROWS, COLS),...  6.01 us
    ppermute x1, starting transfers between devices, local(): south_edge = lax.ppermute(to_north, 'lat', line)  4.38 us
    pallas_call x1, Pallas kernels, local(): call(gram_kernel, (struct(3, EXT_ROWS, EXT_COLS), struct(lons, (SUM_ROWS...  3.13 us
    ppermute x1, starting transfers between devices, local(): west_corner = lax.ppermute(to_east, 'lon', ring)  2.93 us
  transfers between devices with their start and end apart: 6, of which 2 were waited for; matrix products, arithmetic and copies ran while one was open for 0% of the time, Pallas kernels for 25%

profile of v3, /device:TPU:1, one launch (start us, length us, event | category | flops | bytes accessed | tf_op | source)
XLA Modules:
  0.0 91.0 jit_solution(12250928698596176852)
XLA Ops:
  0.7 2.0 %shard_map.179 = (f32[17,8,256]{2,1,0:T(8,128)}, f32[17,8,256]{2,1,0:T(8,128)}) custom-call(f32[8,128,256]{2,1,0:T(8,128)} %thermal.5, f32[8,128,256]{2,1,0:T(8,128)} %zonal.5, f32[8,128,256]{2,1,0:T(8,128)} %meridian.5, s32[8,128,256]{2,1,0:T(8,128)} %sea.7, s32[128,256]{1,0:T(8,128)} %depth.5), custom_call_target="tpu_custom_call" | custom-call | bytes 1000000 | tf_op jit(solution)/shard_map/pallas_call | solution.py:561
  2.7 4.4 %collective-permute-start = (f32[17,8,256]{2,1,0:T(8,128)}, f32[17,8,256]{2,1,0:T(8,128)S(1)}, u32[]{:S(2)}, u32[]{:S(2)}) collective-permute-start(f32[17,8,256]{2,1,0:T(8,128)} %get-tuple-element.28), channel_id=1, source_target_pairs={{0,1},{1,2},{2,3},{3,4},{4,5},{5,6},{6,7},{7,8},{8,9},{9,10},{10,1... | collective-permute-start | bytes 417800 | tf_op jit(solution)/shard_map/ppermute | solution.py:574
  7.1 0.0 copy-start.5
  7.1 1.4 %collective-permute-start.1 = (f32[17,8,256]{2,1,0:T(8,128)}, f32[17,8,256]{2,1,0:T(8,128)S(1)}, u32[]{:S(2)}, u32[]{:S(2)}) collective-permute-start(f32[17,8,256]{2,1,0:T(8,128)} %get-tuple-element.29), channel_id=1, source_target_pairs={{1,0},{2,1},{3,2},{4,3},{5,4},{6,5},{7,6},{8,7},{9,8},{10,9},{11,1... | collective-permute-start | bytes 417800 | tf_op jit(solution)/shard_map/ppermute | solution.py:575
  8.6 1.2 %shard_map.180 = (f32[128,128]{1,0:T(8,128)S(1)}, f32[128,128]{1,0:T(8,128)S(1)}) custom-call(f32[8,128,256]{2,1,0:T(8,128)S(1)} %copy-done.3, f32[8,128,256]{2,1,0:T(8,128)S(1)} %copy-done, f32[8,128,256]{2,1,0:T(8,128)S(1)} %copy-done.1, s32[8,128,256]{2,1,0:T(8,128)S(1)} %copy-done.2, s32[128,256]{1,0:T(8,128)S(1)} %copy-done.4), custom_call_target="tpu_custom_call" | custom-call | flops 4000000 | bytes 5000000 | tf_op jit(solution)/shard_map/pallas_call | solution.py:576
  9.8 2.2 %collective-permute-start.2 = (f32[128,128]{1,0:T(8,128)S(1)}, f32[128,128]{1,0:T(8,128)S(1)}, u32[]{:S(2)}, u32[]{:S(2)}) collective-permute-start(f32[128,128]{1,0:T(8,128)S(1)} %get-tuple-element.30), channel_id=1, source_target_pairs={{0,16},{16,32},{32,48},{48,64},{64,80},{80,96},{96,112},{112,128},... | collective-permute-start | bytes 196616 | tf_op jit(solution)/shard_map/ppermute | solution.py:583
  12.0 0.0 collective-permute-start.3
  12.0 0.0 collective-permute-done.south_edge
  12.0 1.9 %collective-permute-done.1.north_edge = f32[17,8,256]{2,1,0:T(8,128)S(1)} collective-permute-done((f32[17,8,256]{2,1,0:T(8,128)}, f32[17,8,256]{2,1,0:T(8,128)S(1)}, u32[]{:S(2)}, u32[]{:S(2)}) %collective-permute-start.1) | collective-permute-done | bytes 139296 | tf_op jit(solution)/shard_map/ppermute | solution.py:575
  14.0 0.2 shard_map.182
  14.2 0.0 copy-start.8
  14.2 2.9 %collective-permute-start.4 = (f32[16,128]{1,0:T(8,128)S(1)}, f32[16,128]{1,0:T(8,128)S(1)}, u32[]{:S(2)}, u32[]{:S(2)}) collective-permute-start(f32[16,128]{1,0:T(8,128)S(1)} %get-tuple-element.33), channel_id=1, source_target_pairs={{0,16},{16,32},{32,48},{48,64},{64,80},{80,96},{96,112},{112,128},... | collective-permute-start | bytes 24584 | tf_op jit(solution)/shard_map/ppermute | solution.py:591
  17.1 0.0 collective-permute-start.5
  17.1 0.5 collective-permute-done.3.east_edge
  17.6 0.6 copy-done.9
  18.3 0.0 copy-done.10
  18.3 0.0 copy-done.11
  18.3 21.2 %shard_map.181 = (f32[8,128,256]{2,1,0:T(8,128)S(1)}, f32[192,128]{1,0:T(8,128)S(1)}) custom-call(f32[8,128,256]{2,1,0:T(8,128)S(1)} %copy-done.3, s32[8,128,256]{2,1,0:T(8,128)S(1)} %copy-done.2, s32[128,256]{1,0:T(8,128)S(1)} %copy-done.4, f32[8,128,256]{2,1,0:T(8,128)S(1)} %copy-done.5, f32[17,8,256]{2,1,0:T(8,128)S(1)} %collective-permute-done.south_edge, ...), custom_call_target="tpu_custom_call" | custom-call | flops 8000000000 | bytes 5000000 | tf_op jit(solution)/shard_map/pallas_call | solution.py:594
  39.5 0.0 collective-permute-done.4.west_corner
  39.5 3.1 %shard_map.183 = (f32[3,144,384]{2,1,0:T(8,128)S(1)}, f32[16,16,128]{2,1,0:T(8,128)S(1)}, s32[128,384]{1,0:T(8,128)S(1)}, s32[144,256]{1,0:T(8,128)S(1)}) custom-call(f32[8,128,256]{2,1,0:T(8,128)S(1)} %copy-done, f32[8,128,256]{2,1,0:T(8,128)S(1)} %copy-done.1, s32[8,128,256]{2,1,0:T(8,128)S(1)} %copy-done.2, s32[128,256]{1,0:T(8,128)S(1)} %copy-done.4, ...), custom_call_target="tpu_custom_call" | custom-call | flops 20000000 | bytes 5000000 | tf_op jit(solution)/shard_map/pallas_call | solution.py:633
  42.6 11.4 %all_to_all.15.parts = f32[16,16,128]{2,1,0:T(8,128)S(1)} all-to-all(f32[16,16,128]{2,1,0:T(8,128)S(1)} %get-tuple-element.39), channel_id=1, replica_groups=mesh['lon'=16,'lat'=16] {'lon'}, dimensions={0} | all-to-all | bytes 262144 | tf_op jit(solution)/shard_map/all_to_all | solution.py:649
  54.0 20.4 %all_to_all.16.parts = f32[16,16,128]{2,1,0:T(8,128)S(1)} all-to-all(f32[16,16,128]{2,1,0:T(8,128)S(1)} %shard_map.184), channel_id=1, replica_groups=mesh['lon'=16,'lat'=16] {'lat'}, dimensions={0} | all-to-all | bytes 262144 | tf_op jit(solution)/shard_map/all_to_all | solution.py:650
  74.4 10.6 %all_to_all.17.parts = f32[16,16,128]{2,1,0:T(8,128)S(1)} all-to-all(f32[16,16,128]{2,1,0:T(8,128)S(1)} %shard_map.185), channel_id=1, replica_groups=mesh['lon'=16,'lat'=16] {'lon'}, dimensions={0} | all-to-all | bytes 262144 | tf_op jit(solution)/shard_map/all_to_all | solution.py:651
  85.0 6.0 %shard_map.186 = (f32[8,128,256]{2,1,0:T(8,128)}, f32[128,256]{1,0:T(8,128)}, f32[32,128]{1,0:T(8,128)}, f32[1,128]{1,0:T(1,128)}, f32[128,128]{1,0:T(8,128)}, /...) custom-call(f32[8,128,256]{2,1,0:T(8,128)S(1)} %copy-done.3, f32[8,128,256]{2,1,0:T(8,128)S(1)} %copy-done, ...), custom_call_target="tpu_custom_call" | custom-call | flops 20000000 | bytes 8000000 | tf_op jit(solution)/shard_map/pallas_call | solution.py:653
  (23 shorter events, 0.1 us)
Async XLA Ops:
  0.6 7.9 %copy-start.2 = (s32[8,128,256]{2,1,0:T(8,128)S(1)}, s32[8,128,256]{2,1,0:T(8,128)}, u32[]{:S(2)}) copy-start(s32[8,128,256]{2,1,0:T(8,128)} %sea.7) | copy-start | bytes 3145732
  0.6 7.9 %copy-start.4 = (s32[128,256]{1,0:T(8,128)S(1)}, s32[128,256]{1,0:T(8,128)}, u32[]{:S(2)}) copy-start(s32[128,256]{1,0:T(8,128)} %depth.5) | copy-start | bytes 393220
  0.7 7.9 %copy-start.1 = (f32[8,128,256]{2,1,0:T(8,128)S(1)}, f32[8,128,256]{2,1,0:T(8,128)}, u32[]{:S(2)}) copy-start(f32[8,128,256]{2,1,0:T(8,128)} %meridian.5) | copy-start | bytes 3145732
  0.7 7.9 %copy-start = (f32[8,128,256]{2,1,0:T(8,128)S(1)}, f32[8,128,256]{2,1,0:T(8,128)}, u32[]{:S(2)}) copy-start(f32[8,128,256]{2,1,0:T(8,128)} %zonal.5) | copy-start | bytes 3145732
  0.7 7.9 %copy-start.3 = (f32[8,128,256]{2,1,0:T(8,128)S(1)}, f32[8,128,256]{2,1,0:T(8,128)}, u32[]{:S(2)}) copy-start(f32[8,128,256]{2,1,0:T(8,128)} %thermal.5) | copy-start | bytes 3145732
  2.7 9.3 %collective-permute-start = (f32[17,8,256]{2,1,0:T(8,128)}, f32[17,8,256]{2,1,0:T(8,128)S(1)}, u32[]{:S(2)}, u32[]{:S(2)}) collective-permute-start(f32[17,8,256]{2,1,0:T(8,128)} %get-tuple-element.28), channel_id=1, source_target_pairs={{0,1},{1,2},{2,3},{3,4},{4,5},{5,6},{6,7},{7,8},{8,9},{9,10},{10,1... | collective-permute-start | bytes 417800 | tf_op jit(solution)/shard_map/ppermute | solution.py:574
  7.1 10.5 %copy-start.5 = (f32[8,128,256]{2,1,0:T(8,128)S(1)}, f32[8,128,256]{2,1,0:T(8,128)}, u32[]{:S(2)}) copy-start(f32[8,128,256]{2,1,0:T(8,128)} %adjoint.1) | copy-start | bytes 3145732
  7.1 6.8 %collective-permute-start.1 = (f32[17,8,256]{2,1,0:T(8,128)}, f32[17,8,256]{2,1,0:T(8,128)S(1)}, u32[]{:S(2)}, u32[]{:S(2)}) collective-permute-start(f32[17,8,256]{2,1,0:T(8,128)} %get-tuple-element.29), channel_id=1, source_target_pairs={{1,0},{2,1},{3,2},{4,3},{5,4},{6,5},{7,6},{8,7},{9,8},{10,9},{11,1... | collective-permute-start | bytes 417800 | tf_op jit(solution)/shard_map/ppermute | solution.py:575
  9.8 7.3 %collective-permute-start.2 = (f32[128,128]{1,0:T(8,128)S(1)}, f32[128,128]{1,0:T(8,128)S(1)}, u32[]{:S(2)}, u32[]{:S(2)}) collective-permute-start(f32[128,128]{1,0:T(8,128)S(1)} %get-tuple-element.30), channel_id=1, source_target_pairs={{0,16},{16,32},{32,48},{48,64},{64,80},{80,96},{96,112},{112,128},... | collective-permute-start | bytes 196616 | tf_op jit(solution)/shard_map/ppermute | solution.py:583
  12.0 5.6 %copy-start.6 = (f32[128,128]{1,0:T(8,128)S(1)}, f32[128,128]{1,0:T(8,128)}, u32[]{:S(2)}) copy-start(f32[128,128]{1,0:T(8,128)} %w2.1) | copy-start | bytes 196612
  12.0 5.6 %copy-start.7 = (f32[128,32]{0,1:T(8,128)S(1)}, f32[128,32]{0,1:T(8,128)}, u32[]{:S(2)}) copy-start(f32[128,32]{0,1:T(8,128)} %param.18) | copy-start | bytes 49156
  12.0 5.6 %collective-permute-start.3 = (f32[128,128]{1,0:T(8,128)S(1)}, f32[128,128]{1,0:T(8,128)S(1)}, u32[]{:S(2)}, u32[]{:S(2)}) collective-permute-start(f32[128,128]{1,0:T(8,128)S(1)} %get-tuple-element.31), channel_id=1, source_target_pairs={{16,0},{32,16},{48,32},{64,48},{80,64},{96,80},{112,96},{128,112},... | collective-permute-start | bytes 196616 | tf_op jit(solution)/shard_map/ppermute | solution.py:584
  14.2 3.5 %copy-start.8 = (f32[8,128]{1,0:T(8,128)S(1)}, f32[8,128]{1,0:T(8,128)}, u32[]{:S(2)}) copy-start(f32[8,128]{1,0:T(8,128)} %w3.1) | copy-start | bytes 12292
  14.2 25.3 %collective-permute-start.4 = (f32[16,128]{1,0:T(8,128)S(1)}, f32[16,128]{1,0:T(8,128)S(1)}, u32[]{:S(2)}, u32[]{:S(2)}) collective-permute-start(f32[16,128]{1,0:T(8,128)S(1)} %get-tuple-element.33), channel_id=1, source_target_pairs={{0,16},{16,32},{32,48},{48,64},{64,80},{80,96},{96,112},{112,128},... | collective-permute-start | bytes 24584 | tf_op jit(solution)/shard_map/ppermute | solution.py:591
  17.1 22.4 %collective-permute-start.5 = (f32[16,128]{1,0:T(8,128)S(1)}, f32[16,128]{1,0:T(8,128)S(1)}, u32[]{:S(2)}, u32[]{:S(2)}) collective-permute-start(f32[16,128]{1,0:T(8,128)S(1)} %get-tuple-element.34), channel_id=1, source_target_pairs={{16,0},{32,16},{48,32},{64,48},{80,64},{96,80},{112,96},{128,112},... | collective-permute-start | bytes 24584 | tf_op jit(solution)/shard_map/ppermute | solution.py:592
  17.6 0.7 copy-start.9
  17.6 0.7 copy-start.10
  17.6 0.7 copy-start.11

commit v4 on v3

--- a/solution.py
+++ b/solution.py
@@ -161,10 +161,14 @@
     return jnp.where(iota(ahead.shape, 1) < 64, ahead, behind)
 
 
+def face_value(here, ahead, behind, second):
+    return (TRANSPORT_TICK / 12.0) * (7.0 * (here + ahead) - (behind + second))
+
+
 def closure_kernel(
     thermal, sea, depth, adjoint, south_edge, north_edge, west_edge, east_edge,
     w1, b1, w2, b2, w3, b3,
-    base, sums,
+    base, east_face, north_face, sums,
     tracer_ext, tracer_cols, w1_big, w2_pair, w2_pair_t, w3_big, w3_t, b1_wide, b2_wide,
     first0, left0, second0, slope10, slope20, outer0,
     first1, left1, second1, slope11, slope21, outer1,
@@ -218,6 +222,11 @@
     bias2[...] = jnp.zeros_like(bias2)
     bias3[...] = jnp.zeros_like(bias3)
     level = iota((LEVELS, 8, COLS), 0).astype(F32)
+    tall = tracer_ext[:, 0:24, :]
+    ahead = north(tall)
+    north_face[:, 0:8, :] = face_value(
+        tall[:, 0:8], ahead[:, 0:8], south(tall)[:, 0:8], north(ahead)[:, 0:8]
+    )
     b3_cube = jnp.concatenate([jnp.full((1, 8, COLS), b3[k], F32) for k in range(LEVELS)], 0)
 
     def forward(j, first, left, second, slope1, slope2, outer):
@@ -227,8 +236,14 @@
         wet = sea[:, pl.ds(start, 8), :].astype(F32)
         floor = depth[pl.ds(start, 8), :].astype(F32)
         wide = jnp.concatenate([tracer, tracer_cols[:, pl.ds(start, 8), :]], axis=2)
-        zonal_slope = 0.5 * (east(wide)[:, :, :COLS] - west(wide)[:, :, :COLS])
-        meridian_slope = 0.5 * (north(tall)[:, 8:16] - south(tall)[:, 8:16])
+        ahead, behind = east(wide), west(wide)
+        zonal_slope = 0.5 * (ahead[:, :, :COLS] - behind[:, :, :COLS])
+        east_face[:, pl.ds(start, 8), :] = face_value(wide, ahead, behind, east(ahead))
+        ahead, behind = north(tall), south(tall)
+        meridian_slope = 0.5 * (ahead[:, 8:16] - behind[:, 8:16])
+        north_face[:, pl.ds(start + 8, 8), :] = face_value(
+            tracer, ahead[:, 8:16], behind[:, 8:16], north(ahead)[:, 8:16]
+        )
         clearance = wet * (floor[None] - level) * (1.0 / LEVELS)
         features = (
             jnp.concatenate([tracer, zonal_slope, meridian_slope, clearance], axis=0)
@@ -457,10 +472,10 @@
 
 
 def final_kernel(
-    scale, thermal, zonal, meridian, sea, base, south_edge, north_edge, west_edge, east_edge,
-    west_corner, east_corner, basis, east_open, north_open, parts,
+    scale, zonal, meridian, base, east_face, north_face, south_edge, west_edge, basis, east_open, north_open,
+    parts,
     revised_far, height_out, grad1, bias1, grad2, bias2, grad3, bias3,
-    revised, falls, west_tile, east_tile, totals, sent,
+    revised, falls, totals, sent,
 ):
     def store(k):
         return pltpu.make_async_copy(revised.at[k], revised_far.at[k], sent.at[k])
@@ -473,28 +488,17 @@
     height_out[...] = height[8 : ROWS + 8, :COLS]
     falls[0] = east(height) - height
     falls[1] = north(height) - height
-    west_tile[...] = with_corners(west_edge, west_corner)
-    east_tile[...] = with_corners(east_edge, east_corner)
+    tall = ROWS + 8
 
     def level(k, carry):
         bit = lax.shift_left(jnp.int32(1), k)
-        tracer = field_extended(
-            thermal[k] * sea[k].astype(F32), south_edge[k], north_edge[k], False,
-            west_tile[...], east_tile[...], TRACER_LANE + TRACER_WIDE * k, TRACER_WIDE,
-        )
         u = jnp.concatenate([zonal[k], turn(west_edge[...], 128 - WIDE - ZONAL_LANE - WIDE * k, 1)], 1)
-        v = rows_extended(meridian[k], south_edge[k], north_edge[k], True)
-        mid = tracer[8 : ROWS + 8]
-        pair = mid + east(mid)
-        face = 8.0 * pair - (west(pair) + east(pair))
-        flux = jnp.where((east_open[...] & bit) != 0, (u - falls[0, 8 : ROWS + 8]) * face, 0.0)
+        v = jnp.concatenate([turn(south_edge[k], 4, 0), meridian[k]], 0)
+        flux = jnp.where((east_open[...] & bit) != 0, (u - falls[0, 8 : ROWS + 8]) * east_face[k], 0.0)
         spread = (flux - west(flux))[:, :COLS]
-        mid = tracer[:, :COLS]
-        pair = mid + north(mid)
-        face = 8.0 * pair - (south(pair) + north(pair))
-        flux = jnp.where((north_open[...] & bit) != 0, (v - falls[1, :, :COLS]) * face, 0.0)
-        spread = spread + (flux - south(flux))[8 : ROWS + 8]
-        revised[k] = base[k] - (TRANSPORT_TICK / 12.0) * spread
+        flux = jnp.where((north_open[:tall] & bit) != 0, (v - falls[1, :tall, :COLS]) * north_face[k], 0.0)
+        spread = spread + (flux - south(flux))[8:]
+        revised[k] = base[k] - spread
         store(k).start()
         return carry
 
@@ -591,9 +595,14 @@
     west_corner = lax.ppermute(to_east, "lon", ring)
     east_corner = lax.ppermute(to_west, "lon", back(ring))
 
-    base, sums = call(
+    base, east_face, north_face, sums = call(
         closure_kernel,
-        (struct(LEVELS, ROWS, COLS), struct(SUM_ROWS, 128)),
+        (
+            struct(LEVELS, ROWS, COLS),
+            struct(LEVELS, ROWS, EXT_COLS),
+            struct(LEVELS, ROWS + 8, COLS),
+            struct(SUM_ROWS, 128),
+        ),
         scratch=[
             pltpu.VMEM((LEVELS, EXT_ROWS, COLS), F32),
             pltpu.VMEM((LEVELS, ROWS, 128), F32),
@@ -665,8 +674,6 @@
         scratch=[
             pltpu.VMEM((LEVELS, ROWS, COLS), F32),
             pltpu.VMEM((2, EXT_ROWS, EXT_COLS), F32),
-            pltpu.VMEM((EXT_ROWS, 128), F32),
-            pltpu.VMEM((EXT_ROWS, 128), F32),
             pltpu.VMEM((SUM_ROWS, 128), F32),
             pltpu.SemaphoreType.DMA((LEVELS,)),
         ],
@@ -674,8 +681,7 @@
         flops=20_000_000,
         nbytes=8_000_000,
     )(
-        thermal, zonal, meridian, sea, base, south_edge, north_edge, west_edge, east_edge,
-        west_corner, east_corner, basis, east_open, north_open, parts,
+        zonal, meridian, base, east_face, north_face, south_edge, west_edge, basis, east_open, north_open, parts,
     )
     return (
         revised,

time: 91.3 us -> 88.6 us (0.970)
  Pallas kernels: 33.8 us -> 31.7 us
    pallas_call x1, Pallas kernels: 6.01 us -> 3.71 us  [local(): call(functools.partial(final_kernel, scale), (struct(LEVELS, ROWS, COLS),...]
  transfers between devices with their start and end apart: 6 -> 6, of which waited for: 2 -> 2; matrix products, arithmetic and copies ran while one was open for 0% -> 0% of each run, Pallas kernels for 25% -> 26%
where the time goes in v4:
time: 88.6 us; the launch traced here: 88.4 us
  blocking collectives  42.4 us (48%)
  Pallas kernels  31.7 us (36%)
  starting transfers between devices  10.9 us (12%)
  waiting for transfers between devices  2.36 us (3%)
    pallas_call x1, Pallas kernels, local(): call(closure_kernel, (struct(LEVELS, ROWS, COLS), struct(LEVELS, ROWS, EX...  21.4 us
    all_to_all x1, blocking collectives, local(): parts = lax.all_to_all(summed_copies(parts, lats), 'lat', 0, 0)  20.4 us
    all_to_all x1, blocking collectives, local(): parts = lax.all_to_all(parts, 'lon', 0, 0)  11.4 us
    all_to_all x1, blocking collectives, local(): parts = lax.all_to_all(summed_copies(parts, lons), 'lon', 0, 0)  10.6 us
    ppermute x1, starting transfers between devices, local(): south_edge = lax.ppermute(to_north, 'lat', line)  4.38 us
    pallas_call x1, Pallas kernels, local(): call(functools.partial(final_kernel, scale), (struct(LEVELS, ROWS, COLS),...  3.71 us
    pallas_call x1, Pallas kernels, local(): call(gram_kernel, (struct(3, EXT_ROWS, EXT_COLS), struct(lons, (SUM_ROWS...  3.13 us
    ppermute x1, starting transfers between devices, local(): west_corner = lax.ppermute(to_east, 'lon', ring)  2.93 us
  transfers between devices with their start and end apart: 6, of which 2 were waited for; matrix products, arithmetic and copies ran while one was open for 0% of the time, Pallas kernels for 26%

profile of v4, /device:TPU:1, one launch (start us, length us, event | category | flops | bytes accessed | tf_op | source)
XLA Modules:
  0.0 88.4 jit_solution(10300085142091477131)
XLA Ops:
  0.7 2.0 %shard_map.179 = (f32[17,8,256]{2,1,0:T(8,128)}, f32[17,8,256]{2,1,0:T(8,128)}) custom-call(f32[8,128,256]{2,1,0:T(8,128)} %thermal.3, f32[8,128,256]{2,1,0:T(8,128)} %zonal.5, f32[8,128,256]{2,1,0:T(8,128)} %meridian.5, s32[8,128,256]{2,1,0:T(8,128)} %sea.5, s32[128,256]{1,0:T(8,128)} %depth.5), custom_call_target="tpu_custom_call" | custom-call | bytes 1000000 | tf_op jit(solution)/shard_map/pallas_call | solution.py:565
  2.7 4.4 %collective-permute-start = (f32[17,8,256]{2,1,0:T(8,128)}, f32[17,8,256]{2,1,0:T(8,128)S(1)}, u32[]{:S(2)}, u32[]{:S(2)}) collective-permute-start(f32[17,8,256]{2,1,0:T(8,128)} %get-tuple-element.30), channel_id=1, source_target_pairs={{0,1},{1,2},{2,3},{3,4},{4,5},{5,6},{6,7},{7,8},{8,9},{9,10},{10,1... | collective-permute-start | bytes 417800 | tf_op jit(solution)/shard_map/ppermute | solution.py:578
  7.1 0.0 copy-start.5
  7.1 0.0 copy-start.6
  7.1 0.0 copy-start.7
  7.1 0.0 copy-start.8
  7.2 0.0 copy-start.9
  7.2 0.0 copy-start.10
  7.2 0.0 copy-start.11
  7.2 1.4 %collective-permute-start.1 = (f32[17,8,256]{2,1,0:T(8,128)}, f32[17,8,256]{2,1,0:T(8,128)S(1)}, u32[]{:S(2)}, u32[]{:S(2)}) collective-permute-start(f32[17,8,256]{2,1,0:T(8,128)} %get-tuple-element.31), channel_id=1, source_target_pairs={{1,0},{2,1},{3,2},{4,3},{5,4},{6,5},{7,6},{8,7},{9,8},{10,9},{11,1... | collective-permute-start | bytes 417800 | tf_op jit(solution)/shard_map/ppermute | solution.py:579
  8.7 1.2 %shard_map.180 = (f32[128,128]{1,0:T(8,128)S(1)}, f32[128,128]{1,0:T(8,128)S(1)}) custom-call(f32[8,128,256]{2,1,0:T(8,128)S(1)} %copy-done.3, f32[8,128,256]{2,1,0:T(8,128)S(1)} %copy-done, f32[8,128,256]{2,1,0:T(8,128)S(1)} %copy-done.1, s32[8,128,256]{2,1,0:T(8,128)S(1)} %copy-done.2, s32[128,256]{1,0:T(8,128)S(1)} %copy-done.4), custom_call_target="tpu_custom_call" | custom-call | flops 4000000 | bytes 5000000 | tf_op jit(solution)/shard_map/pallas_call | solution.py:580
  9.9 2.2 %collective-permute-start.2 = (f32[128,128]{1,0:T(8,128)S(1)}, f32[128,128]{1,0:T(8,128)S(1)}, u32[]{:S(2)}, u32[]{:S(2)}) collective-permute-start(f32[128,128]{1,0:T(8,128)S(1)} %get-tuple-element.32), channel_id=1, source_target_pairs={{0,16},{16,32},{32,48},{48,64},{64,80},{80,96},{96,112},{112,128},... | collective-permute-start | bytes 196616 | tf_op jit(solution)/shard_map/ppermute | solution.py:587
  12.1 1.9 %collective-permute-done.1.north_edge = f32[17,8,256]{2,1,0:T(8,128)S(1)} collective-permute-done((f32[17,8,256]{2,1,0:T(8,128)}, f32[17,8,256]{2,1,0:T(8,128)S(1)}, u32[]{:S(2)}, u32[]{:S(2)}) %collective-permute-start.1) | collective-permute-done | bytes 139296 | tf_op jit(solution)/shard_map/ppermute | solution.py:579
  14.0 0.2 shard_map.182
  14.2 2.9 %collective-permute-start.4 = (f32[16,128]{1,0:T(8,128)S(1)}, f32[16,128]{1,0:T(8,128)S(1)}, u32[]{:S(2)}, u32[]{:S(2)}) collective-permute-start(f32[16,128]{1,0:T(8,128)S(1)} %get-tuple-element.37), channel_id=1, source_target_pairs={{0,16},{16,32},{32,48},{48,64},{64,80},{80,96},{96,112},{112,128},... | collective-permute-start | bytes 24584 | tf_op jit(solution)/shard_map/ppermute | solution.py:595
  17.2 0.0 collective-permute-start.5
  17.2 0.0 collective-permute-done.2.west_edge
  17.2 0.4 collective-permute-done.3.east_edge
  17.6 21.4 %shard_map.181 = (f32[8,128,256]{2,1,0:T(8,128)S(1)}, f32[8,128,384]{2,1,0:T(8,128)S(1)}, f32[8,136,256]{2,1,0:T(8,128)S(1)}, f32[192,128]{1,0:T(8,128)S(1)}) custom-call(f32[8,128,256]{2,1,0:T(8,128)S(1)} %copy-done.3, s32[8,128,256]{2,1,0:T(8,128)S(1)} %copy-done.2, s32[128,256]{1,0:T(8,128)S(1)} %copy-done.4, f32[8,128,256]{2,1,0:T(8,128)S(1)} %copy-done.5, ...), custom_call_target="tpu_custom_call" | custom-call | flops 8000000000 | bytes 5000000 | tf_op jit(solution)/shard_map/pallas_call | solution.py:598
  39.0 3.1 %shard_map.183 = (f32[3,144,384]{2,1,0:T(8,128)S(1)}, f32[16,16,128]{2,1,0:T(8,128)S(1)}, s32[128,384]{1,0:T(8,128)S(1)}, s32[144,256]{1,0:T(8,128)S(1)}) custom-call(f32[8,128,256]{2,1,0:T(8,128)S(1)} %copy-done, f32[8,128,256]{2,1,0:T(8,128)S(1)} %copy-done.1, s32[8,128,256]{2,1,0:T(8,128)S(1)} %copy-done.2, s32[128,256]{1,0:T(8,128)S(1)} %copy-done.4, ...), custom_call_target="tpu_custom_call" | custom-call | flops 20000000 | bytes 5000000 | tf_op jit(solution)/shard_map/pallas_call | solution.py:642
  42.2 11.4 %all_to_all.15.parts = f32[16,16,128]{2,1,0:T(8,128)S(1)} all-to-all(f32[16,16,128]{2,1,0:T(8,128)S(1)} %get-tuple-element.43), channel_id=1, replica_groups=mesh['lon'=16,'lat'=16] {'lon'}, dimensions={0} | all-to-all | bytes 262144 | tf_op jit(solution)/shard_map/all_to_all | solution.py:658
  53.6 20.4 %all_to_all.16.parts = f32[16,16,128]{2,1,0:T(8,128)S(1)} all-to-all(f32[16,16,128]{2,1,0:T(8,128)S(1)} %shard_map.184), channel_id=1, replica_groups=mesh['lon'=16,'lat'=16] {'lat'}, dimensions={0} | all-to-all | bytes 262144 | tf_op jit(solution)/shard_map/all_to_all | solution.py:659
  74.1 10.6 %all_to_all.17.parts = f32[16,16,128]{2,1,0:T(8,128)S(1)} all-to-all(f32[16,16,128]{2,1,0:T(8,128)S(1)} %shard_map.185), channel_id=1, replica_groups=mesh['lon'=16,'lat'=16] {'lon'}, dimensions={0} | all-to-all | bytes 262144 | tf_op jit(solution)/shard_map/all_to_all | solution.py:660
  84.7 3.7 %shard_map.186 = (f32[8,128,256]{2,1,0:T(8,128)}, f32[128,256]{1,0:T(8,128)}, f32[32,128]{1,0:T(8,128)}, f32[1,128]{1,0:T(1,128)}, f32[128,128]{1,0:T(8,128)}, /...) custom-call(f32[8,128,256]{2,1,0:T(8,128)S(1)} %copy-done, f32[8,128,256]{2,1,0:T(8,128)S(1)} %copy-done.1, ...), custom_call_target="tpu_custom_call" | custom-call | flops 20000000 | bytes 8000000 | tf_op jit(solution)/shard_map/pallas_call | solution.py:662
  (23 shorter events, 0.1 us)
Async XLA Ops:
  0.6 8.0 %copy-start.4 = (s32[128,256]{1,0:T(8,128)S(1)}, s32[128,256]{1,0:T(8,128)}, u32[]{:S(2)}) copy-start(s32[128,256]{1,0:T(8,128)} %depth.5) | copy-start | bytes 393220
  0.6 8.0 %copy-start.2 = (s32[8,128,256]{2,1,0:T(8,128)S(1)}, s32[8,128,256]{2,1,0:T(8,128)}, u32[]{:S(2)}) copy-start(s32[8,128,256]{2,1,0:T(8,128)} %sea.5) | copy-start | bytes 3145732
  0.7 8.0 %copy-start.1 = (f32[8,128,256]{2,1,0:T(8,128)S(1)}, f32[8,128,256]{2,1,0:T(8,128)}, u32[]{:S(2)}) copy-start(f32[8,128,256]{2,1,0:T(8,128)} %meridian.5) | copy-start | bytes 3145732
  0.7 8.0 %copy-start = (f32[8,128,256]{2,1,0:T(8,128)S(1)}, f32[8,128,256]{2,1,0:T(8,128)}, u32[]{:S(2)}) copy-start(f32[8,128,256]{2,1,0:T(8,128)} %zonal.5) | copy-start | bytes 3145732
  0.7 8.0 %copy-start.3 = (f32[8,128,256]{2,1,0:T(8,128)S(1)}, f32[8,128,256]{2,1,0:T(8,128)}, u32[]{:S(2)}) copy-start(f32[8,128,256]{2,1,0:T(8,128)} %thermal.3) | copy-start | bytes 3145732
  2.7 9.4 %collective-permute-start = (f32[17,8,256]{2,1,0:T(8,128)}, f32[17,8,256]{2,1,0:T(8,128)S(1)}, u32[]{:S(2)}, u32[]{:S(2)}) collective-permute-start(f32[17,8,256]{2,1,0:T(8,128)} %get-tuple-element.30), channel_id=1, source_target_pairs={{0,1},{1,2},{2,3},{3,4},{4,5},{5,6},{6,7},{7,8},{8,9},{9,10},{10,1... | collective-permute-start | bytes 417800 | tf_op jit(solution)/shard_map/ppermute | solution.py:578
  7.1 10.5 %copy-start.5 = (f32[8,128,256]{2,1,0:T(8,128)S(1)}, f32[8,128,256]{2,1,0:T(8,128)}, u32[]{:S(2)}) copy-start(f32[8,128,256]{2,1,0:T(8,128)} %adjoint.1) | copy-start | bytes 3145732
  7.1 10.5 %copy-start.6 = (f32[128,128]{1,0:T(8,128)S(1)}, f32[128,128]{1,0:T(8,128)}, u32[]{:S(2)}) copy-start(f32[128,128]{1,0:T(8,128)} %w2.1) | copy-start | bytes 196612
  7.1 10.5 %copy-start.7 = (f32[128,32]{0,1:T(8,128)S(1)}, f32[128,32]{0,1:T(8,128)}, u32[]{:S(2)}) copy-start(f32[128,32]{0,1:T(8,128)} %param.18) | copy-start | bytes 49156
  7.1 10.5 %copy-start.8 = (f32[8,128]{1,0:T(8,128)S(1)}, f32[8,128]{1,0:T(8,128)}, u32[]{:S(2)}) copy-start(f32[8,128]{1,0:T(8,128)} %w3.1) | copy-start | bytes 12292
  7.2 10.5 %copy-start.9 = (f32[128]{0:T(128)S(1)}, f32[128]{0:T(128)}, u32[]{:S(2)}) copy-start(f32[128]{0:T(128)} %param.19) | copy-start | bytes 1540
  7.2 10.5 %copy-start.10 = (f32[128]{0:T(128)S(1)}, f32[128]{0:T(128)}, u32[]{:S(2)}) copy-start(f32[128]{0:T(128)} %param.21) | copy-start | bytes 1540
  7.2 10.5 %copy-start.11 = (f32[8]{0:T(128)S(1)}, f32[8]{0:T(128)}, u32[]{:S(2)}) copy-start(f32[8]{0:T(128)} %b3.1) | copy-start | bytes 100
  7.2 6.8 %collective-permute-start.1 = (f32[17,8,256]{2,1,0:T(8,128)}, f32[17,8,256]{2,1,0:T(8,128)S(1)}, u32[]{:S(2)}, u32[]{:S(2)}) collective-permute-start(f32[17,8,256]{2,1,0:T(8,128)} %get-tuple-element.31), channel_id=1, source_target_pairs={{1,0},{2,1},{3,2},{4,3},{5,4},{6,5},{7,6},{8,7},{9,8},{10,9},{11,1... | collective-permute-start | bytes 417800 | tf_op jit(solution)/shard_map/ppermute | solution.py:579
  9.9 7.3 %collective-permute-start.2 = (f32[128,128]{1,0:T(8,128)S(1)}, f32[128,128]{1,0:T(8,128)S(1)}, u32[]{:S(2)}, u32[]{:S(2)}) collective-permute-start(f32[128,128]{1,0:T(8,128)S(1)} %get-tuple-element.32), channel_id=1, source_target_pairs={{0,16},{16,32},{32,48},{48,64},{64,80},{80,96},{96,112},{112,128},... | collective-permute-start | bytes 196616 | tf_op jit(solution)/shard_map/ppermute | solution.py:587
  12.1 5.5 %collective-permute-start.3 = (f32[128,128]{1,0:T(8,128)S(1)}, f32[128,128]{1,0:T(8,128)S(1)}, u32[]{:S(2)}, u32[]{:S(2)}) collective-permute-start(f32[128,128]{1,0:T(8,128)S(1)} %get-tuple-element.33), channel_id=1, source_target_pairs={{16,0},{32,16},{48,32},{64,48},{80,64},{96,80},{112,96},{128,112},... | collective-permute-start | bytes 196616 | tf_op jit(solution)/shard_map/ppermute | solution.py:588
  14.2 24.8 %collective-permute-start.4 = (f32[16,128]{1,0:T(8,128)S(1)}, f32[16,128]{1,0:T(8,128)S(1)}, u32[]{:S(2)}, u32[]{:S(2)}) collective-permute-start(f32[16,128]{1,0:T(8,128)S(1)} %get-tuple-element.37), channel_id=1, source_target_pairs={{0,16},{16,32},{32,48},{48,64},{64,80},{80,96},{96,112},{112,128},... | collective-permute-start | bytes 24584 | tf_op jit(solution)/shard_map/ppermute | solution.py:595
  17.2 21.9 %collective-permute-start.5 = (f32[16,128]{1,0:T(8,128)S(1)}, f32[16,128]{1,0:T(8,128)S(1)}, u32[]{:S(2)}, u32[]{:S(2)}) collective-permute-start(f32[16,128]{1,0:T(8,128)S(1)} %get-tuple-element.38), channel_id=1, source_target_pairs={{16,0},{32,16},{48,32},{64,48},{80,64},{96,80},{112,96},{128,112},... | collective-permute-start | bytes 24584 | tf_op jit(solution)/shard_map/ppermute | solution.py:596

commit v5 on v4

--- a/solution.py
+++ b/solution.py
@@ -380,7 +380,7 @@
             west_tile, east_tile, lane_start, WIDE,
         )
 
-    def gather(k, carry):
+    def gather(k):
         wet = extended(sea[k].astype(F32), LEVELS + k, True, WET_LANE + WIDE * k)
         east_pair = wet * east(wet)
         north_pair = wet * north(wet)
@@ -390,14 +390,14 @@
         north_transport[...] += north_pair * extended(
             meridian[k], k, True, MERIDIAN_LANE + WIDE * k
         )
-        place_value = lax.shift_left(jnp.int32(1), k).astype(F32)
+        place_value = float(1 << k)
         east_bits[...] += east_pair[8 : ROWS + 8] * place_value
         north_bits[...] += north_pair[:, :COLS] * place_value
-        return carry
 
     for total in (east_transport, north_transport, east_bits, north_bits):
         total[...] = jnp.zeros_like(total)
-    lax.fori_loop(0, LEVELS, gather, 0)
+    for k in range(LEVELS):
+        gather(k)
     east_open[...] = east_bits[...].astype(jnp.int32)
     north_open[...] = north_bits[...].astype(jnp.int32)
     source = -(
@@ -490,8 +490,8 @@
     falls[1] = north(height) - height
     tall = ROWS + 8
 
-    def level(k, carry):
-        bit = lax.shift_left(jnp.int32(1), k)
+    def level(k):
+        bit = 1 << k
         u = jnp.concatenate([zonal[k], turn(west_edge[...], 128 - WIDE - ZONAL_LANE - WIDE * k, 1)], 1)
         v = jnp.concatenate([turn(south_edge[k], 4, 0), meridian[k]], 0)
         flux = jnp.where((east_open[...] & bit) != 0, (u - falls[0, 8 : ROWS + 8]) * east_face[k], 0.0)
@@ -500,9 +500,9 @@
         spread = spread + (flux - south(flux))[8:]
         revised[k] = base[k] - spread
         store(k).start()
-        return carry
-
-    lax.fori_loop(0, LEVELS, level, 0)
+
+    for k in range(LEVELS):
+        level(k)
     for i in range(count):
         totals[i * own : (i + 1) * own] = parts[i, :own] * scale
     grad2[...] = totals[0:HID]

time: 88.6 us -> 87.9 us (level)
  no operation moved by 1% of the time
where the time goes in v5:
time: 87.9 us; the launch traced here: 87.7 us
  blocking collectives  42.4 us (48%)
  Pallas kernels  30.9 us (35%)
  starting transfers between devices  10.9 us (12%)
  waiting for transfers between devices  2.36 us (3%)
  between operations  1.03 us (1%)
    pallas_call x1, Pallas kernels, local(): call(closure_kernel, (struct(LEVELS, ROWS, COLS), struct(LEVELS, ROWS, EX...  21.4 us
    all_to_all x1, blocking collectives, local(): parts = lax.all_to_all(summed_copies(parts, lats), 'lat', 0, 0)  20.4 us
    all_to_all x1, blocking collectives, local(): parts = lax.all_to_all(parts, 'lon', 0, 0)  11.4 us
    all_to_all x1, blocking collectives, local(): parts = lax.all_to_all(summed_copies(parts, lons), 'lon', 0, 0)  10.6 us
    ppermute x1, starting transfers between devices, local(): south_edge = lax.ppermute(to_north, 'lat', line)  4.38 us
    pallas_call x1, Pallas kernels, local(): call(functools.partial(final_kernel, scale), (struct(LEVELS, ROWS, COLS),...  3.2 us
    ppermute x1, starting transfers between devices, local(): west_corner = lax.ppermute(to_east, 'lon', ring)  2.93 us
    pallas_call x1, Pallas kernels, local(): call(gram_kernel, (struct(3, EXT_ROWS, EXT_COLS), struct(lons, (SUM_ROWS...  2.8 us
  transfers between devices with their start and end apart: 6, of which 2 were waited for; matrix products, arithmetic and copies ran while one was open for 0% of the time, Pallas kernels for 26%

profile of v5, /device:TPU:1, one launch (start us, length us, event | category | flops | bytes accessed | tf_op | source)
XLA Modules:
  0.0 87.7 jit_solution(6741539529381401155)
XLA Ops:
  0.7 2.0 %shard_map.179 = (f32[17,8,256]{2,1,0:T(8,128)}, f32[17,8,256]{2,1,0:T(8,128)}) custom-call(f32[8,128,256]{2,1,0:T(8,128)} %thermal.3, f32[8,128,256]{2,1,0:T(8,128)} %zonal.5, f32[8,128,256]{2,1,0:T(8,128)} %meridian.5, s32[8,128,256]{2,1,0:T(8,128)} %sea.5, s32[128,256]{1,0:T(8,128)} %depth.5), custom_call_target="tpu_custom_call" | custom-call | bytes 1000000 | tf_op jit(solution)/shard_map/pallas_call | solution.py:565
  2.7 4.4 %collective-permute-start = (f32[17,8,256]{2,1,0:T(8,128)}, f32[17,8,256]{2,1,0:T(8,128)S(1)}, u32[]{:S(2)}, u32[]{:S(2)}) collective-permute-start(f32[17,8,256]{2,1,0:T(8,128)} %get-tuple-element.30), channel_id=1, source_target_pairs={{0,1},{1,2},{2,3},{3,4},{4,5},{5,6},{6,7},{7,8},{8,9},{9,10},{10,1... | collective-permute-start | bytes 417800 | tf_op jit(solution)/shard_map/ppermute | solution.py:578
  7.1 0.0 copy-start.5
  7.1 0.0 copy-start.6
  7.1 0.0 copy-start.7
  7.1 0.0 copy-start.8
  7.2 0.0 copy-start.9
  7.2 0.0 copy-start.10
  7.2 0.0 copy-start.11
  7.2 1.4 %collective-permute-start.1 = (f32[17,8,256]{2,1,0:T(8,128)}, f32[17,8,256]{2,1,0:T(8,128)S(1)}, u32[]{:S(2)}, u32[]{:S(2)}) collective-permute-start(f32[17,8,256]{2,1,0:T(8,128)} %get-tuple-element.31), channel_id=1, source_target_pairs={{1,0},{2,1},{3,2},{4,3},{5,4},{6,5},{7,6},{8,7},{9,8},{10,9},{11,1... | collective-permute-start | bytes 417800 | tf_op jit(solution)/shard_map/ppermute | solution.py:579
  8.7 1.2 %shard_map.180 = (f32[128,128]{1,0:T(8,128)S(1)}, f32[128,128]{1,0:T(8,128)S(1)}) custom-call(f32[8,128,256]{2,1,0:T(8,128)S(1)} %copy-done.3, f32[8,128,256]{2,1,0:T(8,128)S(1)} %copy-done, f32[8,128,256]{2,1,0:T(8,128)S(1)} %copy-done.1, s32[8,128,256]{2,1,0:T(8,128)S(1)} %copy-done.2, s32[128,256]{1,0:T(8,128)S(1)} %copy-done.4), custom_call_target="tpu_custom_call" | custom-call | flops 4000000 | bytes 5000000 | tf_op jit(solution)/shard_map/pallas_call | solution.py:580
  9.9 2.2 %collective-permute-start.2 = (f32[128,128]{1,0:T(8,128)S(1)}, f32[128,128]{1,0:T(8,128)S(1)}, u32[]{:S(2)}, u32[]{:S(2)}) collective-permute-start(f32[128,128]{1,0:T(8,128)S(1)} %get-tuple-element.32), channel_id=1, source_target_pairs={{0,16},{16,32},{32,48},{48,64},{64,80},{80,96},{96,112},{112,128},... | collective-permute-start | bytes 196616 | tf_op jit(solution)/shard_map/ppermute | solution.py:587
  12.1 0.0 collective-permute-done.south_edge
  12.1 1.9 %collective-permute-done.1.north_edge = f32[17,8,256]{2,1,0:T(8,128)S(1)} collective-permute-done((f32[17,8,256]{2,1,0:T(8,128)}, f32[17,8,256]{2,1,0:T(8,128)S(1)}, u32[]{:S(2)}, u32[]{:S(2)}) %collective-permute-start.1) | collective-permute-done | bytes 139296 | tf_op jit(solution)/shard_map/ppermute | solution.py:579
  14.0 0.2 shard_map.182
  14.2 2.9 %collective-permute-start.4 = (f32[16,128]{1,0:T(8,128)S(1)}, f32[16,128]{1,0:T(8,128)S(1)}, u32[]{:S(2)}, u32[]{:S(2)}) collective-permute-start(f32[16,128]{1,0:T(8,128)S(1)} %get-tuple-element.37), channel_id=1, source_target_pairs={{0,16},{16,32},{32,48},{48,64},{64,80},{80,96},{96,112},{112,128},... | collective-permute-start | bytes 24584 | tf_op jit(solution)/shard_map/ppermute | solution.py:595
  17.2 0.0 collective-permute-start.5
  17.2 0.4 collective-permute-done.3.east_edge
  17.6 21.4 %shard_map.181 = (f32[8,128,256]{2,1,0:T(8,128)S(1)}, f32[8,128,384]{2,1,0:T(8,128)S(1)}, f32[8,136,256]{2,1,0:T(8,128)S(1)}, f32[192,128]{1,0:T(8,128)S(1)}) custom-call(f32[8,128,256]{2,1,0:T(8,128)S(1)} %copy-done.3, s32[8,128,256]{2,1,0:T(8,128)S(1)} %copy-done.2, s32[128,256]{1,0:T(8,128)S(1)} %copy-done.4, f32[8,128,256]{2,1,0:T(8,128)S(1)} %copy-done.5, ...), custom_call_target="tpu_custom_call" | custom-call | flops 8000000000 | bytes 5000000 | tf_op jit(solution)/shard_map/pallas_call | solution.py:598
  39.0 2.8 %shard_map.183 = (f32[3,144,384]{2,1,0:T(8,128)S(1)}, f32[16,16,128]{2,1,0:T(8,128)S(1)}, s32[128,384]{1,0:T(8,128)S(1)}, s32[144,256]{1,0:T(8,128)S(1)}) custom-call(f32[8,128,256]{2,1,0:T(8,128)S(1)} %copy-done, f32[8,128,256]{2,1,0:T(8,128)S(1)} %copy-done.1, s32[8,128,256]{2,1,0:T(8,128)S(1)} %copy-done.2, s32[128,256]{1,0:T(8,128)S(1)} %copy-done.4, ...), custom_call_target="tpu_custom_call" | custom-call | flops 20000000 | bytes 5000000 | tf_op jit(solution)/shard_map/pallas_call | solution.py:642
  41.8 11.4 %all_to_all.15.parts = f32[16,16,128]{2,1,0:T(8,128)S(1)} all-to-all(f32[16,16,128]{2,1,0:T(8,128)S(1)} %get-tuple-element.43), channel_id=1, replica_groups=mesh['lon'=16,'lat'=16] {'lon'}, dimensions={0} | all-to-all | bytes 262144 | tf_op jit(solution)/shard_map/all_to_all | solution.py:658
  53.3 20.4 %all_to_all.16.parts = f32[16,16,128]{2,1,0:T(8,128)S(1)} all-to-all(f32[16,16,128]{2,1,0:T(8,128)S(1)} %shard_map.184), channel_id=1, replica_groups=mesh['lon'=16,'lat'=16] {'lat'}, dimensions={0} | all-to-all | bytes 262144 | tf_op jit(solution)/shard_map/all_to_all | solution.py:659
  73.7 10.6 %all_to_all.17.parts = f32[16,16,128]{2,1,0:T(8,128)S(1)} all-to-all(f32[16,16,128]{2,1,0:T(8,128)S(1)} %shard_map.185), channel_id=1, replica_groups=mesh['lon'=16,'lat'=16] {'lon'}, dimensions={0} | all-to-all | bytes 262144 | tf_op jit(solution)/shard_map/all_to_all | solution.py:660
  84.3 3.2 %shard_map.186 = (f32[8,128,256]{2,1,0:T(8,128)}, f32[128,256]{1,0:T(8,128)}, f32[32,128]{1,0:T(8,128)}, f32[1,128]{1,0:T(1,128)}, f32[128,128]{1,0:T(8,128)}, /...) custom-call(f32[8,128,256]{2,1,0:T(8,128)S(1)} %copy-done, f32[8,128,256]{2,1,0:T(8,128)S(1)} %copy-done.1, ...), custom_call_target="tpu_custom_call" | custom-call | flops 20000000 | bytes 8000000 | tf_op jit(solution)/shard_map/pallas_call | solution.py:662
  (23 shorter events, 0.1 us)
Async XLA Ops:
  0.6 8.0 %copy-start.4 = (s32[128,256]{1,0:T(8,128)S(1)}, s32[128,256]{1,0:T(8,128)}, u32[]{:S(2)}) copy-start(s32[128,256]{1,0:T(8,128)} %depth.5) | copy-start | bytes 393220
  0.6 8.0 %copy-start.2 = (s32[8,128,256]{2,1,0:T(8,128)S(1)}, s32[8,128,256]{2,1,0:T(8,128)}, u32[]{:S(2)}) copy-start(s32[8,128,256]{2,1,0:T(8,128)} %sea.5) | copy-start | bytes 3145732
  0.7 8.0 %copy-start.1 = (f32[8,128,256]{2,1,0:T(8,128)S(1)}, f32[8,128,256]{2,1,0:T(8,128)}, u32[]{:S(2)}) copy-start(f32[8,128,256]{2,1,0:T(8,128)} %meridian.5) | copy-start | bytes 3145732
  0.7 8.0 %copy-start = (f32[8,128,256]{2,1,0:T(8,128)S(1)}, f32[8,128,256]{2,1,0:T(8,128)}, u32[]{:S(2)}) copy-start(f32[8,128,256]{2,1,0:T(8,128)} %zonal.5) | copy-start | bytes 3145732
  0.7 8.0 %copy-start.3 = (f32[8,128,256]{2,1,0:T(8,128)S(1)}, f32[8,128,256]{2,1,0:T(8,128)}, u32[]{:S(2)}) copy-start(f32[8,128,256]{2,1,0:T(8,128)} %thermal.3) | copy-start | bytes 3145732
  2.7 9.4 %collective-permute-start = (f32[17,8,256]{2,1,0:T(8,128)}, f32[17,8,256]{2,1,0:T(8,128)S(1)}, u32[]{:S(2)}, u32[]{:S(2)}) collective-permute-start(f32[17,8,256]{2,1,0:T(8,128)} %get-tuple-element.30), channel_id=1, source_target_pairs={{0,1},{1,2},{2,3},{3,4},{4,5},{5,6},{6,7},{7,8},{8,9},{9,10},{10,1... | collective-permute-start | bytes 417800 | tf_op jit(solution)/shard_map/ppermute | solution.py:578
  7.1 10.5 %copy-start.5 = (f32[8,128,256]{2,1,0:T(8,128)S(1)}, f32[8,128,256]{2,1,0:T(8,128)}, u32[]{:S(2)}) copy-start(f32[8,128,256]{2,1,0:T(8,128)} %adjoint.1) | copy-start | bytes 3145732
  7.1 10.5 %copy-start.6 = (f32[128,128]{1,0:T(8,128)S(1)}, f32[128,128]{1,0:T(8,128)}, u32[]{:S(2)}) copy-start(f32[128,128]{1,0:T(8,128)} %w2.1) | copy-start | bytes 196612
  7.1 10.5 %copy-start.7 = (f32[128,32]{0,1:T(8,128)S(1)}, f32[128,32]{0,1:T(8,128)}, u32[]{:S(2)}) copy-start(f32[128,32]{0,1:T(8,128)} %param.18) | copy-start | bytes 49156
  7.1 10.5 %copy-start.8 = (f32[8,128]{1,0:T(8,128)S(1)}, f32[8,128]{1,0:T(8,128)}, u32[]{:S(2)}) copy-start(f32[8,128]{1,0:T(8,128)} %w3.1) | copy-start | bytes 12292
  7.2 10.5 %copy-start.9 = (f32[128]{0:T(128)S(1)}, f32[128]{0:T(128)}, u32[]{:S(2)}) copy-start(f32[128]{0:T(128)} %param.19) | copy-start | bytes 1540
  7.2 10.5 %copy-start.10 = (f32[128]{0:T(128)S(1)}, f32[128]{0:T(128)}, u32[]{:S(2)}) copy-start(f32[128]{0:T(128)} %param.21) | copy-start | bytes 1540
  7.2 10.5 %copy-start.11 = (f32[8]{0:T(128)S(1)}, f32[8]{0:T(128)}, u32[]{:S(2)}) copy-start(f32[8]{0:T(128)} %b3.1) | copy-start | bytes 100
  7.2 6.8 %collective-permute-start.1 = (f32[17,8,256]{2,1,0:T(8,128)}, f32[17,8,256]{2,1,0:T(8,128)S(1)}, u32[]{:S(2)}, u32[]{:S(2)}) collective-permute-start(f32[17,8,256]{2,1,0:T(8,128)} %get-tuple-element.31), channel_id=1, source_target_pairs={{1,0},{2,1},{3,2},{4,3},{5,4},{6,5},{7,6},{8,7},{9,8},{10,9},{11,1... | collective-permute-start | bytes 417800 | tf_op jit(solution)/shard_map/ppermute | solution.py:579
  9.9 7.3 %collective-permute-start.2 = (f32[128,128]{1,0:T(8,128)S(1)}, f32[128,128]{1,0:T(8,128)S(1)}, u32[]{:S(2)}, u32[]{:S(2)}) collective-permute-start(f32[128,128]{1,0:T(8,128)S(1)} %get-tuple-element.32), channel_id=1, source_target_pairs={{0,16},{16,32},{32,48},{48,64},{64,80},{80,96},{96,112},{112,128},... | collective-permute-start | bytes 196616 | tf_op jit(solution)/shard_map/ppermute | solution.py:587
  12.1 5.5 %collective-permute-start.3 = (f32[128,128]{1,0:T(8,128)S(1)}, f32[128,128]{1,0:T(8,128)S(1)}, u32[]{:S(2)}, u32[]{:S(2)}) collective-permute-start(f32[128,128]{1,0:T(8,128)S(1)} %get-tuple-element.33), channel_id=1, source_target_pairs={{16,0},{32,16},{48,32},{64,48},{80,64},{96,80},{112,96},{128,112},... | collective-permute-start | bytes 196616 | tf_op jit(solution)/shard_map/ppermute | solution.py:588
  14.2 24.8 %collective-permute-start.4 = (f32[16,128]{1,0:T(8,128)S(1)}, f32[16,128]{1,0:T(8,128)S(1)}, u32[]{:S(2)}, u32[]{:S(2)}) collective-permute-start(f32[16,128]{1,0:T(8,128)S(1)} %get-tuple-element.37), channel_id=1, source_target_pairs={{0,16},{16,32},{32,48},{48,64},{64,80},{80,96},{96,112},{112,128},... | collective-permute-start | bytes 24584 | tf_op jit(solution)/shard_map/ppermute | solution.py:595
  17.2 21.9 %collective-permute-start.5 = (f32[16,128]{1,0:T(8,128)S(1)}, f32[16,128]{1,0:T(8,128)S(1)}, u32[]{:S(2)}, u32[]{:S(2)}) collective-permute-start(f32[16,128]{1,0:T(8,128)S(1)} %get-tuple-element.38), channel_id=1, source_target_pairs={{16,0},{32,16},{48,32},{64,48},{80,64},{96,80},{112,96},{128,112},... | collective-permute-start | bytes 24584 | tf_op jit(solution)/shard_map/ppermute | solution.py:596
